TPU v7x, 512 devices: a whole 4x8x8 slice. The times are simulated.
512 devices in a mesh: head: 8 (over y_lo, x), seq: 64 (over z, y_hi, core).
Axes of the slice: x: 4, y: 8 (y_hi: 4, y_lo: 2; y = y_hi * 2 + y_lo), z: 8, core: 2. Of those that a mesh axis runs over, the one named last changes fastest.
Arguments:
- hidden: bfloat16 [2048, 5120], P('seq', 'head'), may hold values from -6 to 6
- query: bfloat16 [2048, 3072], P('seq', 'head'), may hold values from -1000 to 1000
- key: bfloat16 [2048, 3072], P('seq', 'head'), may hold values from -1000 to 1000
- value: bfloat16 [2048, 3072], P('seq', 'head'), may hold values from -8 to 8
- query_gain: float32 [3072], P('head'), may hold values from 0.5 to 3
- key_gain: float32 [3072], P('head'), may hold values from 0.5 to 3
- ref_key: bfloat16 [2048, 3072], P('seq', 'head'), may hold values from -8 to 8
- ref_value: bfloat16 [2048, 3072], P('seq', 'head'), may hold values from -8 to 8
- ref_count: int32 [64], P('seq'), may hold values from 1 to 32, 1024 in all
- out_weight: bfloat16 [3072, 5120], P('head'), may hold values from -0.109375 to 0.109375
- gate_table: float32 [50, 5120], P(None, 'head'), may hold values from -8 to 8
- frame_step: int32 [64], P('seq'), may hold values from 0 to 49
Outputs:
- updated: bfloat16 [2048, 5120], P('seq', 'head')
Inputs may be any that keep to these rules, and one draw needn't show every extreme that they name: ref_count[p] counts the live slots of cycle position p, the first ones of its 32; the counts sum to 1024, and some position has all 32 slots live.
All inputs are finite; a program needn't handle non-finite values. No bound on the sum of `ref_count` on one device may be relied on, other than what follows from the above.
Results may differ from a plain program's by a relative error of at most 0.019.
Values may be sent and summed in bfloat16 or wider, within the bound.
No kernel may reach another device: no remote copies, remote signals or barrier semaphores. Data moves between devices by JAX's collectives and lax.ppermute only.
A program may use at most 64 MiB of HBM per device.

v0:
```python
import math

import jax
import jax.numpy as jnp
from jax import lax
from jax.sharding import PartitionSpec as P

HEAD_DIM = 128
FRAME_TOK = 32


EPSILON = 1e-06
NEGATIVE = -1e30


def attend(running, queries, key_rows, value_rows, live_mask):
    run_max, run_total, run_acc = running
    score_scale = 1.0 / math.sqrt(queries.shape[2])
    scores = (
        jnp.einsum("chd,khd->hck", queries, key_rows, preferred_element_type=jnp.float32)
        * score_scale
    )
    if live_mask is not None:
        scores = jnp.where(live_mask[None, None, :], scores, NEGATIVE)
    new_max = jnp.maximum(run_max, jnp.max(scores, axis=2))
    weights = jnp.exp(scores - new_max[:, :, None])
    if live_mask is not None:
        weights = jnp.where(live_mask[None, None, :], weights, 0.0)
    factor = jnp.exp(run_max - new_max)
    new_total = run_total * factor + jnp.sum(weights, axis=2)
    mixed_rows = jnp.einsum(
        "hck,khd->hcd", weights.astype(jnp.bfloat16), value_rows, preferred_element_type=jnp.float32
    )
    return (new_max, new_total, run_acc * factor[:, :, None] + mixed_rows)


def attend_rows(running, queries, key_rows, value_rows, live_mask):
    row_count = key_rows.shape[0]
    head_count = queries.shape[1]
    key_rows = key_rows.reshape(row_count, head_count, HEAD_DIM)
    value_rows = value_rows.reshape(row_count, head_count, HEAD_DIM)
    block_rows = 1024
    block_count = row_count // block_rows
    key_blocks = key_rows.reshape(block_count, block_rows, head_count, HEAD_DIM)
    value_blocks = value_rows.reshape(block_count, block_rows, head_count, HEAD_DIM)
    if live_mask is None:

        def advance(current, blocks):
            return (attend(current, queries, blocks[0], blocks[1], None), None)

        result, unused = lax.scan(advance, running, (key_blocks, value_blocks))
    else:
        live_blocks = live_mask.reshape(block_count, block_rows)

        def advance(current, blocks):
            return (attend(current, queries, blocks[0], blocks[1], blocks[2]), None)

        result, unused = lax.scan(advance, running, (key_blocks, value_blocks, live_blocks))
    return result


def live_rows(counts, row_count):
    slots = row_count // counts.shape[0]
    position = jnp.arange(row_count, dtype=jnp.int32)
    return position % slots < jnp.repeat(counts, slots, total_repeat_length=row_count)


def shards(
    hidden,
    query,
    key,
    value,
    query_gain,
    key_gain,
    ref_key,
    ref_value,
    ref_count,
    out_weight,
    gate_table,
    frame_step,
):
    local_feat = query.shape[1]
    head_count = local_feat // HEAD_DIM
    token_count = query.shape[0]
    query_float = query.astype(jnp.float32)
    key_float = key.astype(jnp.float32)
    query_power, key_power = lax.psum(
        (jnp.sum(query_float * query_float, axis=1), jnp.sum(key_float * key_float, axis=1)), "head"
    )
    all_features = local_feat * lax.axis_size("head")
    query_norm = (
        query_float * lax.rsqrt(query_power / all_features + EPSILON)[:, None] * query_gain[None, :]
    ).astype(jnp.bfloat16)
    key_norm = (
        key_float * lax.rsqrt(key_power / all_features + EPSILON)[:, None] * key_gain[None, :]
    ).astype(jnp.bfloat16)
    queries = query_norm.reshape(token_count, head_count, HEAD_DIM)
    initial = (
        jnp.full((head_count, token_count), NEGATIVE, jnp.float32),
        jnp.zeros((head_count, token_count), jnp.float32),
        jnp.zeros((head_count, token_count, HEAD_DIM), jnp.float32),
    )
    pieces = (
        lax.all_gather(key_norm, "seq", axis=0, tiled=True),
        lax.all_gather(value, "seq", axis=0, tiled=True),
    )
    running = attend_rows(initial, queries, pieces[0], pieces[1], None)
    pieces = (
        lax.all_gather(ref_key, "seq", axis=0, tiled=True),
        lax.all_gather(ref_value, "seq", axis=0, tiled=True),
        lax.all_gather(ref_count, "seq", axis=0, tiled=True),
    )
    running = attend_rows(
        running, queries, pieces[0], pieces[1], live_rows(pieces[2], pieces[0].shape[0])
    )
    run_max, run_total, run_acc = running
    attended = (
        (run_acc / run_total[:, :, None])
        .transpose(1, 0, 2)
        .reshape(token_count, local_feat)
        .astype(jnp.bfloat16)
    )
    local_width = hidden.shape[1]
    projected = (
        lax.psum_scatter(
            jnp.einsum(
                "fd,cf->dc", out_weight, attended, preferred_element_type=jnp.float32
            ).astype(jnp.bfloat16),
            "head",
            scatter_dimension=0,
            tiled=True,
        )
        .astype(jnp.float32)
        .T
    )
    steps_count = gate_table.shape[0]
    onehot = (frame_step[:, None] == jnp.arange(steps_count, dtype=jnp.int32)[None, :]).astype(
        jnp.float32
    )
    gate_rows = jnp.dot(onehot, gate_table, precision=lax.Precision.HIGHEST)
    frames_here = frame_step.shape[0]
    gated = projected.reshape(frames_here, FRAME_TOK, local_width) * gate_rows[:, None, :]
    return (hidden.astype(jnp.float32) + gated.reshape(token_count, local_width)).astype(
        jnp.bfloat16
    )


def solution(mesh):
    in_specs = (
        P("seq", "head"),
        P("seq", "head"),
        P("seq", "head"),
        P("seq", "head"),
        P("head"),
        P("head"),
        P("seq", "head"),
        P("seq", "head"),
        P("seq"),
        P("head", None),
        P(None, "head"),
        P("seq"),
    )
    out_specs = P("seq", "head")
    return jax.shard_map(shards, mesh=mesh, in_specs=in_specs, out_specs=out_specs, check_vma=False)
```

profile of v0, /device:TPU:16, one launch (start us, length us, event | category | flops | bytes accessed | tf_op | source)
XLA Modules:
  0.0 426.5 jit_solution(9837051302664190493)
XLA Ops:
  6.5 0.0 copy-start
  6.5 0.0 all-gather.5.cloned.1.call-start
  6.5 0.9 fusion.29
  7.4 19.7 %all-reduce.1 = (f32[32]{0:T(128)S(1)}, f32[32]{0:T(128)S(1)}) all-reduce(f32[32]{0:T(128)S(1)} %get-tuple-element.323, f32[32]{0:T(128)S(1)} %get-tuple-element.324), channel_id=1, replica_groups=mesh['head'=8,'seq'=64] {'head'}, use_global_device_ids=true, to_apply=%region_1.0 | all-reduce | flops 64 | bytes 512 | tf_op jit(solution)/shard_map/psum | solution.py:87
  27.2 1.4 fusion.31
  28.6 0.0 all-gather.5.cloned.1.call-update
  28.6 0.0 all-gather.7.cloned.1.call-start
  28.7 0.7 all-gather.7.cloned.1.call-update
  29.4 0.0 all-gather.9.cloned.1.call-start
  29.4 0.7 all-gather.9.cloned.1.call-update
  30.1 0.0 all-gather.11.cloned.1.call-start
  30.2 0.5 all-gather.11.cloned.1.call-update
  30.7 0.0 reduce-scatter.4.cloned.1.call-start
  31.4 1.3 dynamic-slice.6
  32.7 0.7 dynamic-update-slice.3
  33.4 28.0 %all-reduce = s32[64]{0:T(128)S(1)} all-reduce(s32[64]{0:T(128)S(1)} %dynamic-update-slice.3), channel_id=1, replica_groups=mesh['head'=8,'seq'=64] {'seq'}, use_global_device_ids=true, to_apply=%add | all-reduce | flops 64 | bytes 512
  61.4 0.7 fusion.49
  62.1 0.7 fusion.50
  62.8 0.7 fusion.47
  63.5 0.8 add_add_fusion.1
  64.3 4.4 %compare_select_fusion.1 = (s32[2048,1]{0,1:T(1,128)S(1)}, s32[2048,1]{0,1:T(1,128)S(1)}) fusion(s32[]{:T(128)} %bitcast.63, s32[]{:T(128)} %bitcast.64, s32[]{:T(128)} %bitcast.65, s32[]{:T(128)} %bitcast.66, s32[]{:T(128)} %bitcast.67, s32[]{:T(128)} %bitcast.69, s32[]{:T(128)} %bitcast.68, s32[2048,1]{0,1:T(1,128)S(1)} %bitcast.131, ...), kind=kLoop, calls=%fused_computation.112 | loop fusion | flops 28672 | bytes 32796 | tf_op jit(solution)/shard_map/jit(_take)/gather | solution.py:65
  68.7 1.4 compare_reduce_fusion.56
  70.1 0.7 fusion.48
  70.9 35.8 %select_select_fusion = s32[2048]{0:T(1024)S(1)} fusion(pred[2048]{0:T(1024)(128)(4,1)S(1)} %get-tuple-element.214, pred[2048]{0:T(1024)(128)(4,1)S(1)} %get-tuple-element.213, pred[2048]{0:T(1024)(128)(4,1)S(1)} %get-tuple-element.212, pred[2048]{0:T(1024)(128)(4,1)S(1)} %get-tuple-element.211, pred[2048]{0:T(1024)(128)(4,1)S(1)} %get-tuple-element.210, ...), kind=kLoop, calls=%fused_computation.130 | loop fusion | flops 116736 | bytes 133348 | tf_op jit(solution)/shard_map/jit(_take)/gather | solution.py:65
  106.8 0.8 copy_bitcast_fusion
  107.6 5.9 %all-gather.5.cloned.1.call-done = bf16[2048,384]{1,0:T(8,128)(2,1)} async-done(((bf16[32,384]{1,0:T(8,128)(2,1)}), bf16[2048,384]{1,0:T(8,128)(2,1)}) %all-gather.5.cloned.1.call-update) | async-done | bytes 1572880 | tf_op jit(solution)/shard_map/all_gather | solution.py:104
  113.5 3.9 reshape.339
  117.4 1.4 copy.26
  118.8 77.9 %all-gather.7.cloned.1.call-done = bf16[2048,384]{1,0:T(8,128)(2,1)} async-done(((bf16[32,384]{1,0:T(8,128)(2,1)}), bf16[2048,384]{1,0:T(8,128)(2,1)}) %all-gather.7.cloned.1.call-update) | async-done | bytes 1572880 | tf_op jit(solution)/shard_map/all_gather | solution.py:105
  196.7 3.9 reshape.340
  200.6 1.4 copy.28
  202.0 78.0 %all-gather.9.cloned.1.call-done = bf16[2048,384]{1,0:T(8,128)(2,1)} async-done(((bf16[32,384]{1,0:T(8,128)(2,1)}), bf16[2048,384]{1,0:T(8,128)(2,1)}) %all-gather.9.cloned.1.call-update) | async-done | bytes 1572880 | tf_op jit(solution)/shard_map/all_gather | solution.py:109
  280.0 5.1 %reshape.341 = bf16[2,1024,3,128]{3,2,1,0:T(4,128)(2,1)} reshape(bf16[2048,384]{1,0:T(8,128)(2,1)} %all-gather.9.cloned.1.call-done) | data formatting | bytes 3145728 | tf_op jit(solution)/shard_map/reshape;reshape | solution.py:44
  285.1 1.8 copy.31
  286.9 6.6 %while.31 = (s32[]{:T(128)}, f32[3,32]{1,0:T(4,128)S(1)}, f32[3,32]{1,0:T(4,128)S(1)}, f32[3,32,128]{2,1,0:T(8,128)S(1)}, bf16[2,1024,3,128]{3,1,2,0:T(8,128)(2,...) while((s32[]{:T(128)}, f32[3,32]{1,0:T(4,128)S(1)}, ...), condition=%wide.region_7.8_spmd.clone, body=%wide.region_4.7_spmd.clone.sunk | while | flops 50958816 | bytes 2882665 | solution.py:51
  286.9 1.6 fusion.77
  288.5 0.2 fusion.78
  288.7 1.5 convolution_add_fusion.5
  290.2 1.6 fusion.77
  291.8 0.2 fusion.78
  292.1 1.4 convolution_add_fusion.5
  293.5 69.5 %all-gather.11.cloned.1.call-done = bf16[2048,384]{1,0:T(8,128)(2,1)} async-done(((bf16[32,384]{1,0:T(8,128)(2,1)}), bf16[2048,384]{1,0:T(8,128)(2,1)}) %all-gather.11.cloned.1.call-update) | async-done | bytes 1572880 | tf_op jit(solution)/shard_map/all_gather | solution.py:110
  363.1 5.1 %reshape.342 = bf16[2,1024,3,128]{3,2,1,0:T(4,128)(2,1)} reshape(bf16[2048,384]{1,0:T(8,128)(2,1)} %all-gather.11.cloned.1.call-done) | data formatting | bytes 3145728 | tf_op jit(solution)/shard_map/reshape;reshape | solution.py:45
  368.2 1.8 copy.33
  370.0 2.2 while.30
  370.0 0.5 fusion.72
  370.5 0.2 fusion.73
  370.7 0.3 convolution_add_fusion.4
  371.1 0.5 fusion.72
  371.6 0.2 fusion.73
  371.8 0.3 convolution_add_fusion.4
  372.2 3.0 fusion.27
  375.1 0.0 copy-start.1
  375.1 1.4 copy.43
  376.5 0.0 reduce-scatter.4.cloned.1.call-update
  377.2 0.0 copy-done
  377.2 0.2 convolution_reduce_fusion
  377.4 40.9 %reduce-scatter.4.cloned.1.call-done = bf16[640,32]{1,0:T(8,128)(2,1)} async-done(((bf16[5120,32]{1,0:T(8,128)(2,1)}), bf16[640,32]{1,0:T(8,128)(2,1)}) %reduce-scatter.4.cloned.1.call-update) | async-done | bytes 40976
  418.3 1.0 copy.44
  419.3 0.0 copy-done.1
  419.3 0.6 fusion.28
  (23 shorter events, 0.2 us)
Async XLA Ops:
  6.5 370.7 %copy-start = (f32[50,640]{1,0:T(8,128)S(1)}, f32[50,640]{1,0:T(8,128)}, u32[]{:S(2)}) copy-start(f32[50,640]{1,0:T(8,128)} %param.28) | copy-start | bytes 384004
  6.5 106.9 %all-gather.5.cloned.1.call-start = ((), (), s32[]{:S(2)}) async-start(), calls=%async_computation.1 | async-start | bytes 1597440 | tf_op jit(solution)/shard_map/all_gather | solution.py:104
  28.6 168.1 %all-gather.7.cloned.1.call-start = ((), (), s32[]{:S(2)}) async-start(), calls=%async_computation.2 | async-start | bytes 1597440 | tf_op jit(solution)/shard_map/all_gather | solution.py:105
  29.4 250.6 %all-gather.9.cloned.1.call-start = ((), (), s32[]{:S(2)}) async-start(), calls=%async_computation.3 | async-start | bytes 1597440 | tf_op jit(solution)/shard_map/all_gather | solution.py:109
  30.1 332.9 %all-gather.11.cloned.1.call-start = ((), (), s32[]{:S(2)}) async-start(), calls=%async_computation.4 | async-start | bytes 1597440 | tf_op jit(solution)/shard_map/all_gather | solution.py:110
  30.7 387.6 %reduce-scatter.4.cloned.1.call-start = ((), (), s32[]{:S(2)}) async-start(), calls=%async_computation.5 | async-start | bytes 1474560
  375.1 44.2 %copy-start.1 = (bf16[32,640]{1,0:T(8,128)(2,1)S(1)}, bf16[32,640]{1,0:T(8,128)(2,1)}, u32[]{:S(2)}) copy-start(bf16[32,640]{1,0:T(8,128)(2,1)} %param.18) | copy-start | bytes 122884
Sparse Core Ops, SparseCore 0:
  28.7 84.6 all-gather.4
  116.8 79.8 all-gather.6
  200.1 79.8 all-gather.8
  283.2 79.8 all-gather.10
  376.7 41.5 reduce-scatter.3
where the time goes:
time: 428 us; the launch traced here: 426 us
  waiting for transfers between devices  274 us (64%)
  blocking collectives  47.7 us (11%)
  other arithmetic  47.2 us (11%)
  local copies, waits for them, and re-layouts  31.9 us (7%)
  between operations  14.6 us (3%)
  matrix products  10.8 us (3%)
    all_gather x1, waiting for transfers between devices, shards(): lax.all_gather(ref_key, 'seq', axis=0, tiled=True)  78 us
    all_gather x1, waiting for transfers between devices, shards(): lax.all_gather(value, 'seq', axis=0, tiled=True)  77.9 us
    all_gather x1, waiting for transfers between devices, shards(): lax.all_gather(ref_value, 'seq', axis=0, tiled=True)  69.5 us
    unnamed x6, waiting for transfers between devices  42.8 us
    gather x3, other arithmetic, live_rows(): jnp.repeat(counts, slots, total_repeat_length=row_count)  41.6 us
    unnamed x1, blocking collectives  28 us
    psum x1, blocking collectives, shards(): lax.psum((jnp.sum(query_float * query_float, axis=1), jnp.sum(key_float *...  19.7 us
    another operation x2, local copies, waits for them, and re-layouts, attend_rows(): key_blocks = key_rows.reshape(block_count, block_rows, head_count, HEAD_DIM)  9.03 us
  transfers between devices with their start and end apart: 5, of which 5 were waited for; matrix products, arithmetic and copies ran while one was open for 17% of the time, Pallas kernels for 0%

commit v1 on v0

v1 whole, which is shorter than its diff:
```python
import math

import jax
import jax.numpy as jnp
from jax import lax
from jax.experimental import pallas as pl
from jax.experimental.pallas import tpu as pltpu
from jax.sharding import Mesh
from jax.sharding import PartitionSpec as P

HEAD_DIM = 128
HEADS = 3
FEAT = HEADS * HEAD_DIM
ROWS = 32
WIDTH = 640
ALL_FEATURES = 3072
EPSILON = 1e-06
NEGATIVE = -1e30
SCALE = 1.0 / math.sqrt(HEAD_DIM)
BF = jnp.bfloat16
F32 = jnp.float32

HEAD_AXES = ("yl", "x")
SEQ_AXES = ("z", "yh", "c")
KEY_AXES = ("yh", "c")
QUERY_AXES = "z"
QB = 8
KB = 8
HB = 8


def call(kernel, out_shape, *args, in_specs=None):
    return pl.pallas_call(
        kernel,
        out_shape=out_shape,
        in_specs=in_specs or [pl.BlockSpec(memory_space=pltpu.VMEM)] * len(args),
        out_specs=pl.BlockSpec(memory_space=pltpu.VMEM),
        compiler_params=pltpu.CompilerParams(vmem_limit_bytes=24 * 1024 * 1024),
    )(*args)


def token_power(rows):
    wide = rows.astype(F32)
    squares = wide * wide
    part = squares[:, :128] + squares[:, 128:256] + squares[:, 256:]
    return jnp.sum(part.T, axis=0, keepdims=True)


def power_kernel(q_ref, kv_ref, out_ref):
    lines = []
    for g in range(2):
        lines.append(token_power(q_ref[g * 4 : g * 4 + 4].reshape(128, FEAT)))
    for g in range(2):
        lines.append(token_power(kv_ref[g * 4 : g * 4 + 4, :, :FEAT].reshape(128, FEAT)))
    block = jnp.concatenate(lines + [jnp.zeros((4, 128), F32)], axis=0)
    for peer in range(HB):
        out_ref[peer] = block


def attend_kernel(q_ref, kv_ref, pw_ref, gq_ref, gk_ref, out_ref):
    power = jnp.sum(pw_ref[...], axis=0) / ALL_FEATURES
    inverse = lax.rsqrt(power + EPSILON)

    def columns(first):
        tiles = [
            jnp.broadcast_to(inverse[first + g : first + g + 1], (128, 128)).T for g in range(2)
        ]
        return jnp.concatenate(tiles, axis=0)

    inv_q = columns(0)
    inv_k = columns(2)
    n_keys = KB * ROWS
    slot = lax.broadcasted_iota(jnp.int32, (1, n_keys), 1)
    counts = jnp.zeros((1, n_keys), F32)
    for p in range(KB):
        line = kv_ref[p, 0:16, 4 * FEAT :][0:1].astype(F32)
        counts = jnp.where(slot // ROWS == p, jnp.concatenate([line, line], axis=1), counts)
    live = (slot % ROWS).astype(F32) < counts
    lane = lax.broadcasted_iota(jnp.int32, (QB * ROWS, 128), 1)
    stats = jnp.zeros((QB * ROWS, 128), F32)
    contract = (((1,), (1,)), ((), ()))
    for h in range(HEADS):
        cols = slice(h * HEAD_DIM, (h + 1) * HEAD_DIM)

        def part(t):
            return kv_ref[:, :, t * FEAT + h * HEAD_DIM : t * FEAT + (h + 1) * HEAD_DIM].reshape(
                n_keys, HEAD_DIM
            )

        q = q_ref[:, :, cols].reshape(QB * ROWS, HEAD_DIM).astype(F32)
        q = (q * inv_q * gq_ref[:, cols]).astype(BF)
        k = (part(0).astype(F32) * inv_k * gk_ref[:, cols]).astype(BF)
        s1 = lax.dot_general(q, k, contract, preferred_element_type=F32) * SCALE
        s2 = lax.dot_general(q, part(2), contract, preferred_element_type=F32) * SCALE
        s2 = jnp.where(live, s2, NEGATIVE)
        peak = jnp.max(jnp.maximum(s1, s2), axis=1, keepdims=True).astype(BF).astype(F32)
        w1 = jnp.exp(s1 - peak)
        w2 = jnp.where(live, jnp.exp(s2 - peak), 0.0)
        total = jnp.sum(w1 + w2, axis=1, keepdims=True)
        mixed = jnp.dot(w1.astype(BF), part(1), preferred_element_type=F32) + jnp.dot(
            w2.astype(BF), part(3), preferred_element_type=F32
        )
        out_ref[:, :, cols] = (mixed / total).astype(BF).reshape(QB, ROWS, HEAD_DIM)
        high = total.astype(BF).astype(F32)
        stats = jnp.where(lane == h, peak, stats)
        stats = jnp.where(lane == HEADS + h, high, stats)
        stats = jnp.where(lane == 2 * HEADS + h, total - high, stats)
    out_ref[:, :, FEAT:] = stats.astype(BF).reshape(QB, ROWS, 128)


def project_kernel(part_ref, weight_ref, out_ref):
    stats = [part_ref[j, :, FEAT:].astype(F32) for j in range(QB)]
    pieces = []
    for h in range(HEADS):
        peaks = [s[:, h : h + 1] for s in stats]
        totals = [
            s[:, HEADS + h : HEADS + h + 1] + s[:, 2 * HEADS + h : 2 * HEADS + h + 1] for s in stats
        ]
        peak = peaks[0]
        for other in peaks[1:]:
            peak = jnp.maximum(peak, other)
        shares = [t * jnp.exp(m - peak) for t, m in zip(totals, peaks)]
        total = sum(shares)
        cols = slice(h * HEAD_DIM, (h + 1) * HEAD_DIM)
        mixed = sum(part_ref[j, :, cols].astype(F32) * shares[j] for j in range(QB))
        pieces.append((mixed / total).astype(BF))
    attended = jnp.concatenate(pieces, axis=1)
    for w in range(HB):
        out_ref[w] = jnp.dot(
            attended, weight_ref[:, w * WIDTH : (w + 1) * WIDTH], preferred_element_type=F32
        ).astype(BF)


def finish_kernel(step_ref, part_ref, hidden_ref, gate_ref, out_ref):
    projected = part_ref[0].astype(F32)
    for h in range(1, HB):
        projected = projected + part_ref[h].astype(F32)
    gate = gate_ref[pl.ds(step_ref[0], 1), :]
    out_ref[...] = (hidden_ref[...].astype(F32) + gate * projected).astype(BF)


def to_all(block, axes, count):
    spread = jnp.broadcast_to(block[None], (count,) + block.shape)
    return lax.all_to_all(spread, axes, 0, 0, tiled=True)


def shards(
    hidden,
    query,
    key,
    value,
    query_gain,
    key_gain,
    ref_key,
    ref_value,
    ref_count,
    out_weight,
    gate_table,
    frame_step,
):
    counts = jnp.broadcast_to(ref_count.astype(BF)[:, None], (ROWS, 128))
    block = jnp.concatenate([key, value, ref_key, ref_value, counts], axis=1)
    kv = lax.all_gather(block, KEY_AXES, axis=0)
    queries = to_all(query, QUERY_AXES, QB)
    powers = call(power_kernel, jax.ShapeDtypeStruct((HB, 8, 128), F32), queries, kv)
    powers = lax.all_to_all(powers, HEAD_AXES, 0, 0, tiled=True)
    parts = call(
        attend_kernel,
        jax.ShapeDtypeStruct((QB, ROWS, FEAT + 128), BF),
        queries,
        kv,
        powers,
        query_gain[None],
        key_gain[None],
    )
    parts = lax.all_to_all(parts, QUERY_AXES, 0, 0, tiled=True)
    projected = call(
        project_kernel, jax.ShapeDtypeStruct((HB, ROWS, WIDTH), BF), parts, out_weight
    )
    projected = lax.all_to_all(projected, HEAD_AXES, 0, 0, tiled=True)
    vmem = pl.BlockSpec(memory_space=pltpu.VMEM)
    return call(
        finish_kernel,
        jax.ShapeDtypeStruct((ROWS, WIDTH), BF),
        frame_step,
        projected,
        hidden,
        gate_table,
        in_specs=[pl.BlockSpec(memory_space=pltpu.SMEM), vmem, vmem, vmem],
    )


def solution(mesh):
    wide = Mesh(mesh.devices.reshape(2, 4, 8, 4, 2), HEAD_AXES + SEQ_AXES)
    both = P(SEQ_AXES, HEAD_AXES)
    in_specs = (
        both,
        both,
        both,
        both,
        P(HEAD_AXES),
        P(HEAD_AXES),
        both,
        both,
        P(SEQ_AXES),
        P(HEAD_AXES, None),
        P(None, HEAD_AXES),
        P(SEQ_AXES),
    )
    return jax.shard_map(shards, mesh=wide, in_specs=in_specs, out_specs=both, check_vma=False)
```

time: 428 us -> 80.8 us (0.19)
  the two profiles are of different devices: /device:TPU:16 before, /device:TPU:8 now
where the time goes in v1:
time: 80.8 us; the launch traced here: 80 us
  blocking collectives  36.4 us (45%)
  starting transfers between devices  20.9 us (26%)
  waiting for transfers between devices  9.03 us (11%)
  local copies, waits for them, and re-layouts  7.9 us (10%)
  Pallas kernels  4.41 us (5%)
  between operations  1.33 us (2%)
    all_gather x1, blocking collectives, shards(): kv = lax.all_gather(block, KEY_AXES, axis=0)  18.5 us
    all_to_all x1, blocking collectives, shards(): parts = lax.all_to_all(parts, QUERY_AXES, 0, 0, tiled=True)  18 us
    all_to_all x1, starting transfers between devices, to_all(): return lax.all_to_all(spread, axes, 0, 0, tiled=True)  10.3 us
    all_to_all x1, starting transfers between devices, shards(): powers = lax.all_to_all(powers, HEAD_AXES, 0, 0, tiled=True)  5.76 us
    all_to_all x1, waiting for transfers between devices, shards(): projected = lax.all_to_all(projected, HEAD_AXES, 0, 0, tiled=True)  5.54 us
    unnamed x10, local copies, waits for them, and re-layouts  5.1 us
    all_to_all x1, starting transfers between devices, shards(): projected = lax.all_to_all(projected, HEAD_AXES, 0, 0, tiled=True)  4.82 us
    pallas_call x4, Pallas kernels, call(): pl.pallas_call(kernel, out_shape=out_shape, in_specs=in_specs or [pl.Bloc...  4.41 us
  transfers between devices with their start and end apart: 3, of which 2 were waited for; matrix products, arithmetic and copies ran while one was open for 5% of the time, Pallas kernels for 0%

profile of v1, /device:TPU:8, one launch (start us, length us, event | category | flops | bytes accessed | tf_op | source)
XLA Modules:
  0.0 80.0 jit_solution(2109300122591310497)
XLA Ops:
  0.0 1.4 %broadcast_in_dim.20 = bf16[8,32,384]{2,1,0:T(8,128)(2,1)} broadcast(bf16[32,384]{1,0:T(8,128)(2,1)} %param.13), dimensions={1,2} | broadcast | bytes 221184 | tf_op jit(solution)/shard_map/broadcast_in_dim | solution.py:143
  1.4 10.3 %all-to-all-start = ((bf16[8,32,384]{2,1,0:T(8,128)(2,1)}), bf16[8,32,384]{2,1,0:T(8,128)(2,1)S(1)}, u32[]{:S(2)}, u32[]{:S(2)}) async-start(bf16[8,32,384]{2,1,0:T(8,128)(2,1)} %broadcast_in_dim.20), calls=%async_computation | async-start | bytes 393216 | tf_op jit(solution)/shard_map/all_to_all | solution.py:144
  11.7 0.7 constant_dynamic-update-slice_fusion.4
  13.1 0.7 constant_dynamic-update-slice_fusion.3
  13.9 0.7 constant_dynamic-update-slice_fusion.2
  14.6 0.7 constant_dynamic-update-slice_fusion.1
  15.4 18.5 %all-gather = bf16[256,1664]{1,0:T(8,128)(2,1)S(1)} all-gather(bf16[32,1664]{1,0:T(8,128)(2,1)S(1)} %constant_dynamic-update-slice_fusion), channel_id=2, replica_groups=mesh['yl'=2,'x'=4,'z'=8,'yh'=4,'c'=2] {'yh','c'}, dimensions={0}, use_global_device_ids=true | all-gather | bytes 958464 | tf_op jit(solution)/shard_map/all_gather | solution.py:163
  33.9 0.0 all-to-all-done.q_ref
  33.9 0.0 copy-start.1
  33.9 0.0 copy-start.2
  33.9 0.8 shard_map.118
  34.6 5.8 %all-to-all-start.1 = ((f32[8,8,128]{2,1,0:T(8,128)}), f32[8,8,128]{2,1,0:T(8,128)S(1)}, u32[]{:S(2)}, u32[]{:S(2)}) async-start(f32[8,8,128]{2,1,0:T(8,128)} %shard_map.118), calls=%async_computation.1 | async-start | bytes 65536 | tf_op jit(solution)/shard_map/all_to_all | solution.py:166
  40.4 0.7 broadcast_in_dim.23.gq_ref
  41.1 0.7 broadcast_in_dim.24.gk_ref
  41.8 3.5 %all-to-all-done.1.pw_ref = f32[8,8,128]{2,1,0:T(8,128)S(1)} async-done(((f32[8,8,128]{2,1,0:T(8,128)}), f32[8,8,128]{2,1,0:T(8,128)S(1)}, u32[]{:S(2)}, u32[]{:S(2)}) %all-to-all-start.1) | async-done | bytes 32800 | tf_op jit(solution)/shard_map/all_to_all | solution.py:166
  45.2 1.2 %shard_map.119 = bf16[8,32,512]{2,1,0:T(8,128)(2,1)S(1)} custom-call(bf16[8,32,384]{2,1,0:T(8,128)(2,1)S(1)} %all-to-all-done.q_ref, bf16[8,32,1664]{2,1,0:T(8,128)(2,1)S(1)} %bitcast.3, f32[8,8,128]{2,1,0:T(8,128)S(1)} %all-to-all-done.1.pw_ref, f32[1,384]{1,0:T(1,128)S(1)} %broadcast_in_dim.23.gq_ref, f32[1,384]{1,0:T(1,128)S(1)} %broadcast_in_dim.24.gk_ref), custom_call_target="tpu_custom_call" | custom-call | tf_op jit(solution)/shard_map/pallas_call | solution.py:33
  46.4 18.0 %all_to_all.20.part_ref = bf16[8,32,512]{2,1,0:T(8,128)(2,1)S(1)} all-to-all(bf16[8,32,512]{2,1,0:T(8,128)(2,1)S(1)} %shard_map.119), channel_id=1, replica_groups=mesh['yl'=2,'x'=4,'z'=8,'yh'=4,'c'=2] {'z'}, dimensions={0} | all-to-all | bytes 524288 | tf_op jit(solution)/shard_map/all_to_all | solution.py:176
  64.4 0.0 copy-start
  64.4 2.1 %copy-done = bf16[384,5120]{1,0:T(8,128)(2,1)S(1)} copy-done((bf16[384,5120]{1,0:T(8,128)(2,1)S(1)}, bf16[384,5120]{1,0:T(8,128)(2,1)}, u32[]{:S(2)}) %copy-start) | copy-done | bytes 3932184
  66.5 1.8 %shard_map.120 = bf16[8,32,640]{2,1,0:T(8,128)(2,1)} custom-call(bf16[8,32,512]{2,1,0:T(8,128)(2,1)S(1)} %all_to_all.20.part_ref, bf16[384,5120]{1,0:T(8,128)(2,1)S(1)} %copy-done), custom_call_target="tpu_custom_call" | custom-call | tf_op jit(solution)/shard_map/pallas_call | solution.py:33
  68.3 4.8 %all-to-all-start.3 = ((bf16[8,32,640]{2,1,0:T(8,128)(2,1)}), bf16[8,32,640]{2,1,0:T(8,128)(2,1)S(1)}, u32[]{:S(2)}, u32[]{:S(2)}) async-start(bf16[8,32,640]{2,1,0:T(8,128)(2,1)} %shard_map.120), calls=%async_computation.3 | async-start | bytes 655360 | tf_op jit(solution)/shard_map/all_to_all | solution.py:180
  73.8 5.5 %all-to-all-done.3.part_ref = bf16[8,32,640]{2,1,0:T(8,128)(2,1)S(1)} async-done(((bf16[8,32,640]{2,1,0:T(8,128)(2,1)}), bf16[8,32,640]{2,1,0:T(8,128)(2,1)S(1)}, u32[]{:S(2)}, u32[]{:S(2)}) %all-to-all-start.3) | async-done | bytes 327712 | tf_op jit(solution)/shard_map/all_to_all | solution.py:180
  79.3 0.0 copy-done.1
  79.3 0.0 copy-done.2
  79.3 0.7 shard_map.121
  (1 shorter events, 0.0 us)
Async XLA Ops:
  1.4 32.4 %all-to-all-start = ((bf16[8,32,384]{2,1,0:T(8,128)(2,1)}), bf16[8,32,384]{2,1,0:T(8,128)(2,1)S(1)}, u32[]{:S(2)}, u32[]{:S(2)}) async-start(bf16[8,32,384]{2,1,0:T(8,128)(2,1)} %broadcast_in_dim.20), calls=%async_computation | async-start | bytes 393216 | tf_op jit(solution)/shard_map/all_to_all | solution.py:144
  33.9 45.5 %copy-start.1 = (f32[50,640]{1,0:T(8,128)S(1)}, f32[50,640]{1,0:T(8,128)}, u32[]{:S(2)}) copy-start(f32[50,640]{1,0:T(8,128)} %gate_ref.1) | copy-start | bytes 384004
  33.9 45.5 %copy-start.2 = (bf16[32,640]{1,0:T(8,128)(2,1)S(1)}, bf16[32,640]{1,0:T(8,128)(2,1)}, u32[]{:S(2)}) copy-start(bf16[32,640]{1,0:T(8,128)(2,1)} %hidden_ref.1) | copy-start | bytes 122884
  34.6 10.6 %all-to-all-start.1 = ((f32[8,8,128]{2,1,0:T(8,128)}), f32[8,8,128]{2,1,0:T(8,128)S(1)}, u32[]{:S(2)}, u32[]{:S(2)}) async-start(f32[8,8,128]{2,1,0:T(8,128)} %shard_map.118), calls=%async_computation.1 | async-start | bytes 65536 | tf_op jit(solution)/shard_map/all_to_all | solution.py:166
  64.4 2.1 %copy-start = (bf16[384,5120]{1,0:T(8,128)(2,1)S(1)}, bf16[384,5120]{1,0:T(8,128)(2,1)}, u32[]{:S(2)}) copy-start(bf16[384,5120]{1,0:T(8,128)(2,1)} %weight_ref.1) | copy-start | bytes 11796484
  68.3 11.0 %all-to-all-start.3 = ((bf16[8,32,640]{2,1,0:T(8,128)(2,1)}), bf16[8,32,640]{2,1,0:T(8,128)(2,1)S(1)}, u32[]{:S(2)}, u32[]{:S(2)}) async-start(bf16[8,32,640]{2,1,0:T(8,128)(2,1)} %shard_map.120), calls=%async_computation.3 | async-start | bytes 655360 | tf_op jit(solution)/shard_map/all_to_all | solution.py:180

commit v2 on v1

--- a/solution.py
+++ b/solution.py
@@ -29,14 +29,27 @@
 HB = 8
 
 
-def call(kernel, out_shape, *args, in_specs=None):
+def call(kernel, out_shape, *args, in_specs=None, n_out=1, cost=1, mib=16, scratch=()):
+    vmem = pl.BlockSpec(memory_space=pltpu.VMEM)
     return pl.pallas_call(
         kernel,
         out_shape=out_shape,
-        in_specs=in_specs or [pl.BlockSpec(memory_space=pltpu.VMEM)] * len(args),
-        out_specs=pl.BlockSpec(memory_space=pltpu.VMEM),
-        compiler_params=pltpu.CompilerParams(vmem_limit_bytes=24 * 1024 * 1024),
+        in_specs=in_specs or [vmem] * len(args),
+        out_specs=vmem if n_out == 1 else [vmem] * n_out,
+        scratch_shapes=scratch,
+        cost_estimate=pl.CostEstimate(flops=cost, bytes_accessed=cost, transcendentals=0),
+        compiler_params=pltpu.CompilerParams(vmem_limit_bytes=mib * 1024 * 1024),
     )(*args)
+
+
+def pack_kernel(count_ref, q_ref, k_ref, v_ref, rk_ref, rv_ref, qb_ref, kv_ref):
+    query = q_ref[...]
+    for peer in range(QB):
+        qb_ref[peer] = query
+    for t, ref in enumerate((k_ref, v_ref, rk_ref, rv_ref)):
+        kv_ref[:, t * FEAT : (t + 1) * FEAT] = ref[...]
+    count = count_ref[0].astype(F32)
+    kv_ref[:, 4 * FEAT :] = jnp.full((ROWS, 128), count, F32).astype(BF)
 
 
 def token_power(rows):
@@ -108,7 +121,17 @@
     out_ref[:, :, FEAT:] = stats.astype(BF).reshape(QB, ROWS, 128)
 
 
-def project_kernel(part_ref, weight_ref, out_ref):
+def project_kernel(part_ref, weight_hbm, out_ref, weight_ref, sems):
+    copies = [
+        pltpu.make_async_copy(
+            weight_hbm.at[:, w * WIDTH : (w + 1) * WIDTH],
+            weight_ref.at[:, w * WIDTH : (w + 1) * WIDTH],
+            sems.at[w],
+        )
+        for w in range(HB)
+    ]
+    for copy in copies:
+        copy.start()
     stats = [part_ref[j, :, FEAT:].astype(F32) for j in range(QB)]
     pieces = []
     for h in range(HEADS):
@@ -126,6 +149,7 @@
         pieces.append((mixed / total).astype(BF))
     attended = jnp.concatenate(pieces, axis=1)
     for w in range(HB):
+        copies[w].wait()
         out_ref[w] = jnp.dot(
             attended, weight_ref[:, w * WIDTH : (w + 1) * WIDTH], preferred_element_type=F32
         ).astype(BF)
@@ -137,11 +161,6 @@
         projected = projected + part_ref[h].astype(F32)
     gate = gate_ref[pl.ds(step_ref[0], 1), :]
     out_ref[...] = (hidden_ref[...].astype(F32) + gate * projected).astype(BF)
-
-
-def to_all(block, axes, count):
-    spread = jnp.broadcast_to(block[None], (count,) + block.shape)
-    return lax.all_to_all(spread, axes, 0, 0, tiled=True)
 
 
 def shards(
@@ -158,10 +177,26 @@
     gate_table,
     frame_step,
 ):
-    counts = jnp.broadcast_to(ref_count.astype(BF)[:, None], (ROWS, 128))
-    block = jnp.concatenate([key, value, ref_key, ref_value, counts], axis=1)
-    kv = lax.all_gather(block, KEY_AXES, axis=0)
-    queries = to_all(query, QUERY_AXES, QB)
+    vmem = pl.BlockSpec(memory_space=pltpu.VMEM)
+    queries, block = call(
+        pack_kernel,
+        (
+            jax.ShapeDtypeStruct((QB, ROWS, FEAT), BF),
+            jax.ShapeDtypeStruct((ROWS, 4 * FEAT + 128), BF),
+        ),
+        ref_count,
+        query,
+        key,
+        value,
+        ref_key,
+        ref_value,
+        in_specs=[pl.BlockSpec(memory_space=pltpu.SMEM)] + [vmem] * 5,
+        n_out=2,
+        mib=60,
+    )
+    queries = lax.all_to_all(queries, QUERY_AXES, 0, 0, tiled=True)
+    kv = lax.all_gather(block, "yh", axis=0)
+    kv = lax.all_gather(kv, "c", axis=0, tiled=True)
     powers = call(power_kernel, jax.ShapeDtypeStruct((HB, 8, 128), F32), queries, kv)
     powers = lax.all_to_all(powers, HEAD_AXES, 0, 0, tiled=True)
     parts = call(
@@ -172,13 +207,20 @@
         powers,
         query_gain[None],
         key_gain[None],
+        cost=4 * 1024 * 1024,
     )
     parts = lax.all_to_all(parts, QUERY_AXES, 0, 0, tiled=True)
     projected = call(
-        project_kernel, jax.ShapeDtypeStruct((HB, ROWS, WIDTH), BF), parts, out_weight
+        project_kernel,
+        jax.ShapeDtypeStruct((HB, ROWS, WIDTH), BF),
+        parts,
+        out_weight,
+        in_specs=[vmem, pl.BlockSpec(memory_space=pl.ANY)],
+        cost=6 * 1024 * 1024,
+        mib=60,
+        scratch=[pltpu.VMEM(out_weight.shape, BF), pltpu.SemaphoreType.DMA((HB,))],
     )
     projected = lax.all_to_all(projected, HEAD_AXES, 0, 0, tiled=True)
-    vmem = pl.BlockSpec(memory_space=pltpu.VMEM)
     return call(
         finish_kernel,
         jax.ShapeDtypeStruct((ROWS, WIDTH), BF),

time: 80.8 us -> 79.8 us (0.988)
  local copies, waits for them, and re-layouts: 7.9 us -> 1.37 us
  Pallas kernels: 4.41 us -> 8.64 us
  blocking collectives: 36.4 us -> 37.6 us
    unnamed x10 -> x4, local copies, waits for them, and re-layouts: 5.1 us -> 0.01 us
    pallas_call x4 -> x5, Pallas kernels: 4.41 us -> 8.64 us  [call(): pl.pallas_call(kernel, out_shape=out_shape, in_specs=in_specs or [vmem] *...]
    broadcast_in_dim x1 -> x0, local copies, waits for them, and re-layouts: 1.42 us -> none  [to_all(): spread = jnp.broadcast_to(block[None], (count,) + block.shape)]
    all_gather x1 -> x2, blocking collectives: 18.5 us -> 19.7 us  [the longest x1 17.3 us: shards(): kv = lax.all_gather(block, 'yh', axis=0)]
  transfers between devices with their start and end apart: 3 -> 3, of which waited for: 2 -> 2; matrix products, arithmetic and copies ran while one was open for 5% -> 2% of each run, Pallas kernels for 0% -> 0%
where the time goes in v2:
time: 79.8 us; the launch traced here: 79.2 us
  blocking collectives  37.6 us (47%)
  starting transfers between devices  21.2 us (27%)
  waiting for transfers between devices  9.03 us (11%)
  Pallas kernels  8.64 us (11%)
  local copies, waits for them, and re-layouts  1.37 us (2%)
  between operations  1.33 us (2%)
    all_to_all x1, blocking collectives, shards(): parts = lax.all_to_all(parts, QUERY_AXES, 0, 0, tiled=True)  17.9 us
    all_gather x1, blocking collectives, shards(): kv = lax.all_gather(block, 'yh', axis=0)  17.3 us
    all_to_all x1, starting transfers between devices, shards(): queries = lax.all_to_all(queries, QUERY_AXES, 0, 0, tiled=True)  10.3 us
    pallas_call x5, Pallas kernels, call(): pl.pallas_call(kernel, out_shape=out_shape, in_specs=in_specs or [vmem] *...  8.64 us
    all_to_all x1, starting transfers between devices, shards(): powers = lax.all_to_all(powers, HEAD_AXES, 0, 0, tiled=True)  6.14 us
    all_to_all x1, waiting for transfers between devices, shards(): projected = lax.all_to_all(projected, HEAD_AXES, 0, 0, tiled=True)  5.54 us
    all_to_all x1, starting transfers between devices, shards(): projected = lax.all_to_all(projected, HEAD_AXES, 0, 0, tiled=True)  4.78 us
    all_to_all x1, waiting for transfers between devices, shards(): powers = lax.all_to_all(powers, HEAD_AXES, 0, 0, tiled=True)  3.48 us
  transfers between devices with their start and end apart: 3, of which 2 were waited for; matrix products, arithmetic and copies ran while one was open for 2% of the time, Pallas kernels for 0%

profile of v2, /device:TPU:8, one launch (start us, length us, event | category | flops | bytes accessed | tf_op | source)
XLA Modules:
  0.0 79.2 jit_solution(15774542913400489300)
XLA Ops:
  0.7 1.5 %shard_map.118 = (bf16[8,32,384]{2,1,0:T(8,128)(2,1)}, bf16[32,1664]{1,0:T(8,128)(2,1)}) custom-call(s32[1]{0:T(128)S(6)} %copy.13.count_ref, bf16[32,384]{1,0:T(8,128)(2,1)} %q_ref.1, bf16[32,384]{1,0:T(8,128)(2,1)} %k_ref.1, bf16[32,384]{1,0:T(8,128)(2,1)} %v_ref.1, bf16[32,384]{1,0:T(8,128)(2,1)} %rk_ref.1, bf16[32,384]{1,0:T(8,128)(2,1)} %rv_ref.1), custom_call_target="tpu_custom_call" | custom-call | flops 1 | bytes 1 | tf_op jit(solution)/shard_map/pallas_call | solution.py:34
  2.2 10.3 %all-to-all-start = ((bf16[8,32,384]{2,1,0:T(8,128)(2,1)}), bf16[8,32,384]{2,1,0:T(8,128)(2,1)S(1)}, u32[]{:S(2)}, u32[]{:S(2)}) async-start(bf16[8,32,384]{2,1,0:T(8,128)(2,1)} %get-tuple-element.7), calls=%async_computation | async-start | bytes 393216 | tf_op jit(solution)/shard_map/all_to_all | solution.py:197
  12.5 17.3 %all-gather = bf16[128,1664]{1,0:T(8,128)(2,1)S(1)} all-gather(bf16[32,1664]{1,0:T(8,128)(2,1)} %get-tuple-element.8), channel_id=2, replica_groups=mesh['yl'=2,'x'=4,'z'=8,'yh'=4,'c'=2] {'yh'}, dimensions={0}, use_global_device_ids=true | all-gather | bytes 532480 | tf_op jit(solution)/shard_map/all_gather | solution.py:198
  29.9 2.4 %all_gather.11.kv_ref = bf16[8,32,1664]{2,1,0:T(8,128)(2,1)S(1)} all-gather(bf16[4,32,1664]{2,1,0:T(8,128)(2,1)S(1)} %bitcast.1), channel_id=1, replica_groups=mesh['yl'=2,'x'=4,'z'=8,'yh'=4,'c'=2] {'c'}, dimensions={0}, use_global_device_ids=true | all-gather | bytes 1277952 | tf_op jit(solution)/shard_map/all_gather | solution.py:199
  32.3 0.0 copy-start
  32.3 0.0 copy-start.1
  32.3 0.0 all-to-all-done.q_ref
  32.3 0.8 shard_map.119
  33.0 6.1 %all-to-all-start.1 = ((f32[8,8,128]{2,1,0:T(8,128)}), f32[8,8,128]{2,1,0:T(8,128)S(1)}, u32[]{:S(2)}, u32[]{:S(2)}) async-start(f32[8,8,128]{2,1,0:T(8,128)} %shard_map.119), calls=%async_computation.1 | async-start | bytes 65536 | tf_op jit(solution)/shard_map/all_to_all | solution.py:201
  39.2 0.7 broadcast_in_dim.6.gq_ref
  39.9 0.7 broadcast_in_dim.7.gk_ref
  40.5 3.5 %all-to-all-done.1.pw_ref = f32[8,8,128]{2,1,0:T(8,128)S(1)} async-done(((f32[8,8,128]{2,1,0:T(8,128)}), f32[8,8,128]{2,1,0:T(8,128)S(1)}, u32[]{:S(2)}, u32[]{:S(2)}) %all-to-all-start.1) | async-done | bytes 32800 | tf_op jit(solution)/shard_map/all_to_all | solution.py:201
  44.0 1.2 %shard_map.120 = bf16[8,32,512]{2,1,0:T(8,128)(2,1)S(1)} custom-call(bf16[8,32,384]{2,1,0:T(8,128)(2,1)S(1)} %all-to-all-done.q_ref, bf16[8,32,1664]{2,1,0:T(8,128)(2,1)S(1)} %all_gather.11.kv_ref, f32[8,8,128]{2,1,0:T(8,128)S(1)} %all-to-all-done.1.pw_ref, f32[1,384]{1,0:T(1,128)S(1)} %broadcast_in_dim.6.gq_ref, f32[1,384]{1,0:T(1,128)S(1)} %broadcast_in_dim.7.gk_ref), custom_call_target="tpu_custom_call" | custom-call | flops 4194304 | bytes 4194304 | tf_op jit(solution)/shard_map/pallas_call | solution.py:34
  45.2 17.9 %all_to_all.20.part_ref = bf16[8,32,512]{2,1,0:T(8,128)(2,1)} all-to-all(bf16[8,32,512]{2,1,0:T(8,128)(2,1)S(1)} %shard_map.120), channel_id=1, replica_groups=mesh['yl'=2,'x'=4,'z'=8,'yh'=4,'c'=2] {'z'}, dimensions={0} | all-to-all | bytes 524288 | tf_op jit(solution)/shard_map/all_to_all | solution.py:212
  63.1 4.5 %shard_map.121 = bf16[8,32,640]{2,1,0:T(8,128)(2,1)} custom-call(bf16[8,32,512]{2,1,0:T(8,128)(2,1)} %all_to_all.20.part_ref, bf16[384,5120]{1,0:T(8,128)(2,1)} %weight_hbm.1), custom_call_target="tpu_custom_call" | custom-call | flops 6291456 | bytes 6291456 | tf_op jit(solution)/shard_map/pallas_call | solution.py:34
  67.6 4.8 %all-to-all-start.3 = ((bf16[8,32,640]{2,1,0:T(8,128)(2,1)}), bf16[8,32,640]{2,1,0:T(8,128)(2,1)S(1)}, u32[]{:S(2)}, u32[]{:S(2)}) async-start(bf16[8,32,640]{2,1,0:T(8,128)(2,1)} %shard_map.121), calls=%async_computation.3 | async-start | bytes 655360 | tf_op jit(solution)/shard_map/all_to_all | solution.py:223
  73.0 5.5 %all-to-all-done.3.part_ref = bf16[8,32,640]{2,1,0:T(8,128)(2,1)S(1)} async-done(((bf16[8,32,640]{2,1,0:T(8,128)(2,1)}), bf16[8,32,640]{2,1,0:T(8,128)(2,1)S(1)}, u32[]{:S(2)}, u32[]{:S(2)}) %all-to-all-start.3) | async-done | bytes 327712 | tf_op jit(solution)/shard_map/all_to_all | solution.py:223
  78.6 0.0 copy-done
  78.6 0.0 copy-done.1
  78.6 0.7 shard_map.122
Async XLA Ops:
  2.2 30.1 %all-to-all-start = ((bf16[8,32,384]{2,1,0:T(8,128)(2,1)}), bf16[8,32,384]{2,1,0:T(8,128)(2,1)S(1)}, u32[]{:S(2)}, u32[]{:S(2)}) async-start(bf16[8,32,384]{2,1,0:T(8,128)(2,1)} %get-tuple-element.7), calls=%async_computation | async-start | bytes 393216 | tf_op jit(solution)/shard_map/all_to_all | solution.py:197
  32.3 46.3 %copy-start = (f32[50,640]{1,0:T(8,128)S(1)}, f32[50,640]{1,0:T(8,128)}, u32[]{:S(2)}) copy-start(f32[50,640]{1,0:T(8,128)} %gate_ref.1) | copy-start | bytes 384004
  32.3 46.3 %copy-start.1 = (bf16[32,640]{1,0:T(8,128)(2,1)S(1)}, bf16[32,640]{1,0:T(8,128)(2,1)}, u32[]{:S(2)}) copy-start(bf16[32,640]{1,0:T(8,128)(2,1)} %hidden_ref.1) | copy-start | bytes 122884
  33.0 11.0 %all-to-all-start.1 = ((f32[8,8,128]{2,1,0:T(8,128)}), f32[8,8,128]{2,1,0:T(8,128)S(1)}, u32[]{:S(2)}, u32[]{:S(2)}) async-start(f32[8,8,128]{2,1,0:T(8,128)} %shard_map.119), calls=%async_computation.1 | async-start | bytes 65536 | tf_op jit(solution)/shard_map/all_to_all | solution.py:201
  67.6 11.0 %all-to-all-start.3 = ((bf16[8,32,640]{2,1,0:T(8,128)(2,1)}), bf16[8,32,640]{2,1,0:T(8,128)(2,1)S(1)}, u32[]{:S(2)}, u32[]{:S(2)}) async-start(bf16[8,32,640]{2,1,0:T(8,128)(2,1)} %shard_map.121), calls=%async_computation.3 | async-start | bytes 655360 | tf_op jit(solution)/shard_map/all_to_all | solution.py:223

commit v3 on v2

--- a/solution.py
+++ b/solution.py
@@ -12,6 +12,8 @@
 HEADS = 3
 FEAT = HEADS * HEAD_DIM
 ROWS = 32
+STATS = 16
+PIECE = HEADS * ROWS + STATS
 WIDTH = 640
 ALL_FEATURES = 3072
 EPSILON = 1e-06
@@ -70,7 +72,7 @@
         out_ref[peer] = block
 
 
-def attend_kernel(q_ref, kv_ref, pw_ref, gq_ref, gk_ref, out_ref):
+def attend_kernel(q_ref, kv_ref, pw_ref, gq_ref, gk_ref, weight_ref, out_ref):
     power = jnp.sum(pw_ref[...], axis=0) / ALL_FEATURES
     inverse = lax.rsqrt(power + EPSILON)
 
@@ -113,43 +115,41 @@
         mixed = jnp.dot(w1.astype(BF), part(1), preferred_element_type=F32) + jnp.dot(
             w2.astype(BF), part(3), preferred_element_type=F32
         )
-        out_ref[:, :, cols] = (mixed / total).astype(BF).reshape(QB, ROWS, HEAD_DIM)
+        out_ref[:, h * ROWS : (h + 1) * ROWS] = (
+            (mixed / total).astype(BF).reshape(QB, ROWS, HEAD_DIM)
+        )
         high = total.astype(BF).astype(F32)
         stats = jnp.where(lane == h, peak, stats)
         stats = jnp.where(lane == HEADS + h, high, stats)
         stats = jnp.where(lane == 2 * HEADS + h, total - high, stats)
-    out_ref[:, :, FEAT:] = stats.astype(BF).reshape(QB, ROWS, 128)
-
-
-def project_kernel(part_ref, weight_hbm, out_ref, weight_ref, sems):
-    copies = [
-        pltpu.make_async_copy(
-            weight_hbm.at[:, w * WIDTH : (w + 1) * WIDTH],
-            weight_ref.at[:, w * WIDTH : (w + 1) * WIDTH],
-            sems.at[w],
-        )
-        for w in range(HB)
-    ]
-    for copy in copies:
-        copy.start()
-    stats = [part_ref[j, :, FEAT:].astype(F32) for j in range(QB)]
+    for half in range(2):
+        lines = stats[half * 128 : (half + 1) * 128].T[:STATS]
+        for j in range(4):
+            turned = lines if j == 0 else pltpu.roll(lines, 128 - j * ROWS, 1)
+            out_ref[half * 4 + j, HEADS * ROWS :] = turned.astype(BF)
+
+
+def project_kernel(part_ref, weight_ref, out_ref):
+    stats = part_ref[:, HEADS * ROWS :].astype(F32).reshape(QB * STATS, 128).T[:ROWS]
     pieces = []
     for h in range(HEADS):
-        peaks = [s[:, h : h + 1] for s in stats]
-        totals = [
-            s[:, HEADS + h : HEADS + h + 1] + s[:, 2 * HEADS + h : 2 * HEADS + h + 1] for s in stats
-        ]
+
+        def column(j, s):
+            return stats[:, j * STATS + s * HEADS + h : j * STATS + s * HEADS + h + 1]
+
+        peaks = [column(j, 0) for j in range(QB)]
+        totals = [column(j, 1) + column(j, 2) for j in range(QB)]
         peak = peaks[0]
         for other in peaks[1:]:
             peak = jnp.maximum(peak, other)
         shares = [t * jnp.exp(m - peak) for t, m in zip(totals, peaks)]
         total = sum(shares)
-        cols = slice(h * HEAD_DIM, (h + 1) * HEAD_DIM)
-        mixed = sum(part_ref[j, :, cols].astype(F32) * shares[j] for j in range(QB))
+        mixed = sum(
+            part_ref[j, h * ROWS : (h + 1) * ROWS].astype(F32) * shares[j] for j in range(QB)
+        )
         pieces.append((mixed / total).astype(BF))
     attended = jnp.concatenate(pieces, axis=1)
     for w in range(HB):
-        copies[w].wait()
         out_ref[w] = jnp.dot(
             attended, weight_ref[:, w * WIDTH : (w + 1) * WIDTH], preferred_element_type=F32
         ).astype(BF)
@@ -195,18 +195,20 @@
         mib=60,
     )
     queries = lax.all_to_all(queries, QUERY_AXES, 0, 0, tiled=True)
-    kv = lax.all_gather(block, "yh", axis=0)
-    kv = lax.all_gather(kv, "c", axis=0, tiled=True)
+    kv = lax.all_gather(block, KEY_AXES, axis=0)
     powers = call(power_kernel, jax.ShapeDtypeStruct((HB, 8, 128), F32), queries, kv)
     powers = lax.all_to_all(powers, HEAD_AXES, 0, 0, tiled=True)
     parts = call(
         attend_kernel,
-        jax.ShapeDtypeStruct((QB, ROWS, FEAT + 128), BF),
+        jax.ShapeDtypeStruct((QB, PIECE, HEAD_DIM), BF),
         queries,
         kv,
         powers,
         query_gain[None],
         key_gain[None],
+        out_weight,
+        in_specs=[vmem] * 5 + [pl.BlockSpec(memory_space=pl.ANY)],
+        mib=50,
         cost=4 * 1024 * 1024,
     )
     parts = lax.all_to_all(parts, QUERY_AXES, 0, 0, tiled=True)
@@ -215,10 +217,7 @@
         jax.ShapeDtypeStruct((HB, ROWS, WIDTH), BF),
         parts,
         out_weight,
-        in_specs=[vmem, pl.BlockSpec(memory_space=pl.ANY)],
         cost=6 * 1024 * 1024,
-        mib=60,
-        scratch=[pltpu.VMEM(out_weight.shape, BF), pltpu.SemaphoreType.DMA((HB,))],
     )
     projected = lax.all_to_all(projected, HEAD_AXES, 0, 0, tiled=True)
     return call(

time: 79.8 us -> 75.6 us (0.947)
  Pallas kernels: 8.64 us -> 6.35 us
  blocking collectives: 37.6 us -> 36.1 us
    pallas_call x5, Pallas kernels: 8.64 us -> 6.35 us  [call(): pl.pallas_call(kernel, out_shape=out_shape, in_specs=in_specs or [vmem] *...]
    all_gather x2 -> x1, blocking collectives: 19.7 us -> 18.6 us  [shards(): kv = lax.all_gather(block, KEY_AXES, axis=0)]
where the time goes in v3:
time: 75.6 us; the launch traced here: 75.1 us
  blocking collectives  36.1 us (48%)
  starting transfers between devices  20.9 us (28%)
  waiting for transfers between devices  9.03 us (12%)
  Pallas kernels  6.35 us (8%)
  local copies, waits for them, and re-layouts  1.38 us (2%)
  between operations  1.34 us (2%)
    all_gather x1, blocking collectives, shards(): kv = lax.all_gather(block, KEY_AXES, axis=0)  18.6 us
    all_to_all x1, blocking collectives, shards(): parts = lax.all_to_all(parts, QUERY_AXES, 0, 0, tiled=True)  17.5 us
    all_to_all x1, starting transfers between devices, shards(): queries = lax.all_to_all(queries, QUERY_AXES, 0, 0, tiled=True)  10.3 us
    pallas_call x5, Pallas kernels, call(): pl.pallas_call(kernel, out_shape=out_shape, in_specs=in_specs or [vmem] *...  6.35 us
    all_to_all x1, starting transfers between devices, shards(): powers = lax.all_to_all(powers, HEAD_AXES, 0, 0, tiled=True)  5.76 us
    all_to_all x1, waiting for transfers between devices, shards(): projected = lax.all_to_all(projected, HEAD_AXES, 0, 0, tiled=True)  5.54 us
    all_to_all x1, starting transfers between devices, shards(): projected = lax.all_to_all(projected, HEAD_AXES, 0, 0, tiled=True)  4.82 us
    all_to_all x1, waiting for transfers between devices, shards(): powers = lax.all_to_all(powers, HEAD_AXES, 0, 0, tiled=True)  3.48 us
  transfers between devices with their start and end apart: 3, of which 2 were waited for; matrix products, arithmetic and copies ran while one was open for 2% of the time, Pallas kernels for 0%

profile of v3, /device:TPU:8, one launch (start us, length us, event | category | flops | bytes accessed | tf_op | source)
XLA Modules:
  0.0 75.1 jit_solution(15572302036770153092)
XLA Ops:
  0.7 1.5 %shard_map.118 = (bf16[8,32,384]{2,1,0:T(8,128)(2,1)}, bf16[32,1664]{1,0:T(8,128)(2,1)}) custom-call(s32[1]{0:T(128)S(6)} %copy.13.count_ref, bf16[32,384]{1,0:T(8,128)(2,1)} %q_ref.1, bf16[32,384]{1,0:T(8,128)(2,1)} %k_ref.1, bf16[32,384]{1,0:T(8,128)(2,1)} %v_ref.1, bf16[32,384]{1,0:T(8,128)(2,1)} %rk_ref.1, bf16[32,384]{1,0:T(8,128)(2,1)} %rv_ref.1), custom_call_target="tpu_custom_call" | custom-call | flops 1 | bytes 1 | tf_op jit(solution)/shard_map/pallas_call | solution.py:36
  2.2 10.3 %all-to-all-start = ((bf16[8,32,384]{2,1,0:T(8,128)(2,1)}), bf16[8,32,384]{2,1,0:T(8,128)(2,1)S(1)}, u32[]{:S(2)}, u32[]{:S(2)}) async-start(bf16[8,32,384]{2,1,0:T(8,128)(2,1)} %get-tuple-element.7), calls=%async_computation | async-start | bytes 393216 | tf_op jit(solution)/shard_map/all_to_all | solution.py:197
  12.5 18.6 %all-gather = bf16[256,1664]{1,0:T(8,128)(2,1)S(1)} all-gather(bf16[32,1664]{1,0:T(8,128)(2,1)} %get-tuple-element.8), channel_id=2, replica_groups=mesh['yl'=2,'x'=4,'z'=8,'yh'=4,'c'=2] {'yh','c'}, dimensions={0}, use_global_device_ids=true | all-gather | bytes 958464 | tf_op jit(solution)/shard_map/all_gather | solution.py:198
  31.1 0.0 all-to-all-done.q_ref
  31.1 0.8 %shard_map.119 = f32[8,8,128]{2,1,0:T(8,128)} custom-call(bf16[8,32,384]{2,1,0:T(8,128)(2,1)S(1)} %all-to-all-done.q_ref, bf16[8,32,1664]{2,1,0:T(8,128)(2,1)S(1)} %bitcast.1), custom_call_target="tpu_custom_call" | custom-call | flops 1 | bytes 1 | tf_op jit(solution)/shard_map/pallas_call | solution.py:36
  31.9 5.8 %all-to-all-start.1 = ((f32[8,8,128]{2,1,0:T(8,128)}), f32[8,8,128]{2,1,0:T(8,128)S(1)}, u32[]{:S(2)}, u32[]{:S(2)}) async-start(f32[8,8,128]{2,1,0:T(8,128)} %shard_map.119), calls=%async_computation.1 | async-start | bytes 65536 | tf_op jit(solution)/shard_map/all_to_all | solution.py:200
  37.7 0.7 broadcast_in_dim.6.gq_ref
  38.3 0.7 broadcast_in_dim.7.gk_ref
  39.0 3.5 %all-to-all-done.1.pw_ref = f32[8,8,128]{2,1,0:T(8,128)S(1)} async-done(((f32[8,8,128]{2,1,0:T(8,128)}), f32[8,8,128]{2,1,0:T(8,128)S(1)}, u32[]{:S(2)}, u32[]{:S(2)}) %all-to-all-start.1) | async-done | bytes 32800 | tf_op jit(solution)/shard_map/all_to_all | solution.py:200
  42.5 0.0 copy-start
  42.5 1.3 %shard_map.120 = bf16[8,112,128]{2,1,0:T(8,128)(2,1)S(1)} custom-call(bf16[8,32,384]{2,1,0:T(8,128)(2,1)S(1)} %all-to-all-done.q_ref, bf16[8,32,1664]{2,1,0:T(8,128)(2,1)S(1)} %bitcast.2, f32[8,8,128]{2,1,0:T(8,128)S(1)} %all-to-all-done.1.pw_ref, f32[1,384]{1,0:T(1,128)S(1)} %broadcast_in_dim.6.gq_ref, f32[1,384]{1,0:T(1,128)S(1)} %broadcast_in_dim.7.gk_ref, ...), custom_call_target="tpu_custom_call" | custom-call | flops 4194304 | bytes 4194304 | tf_op jit(solution)/shard_map/pallas_call | solution.py:36
  43.8 0.0 copy-start.1
  43.8 0.0 copy-start.2
  43.8 17.5 %all_to_all.20.part_ref = bf16[8,112,128]{2,1,0:T(8,128)(2,1)S(1)} all-to-all(bf16[8,112,128]{2,1,0:T(8,128)(2,1)S(1)} %shard_map.120), channel_id=1, replica_groups=mesh['yl'=2,'x'=4,'z'=8,'yh'=4,'c'=2] {'z'}, dimensions={0} | all-to-all | bytes 458752 | tf_op jit(solution)/shard_map/all_to_all | solution.py:214
  61.3 0.0 copy-done
  61.3 2.1 %shard_map.121 = bf16[8,32,640]{2,1,0:T(8,128)(2,1)} custom-call(bf16[8,112,128]{2,1,0:T(8,128)(2,1)S(1)} %all_to_all.20.part_ref, bf16[384,5120]{1,0:T(8,128)(2,1)S(1)} %copy-done), custom_call_target="tpu_custom_call" | custom-call | flops 6291456 | bytes 6291456 | tf_op jit(solution)/shard_map/pallas_call | solution.py:36
  63.4 4.8 %all-to-all-start.3 = ((bf16[8,32,640]{2,1,0:T(8,128)(2,1)}), bf16[8,32,640]{2,1,0:T(8,128)(2,1)S(1)}, u32[]{:S(2)}, u32[]{:S(2)}) async-start(bf16[8,32,640]{2,1,0:T(8,128)(2,1)} %shard_map.121), calls=%async_computation.3 | async-start | bytes 655360 | tf_op jit(solution)/shard_map/all_to_all | solution.py:222
  68.9 5.5 %all-to-all-done.3.part_ref = bf16[8,32,640]{2,1,0:T(8,128)(2,1)S(1)} async-done(((bf16[8,32,640]{2,1,0:T(8,128)(2,1)}), bf16[8,32,640]{2,1,0:T(8,128)(2,1)S(1)}, u32[]{:S(2)}, u32[]{:S(2)}) %all-to-all-start.3) | async-done | bytes 327712 | tf_op jit(solution)/shard_map/all_to_all | solution.py:222
  74.4 0.0 copy-done.1
  74.4 0.0 copy-done.2
  74.4 0.7 shard_map.122
Async XLA Ops:
  2.2 28.9 %all-to-all-start = ((bf16[8,32,384]{2,1,0:T(8,128)(2,1)}), bf16[8,32,384]{2,1,0:T(8,128)(2,1)S(1)}, u32[]{:S(2)}, u32[]{:S(2)}) async-start(bf16[8,32,384]{2,1,0:T(8,128)(2,1)} %get-tuple-element.7), calls=%async_computation | async-start | bytes 393216 | tf_op jit(solution)/shard_map/all_to_all | solution.py:197
  31.9 10.6 %all-to-all-start.1 = ((f32[8,8,128]{2,1,0:T(8,128)}), f32[8,8,128]{2,1,0:T(8,128)S(1)}, u32[]{:S(2)}, u32[]{:S(2)}) async-start(f32[8,8,128]{2,1,0:T(8,128)} %shard_map.119), calls=%async_computation.1 | async-start | bytes 65536 | tf_op jit(solution)/shard_map/all_to_all | solution.py:200
  42.5 18.8 %copy-start = (bf16[384,5120]{1,0:T(8,128)(2,1)S(1)}, bf16[384,5120]{1,0:T(8,128)(2,1)}, u32[]{:S(2)}) copy-start(bf16[384,5120]{1,0:T(8,128)(2,1)} %weight_ref.3) | copy-start | bytes 11796484
  43.8 30.6 %copy-start.1 = (f32[50,640]{1,0:T(8,128)S(1)}, f32[50,640]{1,0:T(8,128)}, u32[]{:S(2)}) copy-start(f32[50,640]{1,0:T(8,128)} %gate_ref.1) | copy-start | bytes 384004
  43.8 30.6 %copy-start.2 = (bf16[32,640]{1,0:T(8,128)(2,1)S(1)}, bf16[32,640]{1,0:T(8,128)(2,1)}, u32[]{:S(2)}) copy-start(bf16[32,640]{1,0:T(8,128)(2,1)} %hidden_ref.1) | copy-start | bytes 122884
  63.4 11.0 %all-to-all-start.3 = ((bf16[8,32,640]{2,1,0:T(8,128)(2,1)}), bf16[8,32,640]{2,1,0:T(8,128)(2,1)S(1)}, u32[]{:S(2)}, u32[]{:S(2)}) async-start(bf16[8,32,640]{2,1,0:T(8,128)(2,1)} %shard_map.121), calls=%async_computation.3 | async-start | bytes 655360 | tf_op jit(solution)/shard_map/all_to_all | solution.py:222

commit v4 on v3

--- a/solution.py
+++ b/solution.py
@@ -44,46 +44,37 @@
     )(*args)
 
 
-def pack_kernel(count_ref, q_ref, k_ref, v_ref, rk_ref, rv_ref, qb_ref, kv_ref):
-    query = q_ref[...]
-    for peer in range(QB):
-        qb_ref[peer] = query
-    for t, ref in enumerate((k_ref, v_ref, rk_ref, rv_ref)):
-        kv_ref[:, t * FEAT : (t + 1) * FEAT] = ref[...]
-    count = count_ref[0].astype(F32)
-    kv_ref[:, 4 * FEAT :] = jnp.full((ROWS, 128), count, F32).astype(BF)
-
-
-def token_power(rows):
+def power_kernel(q_ref, k_ref, out_ref):
+    rows = jnp.concatenate([q_ref[...], k_ref[...], q_ref[...], k_ref[...]], axis=0)
     wide = rows.astype(F32)
     squares = wide * wide
     part = squares[:, :128] + squares[:, 128:256] + squares[:, 256:]
-    return jnp.sum(part.T, axis=0, keepdims=True)
-
-
-def power_kernel(q_ref, kv_ref, out_ref):
-    lines = []
-    for g in range(2):
-        lines.append(token_power(q_ref[g * 4 : g * 4 + 4].reshape(128, FEAT)))
-    for g in range(2):
-        lines.append(token_power(kv_ref[g * 4 : g * 4 + 4, :, :FEAT].reshape(128, FEAT)))
-    block = jnp.concatenate(lines + [jnp.zeros((4, 128), F32)], axis=0)
+    block = jnp.broadcast_to(jnp.sum(part.T, axis=0, keepdims=True), (8, 128))
     for peer in range(HB):
         out_ref[peer] = block
 
 
-def attend_kernel(q_ref, kv_ref, pw_ref, gq_ref, gk_ref, weight_ref, out_ref):
-    power = jnp.sum(pw_ref[...], axis=0) / ALL_FEATURES
-    inverse = lax.rsqrt(power + EPSILON)
-
-    def columns(first):
-        tiles = [
-            jnp.broadcast_to(inverse[first + g : first + g + 1], (128, 128)).T for g in range(2)
-        ]
-        return jnp.concatenate(tiles, axis=0)
-
-    inv_q = columns(0)
-    inv_k = columns(2)
+def stage_kernel(count_ref, q_ref, k_ref, v_ref, rk_ref, rv_ref, out_ref):
+    for t, ref in enumerate((q_ref, k_ref, v_ref, rk_ref, rv_ref)):
+        out_ref[:, t * FEAT : (t + 1) * FEAT] = ref[...]
+    count = count_ref[0].astype(F32)
+    out_ref[:, 5 * FEAT :] = jnp.full((ROWS, 128), count, F32).astype(BF)
+
+
+def pack_kernel(pw_ref, gq_ref, gk_ref, staged_ref, qb_ref, kv_ref):
+    power = jnp.sum(pw_ref[...], axis=0)[0:1] / ALL_FEATURES
+    inverse = jnp.broadcast_to(lax.rsqrt(power + EPSILON), (128, 128)).T
+    inverse = jnp.concatenate([inverse] * HEADS, axis=1)
+    query = staged_ref[:, :FEAT].astype(F32)
+    query = (query * inverse[:ROWS] * gq_ref[...]).astype(BF)
+    for peer in range(QB):
+        qb_ref[peer] = query
+    key = staged_ref[:, FEAT : 2 * FEAT].astype(F32)
+    kv_ref[:, :FEAT] = (key * inverse[ROWS : 2 * ROWS] * gk_ref[...]).astype(BF)
+    kv_ref[:, FEAT:] = staged_ref[:, 2 * FEAT :]
+
+
+def attend_kernel(q_ref, kv_ref, weight_ref, out_ref):
     n_keys = KB * ROWS
     slot = lax.broadcasted_iota(jnp.int32, (1, n_keys), 1)
     counts = jnp.zeros((1, n_keys), F32)
@@ -102,10 +93,8 @@
                 n_keys, HEAD_DIM
             )
 
-        q = q_ref[:, :, cols].reshape(QB * ROWS, HEAD_DIM).astype(F32)
-        q = (q * inv_q * gq_ref[:, cols]).astype(BF)
-        k = (part(0).astype(F32) * inv_k * gk_ref[:, cols]).astype(BF)
-        s1 = lax.dot_general(q, k, contract, preferred_element_type=F32) * SCALE
+        q = q_ref[:, :, cols].reshape(QB * ROWS, HEAD_DIM)
+        s1 = lax.dot_general(q, part(0), contract, preferred_element_type=F32) * SCALE
         s2 = lax.dot_general(q, part(2), contract, preferred_element_type=F32) * SCALE
         s2 = jnp.where(live, s2, NEGATIVE)
         peak = jnp.max(jnp.maximum(s1, s2), axis=1, keepdims=True).astype(BF).astype(F32)
@@ -178,12 +167,13 @@
     frame_step,
 ):
     vmem = pl.BlockSpec(memory_space=pltpu.VMEM)
-    queries, block = call(
-        pack_kernel,
-        (
-            jax.ShapeDtypeStruct((QB, ROWS, FEAT), BF),
-            jax.ShapeDtypeStruct((ROWS, 4 * FEAT + 128), BF),
-        ),
+    powers = call(
+        power_kernel, jax.ShapeDtypeStruct((HB, 8, 128), F32), query, key, mib=60
+    )
+    powers = lax.all_to_all(powers, HEAD_AXES, 0, 0, tiled=True)
+    staged = call(
+        stage_kernel,
+        jax.ShapeDtypeStruct((ROWS, 5 * FEAT + 128), BF),
         ref_count,
         query,
         key,
@@ -191,23 +181,29 @@
         ref_key,
         ref_value,
         in_specs=[pl.BlockSpec(memory_space=pltpu.SMEM)] + [vmem] * 5,
+        mib=52,
+    )
+    queries, block = call(
+        pack_kernel,
+        (
+            jax.ShapeDtypeStruct((QB, ROWS, FEAT), BF),
+            jax.ShapeDtypeStruct((ROWS, 4 * FEAT + 128), BF),
+        ),
+        powers,
+        query_gain[None],
+        key_gain[None],
+        staged,
         n_out=2,
-        mib=60,
     )
     queries = lax.all_to_all(queries, QUERY_AXES, 0, 0, tiled=True)
     kv = lax.all_gather(block, KEY_AXES, axis=0)
-    powers = call(power_kernel, jax.ShapeDtypeStruct((HB, 8, 128), F32), queries, kv)
-    powers = lax.all_to_all(powers, HEAD_AXES, 0, 0, tiled=True)
     parts = call(
         attend_kernel,
         jax.ShapeDtypeStruct((QB, PIECE, HEAD_DIM), BF),
         queries,
         kv,
-        powers,
-        query_gain[None],
-        key_gain[None],
         out_weight,
-        in_specs=[vmem] * 5 + [pl.BlockSpec(memory_space=pl.ANY)],
+        in_specs=[vmem] * 2 + [pl.BlockSpec(memory_space=pl.ANY)],
         mib=50,
         cost=4 * 1024 * 1024,
     )

time: 75.6 us -> 78 us (1.032)
  local copies, waits for them, and re-layouts: 1.38 us -> 5.06 us
  waiting for transfers between devices: 9.03 us -> 5.73 us
  starting transfers between devices: 20.9 us -> 21.8 us
  blocking collectives: 36.1 us -> 37 us
    unnamed x6 -> x16, local copies, waits for them, and re-layouts: 0.02 us -> 3.7 us
    all_to_all x1, waiting for transfers between devices: 3.48 us -> 0.01 us  [shards(): powers = lax.all_to_all(powers, HEAD_AXES, 0, 0, tiled=True)]
    all_to_all x1, starting transfers between devices: 10.3 us -> 6.99 us  [shards(): queries = lax.all_to_all(queries, QUERY_AXES, 0, 0, tiled=True)]
    all_to_all x1, starting transfers between devices: 5.76 us -> 9.09 us  [shards(): powers = lax.all_to_all(powers, HEAD_AXES, 0, 0, tiled=True)]
    all_to_all x1, blocking collectives: 17.5 us -> 18.8 us  [shards(): parts = lax.all_to_all(parts, QUERY_AXES, 0, 0, tiled=True)]
    all_to_all x1, starting transfers between devices: 4.82 us -> 5.75 us  [shards(): projected = lax.all_to_all(projected, HEAD_AXES, 0, 0, tiled=True)]
    pallas_call x5 -> x6, Pallas kernels: 6.35 us -> 6.27 us  [call(): pl.pallas_call(kernel, out_shape=out_shape, in_specs=in_specs or [vmem] *...]
  transfers between devices with their start and end apart: 3 -> 3, of which waited for: 2 -> 1; matrix products, arithmetic and copies ran while one was open for 2% -> 2% of each run, Pallas kernels for 0% -> 0%
where the time goes in v4:
time: 78 us; the launch traced here: 77.2 us
  blocking collectives  37 us (47%)
  starting transfers between devices  21.8 us (28%)
  Pallas kernels  6.27 us (8%)
  waiting for transfers between devices  5.73 us (7%)
  local copies, waits for them, and re-layouts  5.06 us (6%)
  between operations  1.35 us (2%)
    all_to_all x1, blocking collectives, shards(): parts = lax.all_to_all(parts, QUERY_AXES, 0, 0, tiled=True)  18.8 us
    all_gather x1, blocking collectives, shards(): kv = lax.all_gather(block, KEY_AXES, axis=0)  18.2 us
    all_to_all x1, starting transfers between devices, shards(): powers = lax.all_to_all(powers, HEAD_AXES, 0, 0, tiled=True)  9.09 us
    all_to_all x1, starting transfers between devices, shards(): queries = lax.all_to_all(queries, QUERY_AXES, 0, 0, tiled=True)  6.99 us
    pallas_call x6, Pallas kernels, call(): pl.pallas_call(kernel, out_shape=out_shape, in_specs=in_specs or [vmem] *...  6.27 us
    all_to_all x1, starting transfers between devices, shards(): projected = lax.all_to_all(projected, HEAD_AXES, 0, 0, tiled=True)  5.75 us
    all_to_all x1, waiting for transfers between devices, shards(): projected = lax.all_to_all(projected, HEAD_AXES, 0, 0, tiled=True)  5.72 us
    unnamed x16, local copies, waits for them, and re-layouts  3.7 us
  transfers between devices with their start and end apart: 3, of which 1 were waited for; matrix products, arithmetic and copies ran while one was open for 2% of the time, Pallas kernels for 0%

profile of v4, /device:TPU:8, one launch (start us, length us, event | category | flops | bytes accessed | tf_op | source)
XLA Modules:
  0.0 77.2 jit_solution(16911581171911164723)
XLA Ops:
  0.0 1.5 %shard_map.118 = f32[8,8,128]{2,1,0:T(8,128)} custom-call(bf16[32,384]{1,0:T(8,128)(2,1)} %q_ref.3, bf16[32,384]{1,0:T(8,128)(2,1)} %k_ref.3), custom_call_target="tpu_custom_call" | custom-call | flops 1 | bytes 1 | tf_op jit(solution)/shard_map/pallas_call | solution.py:36
  1.5 9.1 %all-to-all-start = ((f32[8,8,128]{2,1,0:T(8,128)}), f32[8,8,128]{2,1,0:T(8,128)S(1)}, u32[]{:S(2)}, u32[]{:S(2)}) async-start(f32[8,8,128]{2,1,0:T(8,128)} %shard_map.118), calls=%async_computation | async-start | bytes 65536 | tf_op jit(solution)/shard_map/all_to_all | solution.py:173
  11.2 0.0 copy-start.2
  11.2 0.7 copy-done.2
  12.0 0.0 copy-start.3
  12.0 0.7 copy-done.3
  12.7 0.0 copy-start.5
  12.7 0.7 copy-done.5
  13.4 0.0 copy-start.6
  13.4 0.7 copy-done.6
  14.2 0.0 copy-start.7
  14.2 0.7 copy-done.7
  14.9 0.7 broadcast_in_dim.6.gq_ref
  15.6 0.7 broadcast_in_dim.7.gk_ref
  16.3 0.0 all-to-all-done.pw_ref
  16.3 0.8 %shard_map.120 = (bf16[8,32,384]{2,1,0:T(8,128)(2,1)}, bf16[32,1664]{1,0:T(8,128)(2,1)S(1)}) custom-call(f32[8,8,128]{2,1,0:T(8,128)S(1)} %all-to-all-done.pw_ref, f32[1,384]{1,0:T(1,128)S(1)} %broadcast_in_dim.6.gq_ref, f32[1,384]{1,0:T(1,128)S(1)} %broadcast_in_dim.7.gk_ref, bf16[32,2048]{1,0:T(8,128)(2,1)S(1)} %shard_map.119.staged_ref), custom_call_target="tpu_custom_call" | custom-call | flops 1 | bytes 1 | tf_op jit(solution)/shard_map/pallas_call | solution.py:36
  17.1 7.0 %all-to-all-start.1 = ((bf16[8,32,384]{2,1,0:T(8,128)(2,1)}), bf16[8,32,384]{2,1,0:T(8,128)(2,1)S(1)}, u32[]{:S(2)}, u32[]{:S(2)}) async-start(bf16[8,32,384]{2,1,0:T(8,128)(2,1)} %get-tuple-element.7), calls=%async_computation.1 | async-start | bytes 393216 | tf_op jit(solution)/shard_map/all_to_all | solution.py:198
  24.1 18.2 %all-gather = bf16[256,1664]{1,0:T(8,128)(2,1)S(1)} all-gather(bf16[32,1664]{1,0:T(8,128)(2,1)S(1)} %get-tuple-element.8), channel_id=2, replica_groups=mesh['yl'=2,'x'=4,'z'=8,'yh'=4,'c'=2] {'yh','c'}, dimensions={0}, use_global_device_ids=true | all-gather | bytes 958464 | tf_op jit(solution)/shard_map/all_gather | solution.py:199
  42.2 0.0 all-to-all-done.1.q_ref
  42.2 0.0 copy-start
  42.2 1.2 %shard_map.121 = bf16[8,112,128]{2,1,0:T(8,128)(2,1)S(1)} custom-call(bf16[8,32,384]{2,1,0:T(8,128)(2,1)S(1)} %all-to-all-done.1.q_ref, bf16[8,32,1664]{2,1,0:T(8,128)(2,1)S(1)} %bitcast.1, bf16[384,5120]{1,0:T(8,128)(2,1)} %weight_ref.3), custom_call_target="tpu_custom_call" | custom-call | flops 4194304 | bytes 4194304 | tf_op jit(solution)/shard_map/pallas_call | solution.py:36
  43.5 0.0 copy-start.1
  43.5 0.0 copy-start.4
  43.5 18.8 %all_to_all.20.part_ref = bf16[8,112,128]{2,1,0:T(8,128)(2,1)S(1)} all-to-all(bf16[8,112,128]{2,1,0:T(8,128)(2,1)S(1)} %shard_map.121), channel_id=1, replica_groups=mesh['yl'=2,'x'=4,'z'=8,'yh'=4,'c'=2] {'z'}, dimensions={0} | all-to-all | bytes 458752 | tf_op jit(solution)/shard_map/all_to_all | solution.py:210
  62.3 0.0 copy-done
  62.3 2.1 %shard_map.122 = bf16[8,32,640]{2,1,0:T(8,128)(2,1)} custom-call(bf16[8,112,128]{2,1,0:T(8,128)(2,1)S(1)} %all_to_all.20.part_ref, bf16[384,5120]{1,0:T(8,128)(2,1)S(1)} %copy-done), custom_call_target="tpu_custom_call" | custom-call | flops 6291456 | bytes 6291456 | tf_op jit(solution)/shard_map/pallas_call | solution.py:36
  64.4 5.8 %all-to-all-start.3 = ((bf16[8,32,640]{2,1,0:T(8,128)(2,1)}), bf16[8,32,640]{2,1,0:T(8,128)(2,1)S(1)}, u32[]{:S(2)}, u32[]{:S(2)}) async-start(bf16[8,32,640]{2,1,0:T(8,128)(2,1)} %shard_map.122), calls=%async_computation.3 | async-start | bytes 655360 | tf_op jit(solution)/shard_map/all_to_all | solution.py:218
  70.8 5.7 %all-to-all-done.3.part_ref = bf16[8,32,640]{2,1,0:T(8,128)(2,1)S(1)} async-done(((bf16[8,32,640]{2,1,0:T(8,128)(2,1)}), bf16[8,32,640]{2,1,0:T(8,128)(2,1)S(1)}, u32[]{:S(2)}, u32[]{:S(2)}) %all-to-all-start.3) | async-done | bytes 327712 | tf_op jit(solution)/shard_map/all_to_all | solution.py:218
  76.5 0.0 copy-done.1
  76.5 0.0 copy-done.4
  76.5 0.7 shard_map.123
  (1 shorter events, 0.0 us)
Async XLA Ops:
  1.5 14.8 %all-to-all-start = ((f32[8,8,128]{2,1,0:T(8,128)}), f32[8,8,128]{2,1,0:T(8,128)S(1)}, u32[]{:S(2)}, u32[]{:S(2)}) async-start(f32[8,8,128]{2,1,0:T(8,128)} %shard_map.118), calls=%async_computation | async-start | bytes 65536 | tf_op jit(solution)/shard_map/all_to_all | solution.py:173
  11.2 0.7 copy-start.2
  12.0 0.7 copy-start.3
  12.7 0.7 copy-start.5
  13.4 0.7 copy-start.6
  14.2 0.7 copy-start.7
  17.1 25.2 %all-to-all-start.1 = ((bf16[8,32,384]{2,1,0:T(8,128)(2,1)}), bf16[8,32,384]{2,1,0:T(8,128)(2,1)S(1)}, u32[]{:S(2)}, u32[]{:S(2)}) async-start(bf16[8,32,384]{2,1,0:T(8,128)(2,1)} %get-tuple-element.7), calls=%async_computation.1 | async-start | bytes 393216 | tf_op jit(solution)/shard_map/all_to_all | solution.py:198
  42.2 20.1 %copy-start = (bf16[384,5120]{1,0:T(8,128)(2,1)S(1)}, bf16[384,5120]{1,0:T(8,128)(2,1)}, u32[]{:S(2)}) copy-start(bf16[384,5120]{1,0:T(8,128)(2,1)} %weight_ref.3) | copy-start | bytes 11796484
  43.5 33.0 %copy-start.1 = (f32[50,640]{1,0:T(8,128)S(1)}, f32[50,640]{1,0:T(8,128)}, u32[]{:S(2)}) copy-start(f32[50,640]{1,0:T(8,128)} %gate_ref.1) | copy-start | bytes 384004
  43.5 33.0 %copy-start.4 = (bf16[32,640]{1,0:T(8,128)(2,1)S(1)}, bf16[32,640]{1,0:T(8,128)(2,1)}, u32[]{:S(2)}) copy-start(bf16[32,640]{1,0:T(8,128)(2,1)} %hidden_ref.1) | copy-start | bytes 122884
  64.4 12.1 %all-to-all-start.3 = ((bf16[8,32,640]{2,1,0:T(8,128)(2,1)}), bf16[8,32,640]{2,1,0:T(8,128)(2,1)S(1)}, u32[]{:S(2)}, u32[]{:S(2)}) async-start(bf16[8,32,640]{2,1,0:T(8,128)(2,1)} %shard_map.122), calls=%async_computation.3 | async-start | bytes 655360 | tf_op jit(solution)/shard_map/all_to_all | solution.py:218

commit v5 on v3

--- a/solution.py
+++ b/solution.py
@@ -44,14 +44,24 @@
     )(*args)
 
 
-def pack_kernel(count_ref, q_ref, k_ref, v_ref, rk_ref, rv_ref, qb_ref, kv_ref):
+def pack_kernel(
+    count_ref, gq_ref, gk_ref, q_ref, k_ref, v_ref, rk_ref, rv_ref, qb_ref, kv_ref
+):
     query = q_ref[...]
     for peer in range(QB):
         qb_ref[peer] = query
     for t, ref in enumerate((k_ref, v_ref, rk_ref, rv_ref)):
         kv_ref[:, t * FEAT : (t + 1) * FEAT] = ref[...]
     count = count_ref[0].astype(F32)
-    kv_ref[:, 4 * FEAT :] = jnp.full((ROWS, 128), count, F32).astype(BF)
+    parts = []
+    for ref in (gq_ref, gk_ref):
+        rest = ref[...]
+        for _ in range(3):
+            part = rest.astype(BF).astype(F32)
+            parts += [part[h * 128 : (h + 1) * 128].reshape(1, 128) for h in range(HEADS)]
+            rest = rest - part
+    lines = [jnp.full((1, 128), count, F32)] + parts + [jnp.zeros((ROWS - 19, 128), F32)]
+    kv_ref[:, 4 * FEAT :] = jnp.concatenate(lines, axis=0).astype(BF)
 
 
 def token_power(rows):
@@ -72,7 +82,7 @@
         out_ref[peer] = block
 
 
-def attend_kernel(q_ref, kv_ref, pw_ref, gq_ref, gk_ref, weight_ref, out_ref):
+def attend_kernel(q_ref, kv_ref, pw_ref, weight_ref, out_ref):
     power = jnp.sum(pw_ref[...], axis=0) / ALL_FEATURES
     inverse = lax.rsqrt(power + EPSILON)
 
@@ -94,8 +104,13 @@
     lane = lax.broadcasted_iota(jnp.int32, (QB * ROWS, 128), 1)
     stats = jnp.zeros((QB * ROWS, 128), F32)
     contract = (((1,), (1,)), ((), ()))
+    extra = kv_ref[0, :, 4 * FEAT :].astype(F32)
     for h in range(HEADS):
         cols = slice(h * HEAD_DIM, (h + 1) * HEAD_DIM)
+
+        def gain(first):
+            rows = [extra[first + t * HEADS + h : first + t * HEADS + h + 1] for t in range(3)]
+            return rows[0] + rows[1] + rows[2]
 
         def part(t):
             return kv_ref[:, :, t * FEAT + h * HEAD_DIM : t * FEAT + (h + 1) * HEAD_DIM].reshape(
@@ -103,8 +118,8 @@
             )
 
         q = q_ref[:, :, cols].reshape(QB * ROWS, HEAD_DIM).astype(F32)
-        q = (q * inv_q * gq_ref[:, cols]).astype(BF)
-        k = (part(0).astype(F32) * inv_k * gk_ref[:, cols]).astype(BF)
+        q = (q * inv_q * gain(1)).astype(BF)
+        k = (part(0).astype(F32) * inv_k * gain(10)).astype(BF)
         s1 = lax.dot_general(q, k, contract, preferred_element_type=F32) * SCALE
         s2 = lax.dot_general(q, part(2), contract, preferred_element_type=F32) * SCALE
         s2 = jnp.where(live, s2, NEGATIVE)
@@ -185,12 +200,14 @@
             jax.ShapeDtypeStruct((ROWS, 4 * FEAT + 128), BF),
         ),
         ref_count,
+        query_gain,
+        key_gain,
         query,
         key,
         value,
         ref_key,
         ref_value,
-        in_specs=[pl.BlockSpec(memory_space=pltpu.SMEM)] + [vmem] * 5,
+        in_specs=[pl.BlockSpec(memory_space=pltpu.SMEM)] + [vmem] * 7,
         n_out=2,
         mib=60,
     )
@@ -204,10 +221,8 @@
         queries,
         kv,
         powers,
-        query_gain[None],
-        key_gain[None],
         out_weight,
-        in_specs=[vmem] * 5 + [pl.BlockSpec(memory_space=pl.ANY)],
+        in_specs=[vmem] * 3 + [pl.BlockSpec(memory_space=pl.ANY)],
         mib=50,
         cost=4 * 1024 * 1024,
     )

time: 75.6 us -> 75 us (level)
  blocking collectives: 36.1 us -> 46.8 us
  starting transfers between devices: 20.9 us -> 15.1 us
  waiting for transfers between devices: 9.03 us -> 5.55 us
  local copies, waits for them, and re-layouts: 1.38 us -> 0.02 us
    all_to_all x0 -> x1, blocking collectives: none -> 10.7 us  [shards(): powers = lax.all_to_all(powers, HEAD_AXES, 0, 0, tiled=True)]
    all_to_all x1 -> x0, starting transfers between devices: 5.76 us -> none  [shards(): powers = lax.all_to_all(powers, HEAD_AXES, 0, 0, tiled=True)]
    all_to_all x1 -> x0, waiting for transfers between devices: 3.48 us -> none  [shards(): powers = lax.all_to_all(powers, HEAD_AXES, 0, 0, tiled=True)]
    broadcast_in_dim x2 -> x0, local copies, waits for them, and re-layouts: 1.37 us -> none  [the longest x1 0.68 us: shards(): query_gain[None]]
  transfers between devices with their start and end apart: 3 -> 2, of which waited for: 2 -> 1; matrix products, arithmetic and copies ran while one was open for 2% -> 0% of each run, Pallas kernels for 0% -> 0%
where the time goes in v5:
time: 75 us; the launch traced here: 74.6 us
  blocking collectives  46.8 us (62%)
  starting transfers between devices  15.1 us (20%)
  Pallas kernels  5.79 us (8%)
  waiting for transfers between devices  5.55 us (7%)
  between operations  1.34 us (2%)
    all_gather x1, blocking collectives, shards(): kv = lax.all_gather(block, KEY_AXES, axis=0)  18.6 us
    all_to_all x1, blocking collectives, shards(): parts = lax.all_to_all(parts, QUERY_AXES, 0, 0, tiled=True)  17.5 us
    all_to_all x1, blocking collectives, shards(): powers = lax.all_to_all(powers, HEAD_AXES, 0, 0, tiled=True)  10.7 us
    all_to_all x1, starting transfers between devices, shards(): queries = lax.all_to_all(queries, QUERY_AXES, 0, 0, tiled=True)  10.3 us
    pallas_call x5, Pallas kernels, call(): pl.pallas_call(kernel, out_shape=out_shape, in_specs=in_specs or [vmem] *...  5.79 us
    all_to_all x1, waiting for transfers between devices, shards(): projected = lax.all_to_all(projected, HEAD_AXES, 0, 0, tiled=True)  5.54 us
    all_to_all x1, starting transfers between devices, shards(): projected = lax.all_to_all(projected, HEAD_AXES, 0, 0, tiled=True)  4.81 us
  transfers between devices with their start and end apart: 2, of which 1 were waited for; matrix products, arithmetic and copies ran while one was open for 0% of the time, Pallas kernels for 0%

profile of v5, /device:TPU:8, one launch (start us, length us, event | category | flops | bytes accessed | tf_op | source)
XLA Modules:
  0.0 74.6 jit_solution(2723862632836540493)
XLA Ops:
  0.7 1.6 %shard_map.118 = (bf16[8,32,384]{2,1,0:T(8,128)(2,1)}, bf16[32,1664]{1,0:T(8,128)(2,1)}) custom-call(s32[1]{0:T(128)S(6)} %copy.13.count_ref, f32[384]{0:T(512)} %gq_ref.1, f32[384]{0:T(512)} %gk_ref.1, bf16[32,384]{1,0:T(8,128)(2,1)} %q_ref.1, bf16[32,384]{1,0:T(8,128)(2,1)} %k_ref.1, bf16[32,384]{1,0:T(8,128)(2,1)} %v_ref.1, bf16[32,384]{1,0:T(8,128)(2,1)} %rk_ref.1, ...), custom_call_target="tpu_custom_call" | custom-call | flops 1 | bytes 1 | tf_op jit(solution)/shard_map/pallas_call | solution.py:36
  2.2 10.3 %all-to-all-start = ((bf16[8,32,384]{2,1,0:T(8,128)(2,1)}), bf16[8,32,384]{2,1,0:T(8,128)(2,1)S(1)}, u32[]{:S(2)}, u32[]{:S(2)}) async-start(bf16[8,32,384]{2,1,0:T(8,128)(2,1)} %get-tuple-element.7), calls=%async_computation | async-start | bytes 393216 | tf_op jit(solution)/shard_map/all_to_all | solution.py:214
  12.6 18.6 %all-gather = bf16[256,1664]{1,0:T(8,128)(2,1)S(1)} all-gather(bf16[32,1664]{1,0:T(8,128)(2,1)} %get-tuple-element.8), channel_id=2, replica_groups=mesh['yl'=2,'x'=4,'z'=8,'yh'=4,'c'=2] {'yh','c'}, dimensions={0}, use_global_device_ids=true | all-gather | bytes 958464 | tf_op jit(solution)/shard_map/all_gather | solution.py:215
  31.2 0.0 all-to-all-done.q_ref
  31.2 0.0 copy-start
  31.2 0.1 shard_map.119
  31.3 10.7 %all_to_all.20.pw_ref = f32[8,8,128]{2,1,0:T(8,128)S(1)} all-to-all(f32[8,8,128]{2,1,0:T(8,128)S(1)} %shard_map.119), channel_id=1, replica_groups=mesh['yl'=2,'x'=4,'z'=8,'yh'=4,'c'=2] {'yl','x'}, dimensions={0} | all-to-all | bytes 65536 | tf_op jit(solution)/shard_map/all_to_all | solution.py:217
  42.0 1.3 %shard_map.120 = bf16[8,112,128]{2,1,0:T(8,128)(2,1)S(1)} custom-call(bf16[8,32,384]{2,1,0:T(8,128)(2,1)S(1)} %all-to-all-done.q_ref, bf16[8,32,1664]{2,1,0:T(8,128)(2,1)S(1)} %bitcast.2, f32[8,8,128]{2,1,0:T(8,128)S(1)} %all_to_all.20.pw_ref, bf16[384,5120]{1,0:T(8,128)(2,1)} %weight_ref.3), custom_call_target="tpu_custom_call" | custom-call | flops 4194304 | bytes 4194304 | tf_op jit(solution)/shard_map/pallas_call | solution.py:36
  43.3 0.0 copy-start.1
  43.3 0.0 copy-start.2
  43.3 17.5 %all_to_all.21.part_ref = bf16[8,112,128]{2,1,0:T(8,128)(2,1)S(1)} all-to-all(bf16[8,112,128]{2,1,0:T(8,128)(2,1)S(1)} %shard_map.120), channel_id=1, replica_groups=mesh['yl'=2,'x'=4,'z'=8,'yh'=4,'c'=2] {'z'}, dimensions={0} | all-to-all | bytes 458752 | tf_op jit(solution)/shard_map/all_to_all | solution.py:229
  60.8 0.0 copy-done
  60.8 2.1 %shard_map.121 = bf16[8,32,640]{2,1,0:T(8,128)(2,1)} custom-call(bf16[8,112,128]{2,1,0:T(8,128)(2,1)S(1)} %all_to_all.21.part_ref, bf16[384,5120]{1,0:T(8,128)(2,1)S(1)} %copy-done), custom_call_target="tpu_custom_call" | custom-call | flops 6291456 | bytes 6291456 | tf_op jit(solution)/shard_map/pallas_call | solution.py:36
  62.9 4.8 %all-to-all-start.3 = ((bf16[8,32,640]{2,1,0:T(8,128)(2,1)}), bf16[8,32,640]{2,1,0:T(8,128)(2,1)S(1)}, u32[]{:S(2)}, u32[]{:S(2)}) async-start(bf16[8,32,640]{2,1,0:T(8,128)(2,1)} %shard_map.121), calls=%async_computation.3 | async-start | bytes 655360 | tf_op jit(solution)/shard_map/all_to_all | solution.py:237
  68.4 5.5 %all-to-all-done.3.part_ref = bf16[8,32,640]{2,1,0:T(8,128)(2,1)S(1)} async-done(((bf16[8,32,640]{2,1,0:T(8,128)(2,1)}), bf16[8,32,640]{2,1,0:T(8,128)(2,1)S(1)}, u32[]{:S(2)}, u32[]{:S(2)}) %all-to-all-start.3) | async-done | bytes 327712 | tf_op jit(solution)/shard_map/all_to_all | solution.py:237
  73.9 0.0 copy-done.1
  73.9 0.0 copy-done.2
  73.9 0.7 shard_map.122
Async XLA Ops:
  2.2 28.9 %all-to-all-start = ((bf16[8,32,384]{2,1,0:T(8,128)(2,1)}), bf16[8,32,384]{2,1,0:T(8,128)(2,1)S(1)}, u32[]{:S(2)}, u32[]{:S(2)}) async-start(bf16[8,32,384]{2,1,0:T(8,128)(2,1)} %get-tuple-element.7), calls=%async_computation | async-start | bytes 393216 | tf_op jit(solution)/shard_map/all_to_all | solution.py:214
  31.2 29.6 %copy-start = (bf16[384,5120]{1,0:T(8,128)(2,1)S(1)}, bf16[384,5120]{1,0:T(8,128)(2,1)}, u32[]{:S(2)}) copy-start(bf16[384,5120]{1,0:T(8,128)(2,1)} %weight_ref.3) | copy-start | bytes 11796484
  43.3 30.6 %copy-start.1 = (f32[50,640]{1,0:T(8,128)S(1)}, f32[50,640]{1,0:T(8,128)}, u32[]{:S(2)}) copy-start(f32[50,640]{1,0:T(8,128)} %gate_ref.1) | copy-start | bytes 384004
  43.3 30.6 %copy-start.2 = (bf16[32,640]{1,0:T(8,128)(2,1)S(1)}, bf16[32,640]{1,0:T(8,128)(2,1)}, u32[]{:S(2)}) copy-start(bf16[32,640]{1,0:T(8,128)(2,1)} %hidden_ref.1) | copy-start | bytes 122884
  62.9 11.0 %all-to-all-start.3 = ((bf16[8,32,640]{2,1,0:T(8,128)(2,1)}), bf16[8,32,640]{2,1,0:T(8,128)(2,1)S(1)}, u32[]{:S(2)}, u32[]{:S(2)}) async-start(bf16[8,32,640]{2,1,0:T(8,128)(2,1)} %shard_map.121), calls=%async_computation.3 | async-start | bytes 655360 | tf_op jit(solution)/shard_map/all_to_all | solution.py:237

commit v6 on v5

--- a/solution.py
+++ b/solution.py
@@ -45,13 +45,35 @@
 
 
 def pack_kernel(
-    count_ref, gq_ref, gk_ref, q_ref, k_ref, v_ref, rk_ref, rv_ref, qb_ref, kv_ref
+    count_ref,
+    frame_ref,
+    gq_hbm,
+    gk_hbm,
+    q_hbm,
+    k_hbm,
+    v_hbm,
+    rk_hbm,
+    rv_hbm,
+    qb_ref,
+    kv_ref,
+    step_ref,
+    gq_ref,
+    gk_ref,
+    q_ref,
+    sems,
 ):
+    pairs = [(q_hbm, q_ref), (gq_hbm, gq_ref), (gk_hbm, gk_ref)]
+    for t, ref in enumerate((k_hbm, v_hbm, rk_hbm, rv_hbm)):
+        pairs.append((ref, kv_ref.at[:, t * FEAT : (t + 1) * FEAT]))
+    copies = [pltpu.make_async_copy(a, b, sems.at[n]) for n, (a, b) in enumerate(pairs)]
+    for copy in copies:
+        copy.start()
+    step_ref[...] = jnp.full((8, 128), frame_ref[0].astype(F32), F32)
+    for copy in copies[:3]:
+        copy.wait()
     query = q_ref[...]
     for peer in range(QB):
         qb_ref[peer] = query
-    for t, ref in enumerate((k_ref, v_ref, rk_ref, rv_ref)):
-        kv_ref[:, t * FEAT : (t + 1) * FEAT] = ref[...]
     count = count_ref[0].astype(F32)
     parts = []
     for ref in (gq_ref, gk_ref):
@@ -62,6 +84,8 @@
             rest = rest - part
     lines = [jnp.full((1, 128), count, F32)] + parts + [jnp.zeros((ROWS - 19, 128), F32)]
     kv_ref[:, 4 * FEAT :] = jnp.concatenate(lines, axis=0).astype(BF)
+    for copy in copies[3:]:
+        copy.wait()
 
 
 def token_power(rows):
@@ -77,7 +101,7 @@
         lines.append(token_power(q_ref[g * 4 : g * 4 + 4].reshape(128, FEAT)))
     for g in range(2):
         lines.append(token_power(kv_ref[g * 4 : g * 4 + 4, :, :FEAT].reshape(128, FEAT)))
-    block = jnp.concatenate(lines + [jnp.zeros((4, 128), F32)], axis=0)
+    block = jnp.concatenate(lines, axis=0)
     for peer in range(HB):
         out_ref[peer] = block
 
@@ -174,7 +198,9 @@
     projected = part_ref[0].astype(F32)
     for h in range(1, HB):
         projected = projected + part_ref[h].astype(F32)
-    gate = gate_ref[pl.ds(step_ref[0], 1), :]
+    table = gate_ref[...]
+    row = lax.broadcasted_iota(jnp.int32, table.shape, 0).astype(F32)
+    gate = jnp.sum(jnp.where(row == step_ref[0:1, 0:1], table, 0.0), axis=0, keepdims=True)
     out_ref[...] = (hidden_ref[...].astype(F32) + gate * projected).astype(BF)
 
 
@@ -193,27 +219,40 @@
     frame_step,
 ):
     vmem = pl.BlockSpec(memory_space=pltpu.VMEM)
-    queries, block = call(
+    hbm = pl.BlockSpec(memory_space=pltpu.HBM)
+    smem = pl.BlockSpec(memory_space=pltpu.SMEM)
+
+    def pin(array):
+        return pltpu.with_memory_space_constraint(array, pltpu.HBM)
+
+    queries, block, step = call(
         pack_kernel,
         (
             jax.ShapeDtypeStruct((QB, ROWS, FEAT), BF),
             jax.ShapeDtypeStruct((ROWS, 4 * FEAT + 128), BF),
+            jax.ShapeDtypeStruct((8, 128), F32),
         ),
         ref_count,
-        query_gain,
-        key_gain,
-        query,
-        key,
-        value,
-        ref_key,
-        ref_value,
-        in_specs=[pl.BlockSpec(memory_space=pltpu.SMEM)] + [vmem] * 7,
-        n_out=2,
-        mib=60,
+        frame_step,
+        pin(query_gain),
+        pin(key_gain),
+        pin(query),
+        pin(key),
+        pin(value),
+        pin(ref_key),
+        pin(ref_value),
+        in_specs=[smem] * 2 + [hbm] * 7,
+        n_out=3,
+        scratch=[
+            pltpu.VMEM((FEAT,), F32),
+            pltpu.VMEM((FEAT,), F32),
+            pltpu.VMEM((ROWS, FEAT), BF),
+            pltpu.SemaphoreType.DMA((7,)),
+        ],
     )
     queries = lax.all_to_all(queries, QUERY_AXES, 0, 0, tiled=True)
     kv = lax.all_gather(block, KEY_AXES, axis=0)
-    powers = call(power_kernel, jax.ShapeDtypeStruct((HB, 8, 128), F32), queries, kv)
+    powers = call(power_kernel, jax.ShapeDtypeStruct((HB, 4, 128), F32), queries, kv)
     powers = lax.all_to_all(powers, HEAD_AXES, 0, 0, tiled=True)
     parts = call(
         attend_kernel,
@@ -238,11 +277,10 @@
     return call(
         finish_kernel,
         jax.ShapeDtypeStruct((ROWS, WIDTH), BF),
-        frame_step,
+        step,
         projected,
         hidden,
         gate_table,
-        in_specs=[pl.BlockSpec(memory_space=pltpu.SMEM), vmem, vmem, vmem],
     )
 
 

time: 75 us -> 73.9 us (0.985)
  blocking collectives: 46.8 us -> 56.7 us
  waiting for transfers between devices: 5.55 us -> 0.01 us
  starting transfers between devices: 15.1 us -> 10.3 us
    all_to_all x0 -> x1, blocking collectives: none -> 10.3 us  [shards(): projected = lax.all_to_all(projected, HEAD_AXES, 0, 0, tiled=True)]
    all_to_all x1 -> x0, waiting for transfers between devices: 5.54 us -> none  [shards(): projected = lax.all_to_all(projected, HEAD_AXES, 0, 0, tiled=True)]
    all_to_all x1 -> x0, starting transfers between devices: 4.81 us -> none  [shards(): projected = lax.all_to_all(projected, HEAD_AXES, 0, 0, tiled=True)]
  transfers between devices with their start and end apart: 2 -> 1, of which waited for: 1 -> 0; matrix products, arithmetic and copies ran while one was open for 0% -> 0% of each run, Pallas kernels for 0% -> 0%
where the time goes in v6:
time: 73.9 us; the launch traced here: 73.4 us
  blocking collectives  56.7 us (77%)
  starting transfers between devices  10.3 us (14%)
  Pallas kernels  5.05 us (7%)
  between operations  1.34 us (2%)
    all_gather x1, blocking collectives, shards(): kv = lax.all_gather(block, KEY_AXES, axis=0)  18.4 us
    all_to_all x1, blocking collectives, shards(): parts = lax.all_to_all(parts, QUERY_AXES, 0, 0, tiled=True)  17.4 us
    all_to_all x1, blocking collectives, shards(): powers = lax.all_to_all(powers, HEAD_AXES, 0, 0, tiled=True)  10.6 us
    all_to_all x1, starting transfers between devices, shards(): queries = lax.all_to_all(queries, QUERY_AXES, 0, 0, tiled=True)  10.3 us
    all_to_all x1, blocking collectives, shards(): projected = lax.all_to_all(projected, HEAD_AXES, 0, 0, tiled=True)  10.3 us
    pallas_call x5, Pallas kernels, call(): pl.pallas_call(kernel, out_shape=out_shape, in_specs=in_specs or [vmem] *...  5.05 us
  transfers between devices with their start and end apart: 1, of which 0 were waited for; matrix products, arithmetic and copies ran while one was open for 0% of the time, Pallas kernels for 0%

profile of v6, /device:TPU:8, one launch (start us, length us, event | category | flops | bytes accessed | tf_op | source)
XLA Modules:
  0.0 73.4 jit_solution(6393811699730359049)
XLA Ops:
  1.3 1.6 %shard_map.118 = (bf16[8,32,384]{2,1,0:T(8,128)(2,1)}, bf16[32,1664]{1,0:T(8,128)(2,1)S(1)}, f32[8,128]{1,0:T(8,128)S(1)}) custom-call(s32[1]{0:T(128)S(6)} %copy.13.count_ref, s32[1]{0:T(128)S(6)} %copy.14.frame_ref, f32[384]{0:T(512)} %gq_hbm.1, f32[384]{0:T(512)} %gk_hbm.1, bf16[32,384]{1,0:T(8,128)(2,1)} %q_hbm.1, bf16[32,384]{1,0:T(8,128)(2,1)} %k_hbm.1, ...), custom_call_target="tpu_custom_call" | custom-call | flops 1 | bytes 1 | tf_op jit(solution)/shard_map/pallas_call | solution.py:36
  2.9 10.3 %all-to-all-start = ((bf16[8,32,384]{2,1,0:T(8,128)(2,1)}), bf16[8,32,384]{2,1,0:T(8,128)(2,1)S(1)}, u32[]{:S(2)}, u32[]{:S(2)}) async-start(bf16[8,32,384]{2,1,0:T(8,128)(2,1)} %get-tuple-element.9), calls=%async_computation | async-start | bytes 393216 | tf_op jit(solution)/shard_map/all_to_all | solution.py:253
  13.2 18.4 %all-gather = bf16[256,1664]{1,0:T(8,128)(2,1)S(1)} all-gather(bf16[32,1664]{1,0:T(8,128)(2,1)S(1)} %get-tuple-element.10), channel_id=2, replica_groups=mesh['yl'=2,'x'=4,'z'=8,'yh'=4,'c'=2] {'yh','c'}, dimensions={0}, use_global_device_ids=true | all-gather | bytes 958464 | tf_op jit(solution)/shard_map/all_gather | solution.py:254
  31.6 0.0 all-to-all-done.q_ref
  31.6 0.0 copy-start
  31.6 0.1 shard_map.119
  31.8 10.6 %all_to_all.20.pw_ref = f32[8,4,128]{2,1,0:T(4,128)S(1)} all-to-all(f32[8,4,128]{2,1,0:T(4,128)S(1)} %shard_map.119), channel_id=1, replica_groups=mesh['yl'=2,'x'=4,'z'=8,'yh'=4,'c'=2] {'yl','x'}, dimensions={0} | all-to-all | bytes 32768 | tf_op jit(solution)/shard_map/all_to_all | solution.py:256
  42.4 1.3 %shard_map.120 = bf16[8,112,128]{2,1,0:T(8,128)(2,1)S(1)} custom-call(bf16[8,32,384]{2,1,0:T(8,128)(2,1)S(1)} %all-to-all-done.q_ref, bf16[8,32,1664]{2,1,0:T(8,128)(2,1)S(1)} %bitcast.2, f32[8,4,128]{2,1,0:T(4,128)S(1)} %all_to_all.20.pw_ref, bf16[384,5120]{1,0:T(8,128)(2,1)} %weight_ref.3), custom_call_target="tpu_custom_call" | custom-call | flops 4194304 | bytes 4194304 | tf_op jit(solution)/shard_map/pallas_call | solution.py:36
  43.7 0.0 copy-start.1
  43.7 0.0 copy-start.2
  43.7 17.4 %all_to_all.21.part_ref = bf16[8,112,128]{2,1,0:T(8,128)(2,1)S(1)} all-to-all(bf16[8,112,128]{2,1,0:T(8,128)(2,1)S(1)} %shard_map.120), channel_id=1, replica_groups=mesh['yl'=2,'x'=4,'z'=8,'yh'=4,'c'=2] {'z'}, dimensions={0} | all-to-all | bytes 458752 | tf_op jit(solution)/shard_map/all_to_all | solution.py:268
  61.1 0.0 copy-done
  61.1 1.3 %shard_map.121 = bf16[8,32,640]{2,1,0:T(8,128)(2,1)S(1)} custom-call(bf16[8,112,128]{2,1,0:T(8,128)(2,1)S(1)} %all_to_all.21.part_ref, bf16[384,5120]{1,0:T(8,128)(2,1)S(1)} %copy-done), custom_call_target="tpu_custom_call" | custom-call | flops 6291456 | bytes 6291456 | tf_op jit(solution)/shard_map/pallas_call | solution.py:36
  62.5 10.3 %all_to_all.22.part_ref = bf16[8,32,640]{2,1,0:T(8,128)(2,1)S(1)} all-to-all(bf16[8,32,640]{2,1,0:T(8,128)(2,1)S(1)} %shard_map.121), channel_id=1, replica_groups=mesh['yl'=2,'x'=4,'z'=8,'yh'=4,'c'=2] {'yl','x'}, dimensions={0} | all-to-all | bytes 655360 | tf_op jit(solution)/shard_map/all_to_all | solution.py:276
  72.7 0.0 copy-done.1
  72.7 0.0 copy-done.2
  72.7 0.7 shard_map.122
Async XLA Ops:
  2.9 28.7 %all-to-all-start = ((bf16[8,32,384]{2,1,0:T(8,128)(2,1)}), bf16[8,32,384]{2,1,0:T(8,128)(2,1)S(1)}, u32[]{:S(2)}, u32[]{:S(2)}) async-start(bf16[8,32,384]{2,1,0:T(8,128)(2,1)} %get-tuple-element.9), calls=%async_computation | async-start | bytes 393216 | tf_op jit(solution)/shard_map/all_to_all | solution.py:253
  31.6 29.5 %copy-start = (bf16[384,5120]{1,0:T(8,128)(2,1)S(1)}, bf16[384,5120]{1,0:T(8,128)(2,1)}, u32[]{:S(2)}) copy-start(bf16[384,5120]{1,0:T(8,128)(2,1)} %weight_ref.3) | copy-start | bytes 11796484
  43.7 29.1 %copy-start.1 = (f32[50,640]{1,0:T(8,128)S(1)}, f32[50,640]{1,0:T(8,128)}, u32[]{:S(2)}) copy-start(f32[50,640]{1,0:T(8,128)} %gate_ref.1) | copy-start | bytes 384004
  43.7 29.0 %copy-start.2 = (bf16[32,640]{1,0:T(8,128)(2,1)S(1)}, bf16[32,640]{1,0:T(8,128)(2,1)}, u32[]{:S(2)}) copy-start(bf16[32,640]{1,0:T(8,128)(2,1)} %hidden_ref.1) | copy-start | bytes 122884

commit v7 on v6

--- a/solution.py
+++ b/solution.py
@@ -46,7 +46,6 @@
 
 def pack_kernel(
     count_ref,
-    frame_ref,
     gq_hbm,
     gk_hbm,
     q_hbm,
@@ -56,7 +55,6 @@
     rv_hbm,
     qb_ref,
     kv_ref,
-    step_ref,
     gq_ref,
     gk_ref,
     q_ref,
@@ -68,7 +66,6 @@
     copies = [pltpu.make_async_copy(a, b, sems.at[n]) for n, (a, b) in enumerate(pairs)]
     for copy in copies:
         copy.start()
-    step_ref[...] = jnp.full((8, 128), frame_ref[0].astype(F32), F32)
     for copy in copies[:3]:
         copy.wait()
     query = q_ref[...]
@@ -106,7 +103,8 @@
         out_ref[peer] = block
 
 
-def attend_kernel(q_ref, kv_ref, pw_ref, weight_ref, out_ref):
+def attend_kernel(frame_ref, q_ref, kv_ref, pw_ref, weight_ref, out_ref, step_ref):
+    step_ref[...] = jnp.full((8, 128), frame_ref[0].astype(F32), F32)
     power = jnp.sum(pw_ref[...], axis=0) / ALL_FEATURES
     inverse = lax.rsqrt(power + EPSILON)
 
@@ -204,6 +202,11 @@
     out_ref[...] = (hidden_ref[...].astype(F32) + gate * projected).astype(BF)
 
 
+def over_z(pieces):
+    order = [list(range(QB))[::-1]]
+    return lax.all_to_all(pieces, QUERY_AXES, 0, 0, tiled=True, axis_index_groups=order)
+
+
 def shards(
     hidden,
     query,
@@ -225,15 +228,13 @@
     def pin(array):
         return pltpu.with_memory_space_constraint(array, pltpu.HBM)
 
-    queries, block, step = call(
+    queries, block = call(
         pack_kernel,
         (
             jax.ShapeDtypeStruct((QB, ROWS, FEAT), BF),
             jax.ShapeDtypeStruct((ROWS, 4 * FEAT + 128), BF),
-            jax.ShapeDtypeStruct((8, 128), F32),
         ),
         ref_count,
-        frame_step,
         pin(query_gain),
         pin(key_gain),
         pin(query),
@@ -241,8 +242,8 @@
         pin(value),
         pin(ref_key),
         pin(ref_value),
-        in_specs=[smem] * 2 + [hbm] * 7,
-        n_out=3,
+        in_specs=[smem] + [hbm] * 7,
+        n_out=2,
         scratch=[
             pltpu.VMEM((FEAT,), F32),
             pltpu.VMEM((FEAT,), F32),
@@ -250,22 +251,27 @@
             pltpu.SemaphoreType.DMA((7,)),
         ],
     )
-    queries = lax.all_to_all(queries, QUERY_AXES, 0, 0, tiled=True)
+    queries = over_z(queries)
     kv = lax.all_gather(block, KEY_AXES, axis=0)
     powers = call(power_kernel, jax.ShapeDtypeStruct((HB, 4, 128), F32), queries, kv)
     powers = lax.all_to_all(powers, HEAD_AXES, 0, 0, tiled=True)
-    parts = call(
+    parts, step = call(
         attend_kernel,
-        jax.ShapeDtypeStruct((QB, PIECE, HEAD_DIM), BF),
+        (
+            jax.ShapeDtypeStruct((QB, PIECE, HEAD_DIM), BF),
+            jax.ShapeDtypeStruct((8, 128), F32),
+        ),
+        frame_step,
         queries,
         kv,
         powers,
         out_weight,
-        in_specs=[vmem] * 3 + [pl.BlockSpec(memory_space=pl.ANY)],
+        in_specs=[smem] + [vmem] * 3 + [pl.BlockSpec(memory_space=pl.ANY)],
+        n_out=2,
         mib=50,
         cost=4 * 1024 * 1024,
     )
-    parts = lax.all_to_all(parts, QUERY_AXES, 0, 0, tiled=True)
+    parts = over_z(parts)
     projected = call(
         project_kernel,
         jax.ShapeDtypeStruct((HB, ROWS, WIDTH), BF),

time: 73.9 us -> 72.9 us (0.986)
  blocking collectives: 56.7 us -> 43.2 us
  starting transfers between devices: 10.3 us -> 18.1 us
  waiting for transfers between devices: 0.01 us -> 4.13 us
    all_to_all x2 -> x1, blocking collectives: 28 us -> 14.7 us  [over_z(): lax.all_to_all(pieces, QUERY_AXES, 0, 0, tiled=True, axis_index_groups=or...]
    all_to_all x1 -> x2, starting transfers between devices: 10.3 us -> 18.1 us  [the longest x1 12.4 us: over_z(): lax.all_to_all(pieces, QUERY_AXES, 0, 0, tiled=True, axis_index_groups=or...]
    all_to_all x1 -> x2, waiting for transfers between devices: 0.01 us -> 4.13 us  [the longest x1 4.13 us: shards(): powers = lax.all_to_all(powers, HEAD_AXES, 0, 0, tiled=True)]
  transfers between devices with their start and end apart: 1 -> 2, of which waited for: 0 -> 1; matrix products, arithmetic and copies ran while one was open for 0% -> 0% of each run, Pallas kernels for 0% -> 0%
where the time goes in v7:
time: 72.9 us; the launch traced here: 72.5 us
  blocking collectives  43.2 us (59%)
  starting transfers between devices  18.1 us (25%)
  Pallas kernels  5.65 us (8%)
  waiting for transfers between devices  4.13 us (6%)
  between operations  1.34 us (2%)
    all_gather x1, blocking collectives, shards(): kv = lax.all_gather(block, KEY_AXES, axis=0)  18.2 us
    all_to_all x1, blocking collectives, over_z(): lax.all_to_all(pieces, QUERY_AXES, 0, 0, tiled=True, axis_index_groups=or...  14.7 us
    all_to_all x1, starting transfers between devices, over_z(): lax.all_to_all(pieces, QUERY_AXES, 0, 0, tiled=True, axis_index_groups=or...  12.4 us
    all_to_all x1, blocking collectives, shards(): projected = lax.all_to_all(projected, HEAD_AXES, 0, 0, tiled=True)  10.2 us
    all_to_all x1, starting transfers between devices, shards(): powers = lax.all_to_all(powers, HEAD_AXES, 0, 0, tiled=True)  5.76 us
    pallas_call x5, Pallas kernels, call(): pl.pallas_call(kernel, out_shape=out_shape, in_specs=in_specs or [vmem] *...  5.65 us
    all_to_all x1, waiting for transfers between devices, shards(): powers = lax.all_to_all(powers, HEAD_AXES, 0, 0, tiled=True)  4.13 us
  transfers between devices with their start and end apart: 2, of which 1 were waited for; matrix products, arithmetic and copies ran while one was open for 0% of the time, Pallas kernels for 0%

profile of v7, /device:TPU:8, one launch (start us, length us, event | category | flops | bytes accessed | tf_op | source)
XLA Modules:
  0.0 72.5 jit_solution(18206371080330106414)
XLA Ops:
  0.7 1.6 %shard_map.118 = (bf16[8,32,384]{2,1,0:T(8,128)(2,1)}, bf16[32,1664]{1,0:T(8,128)(2,1)S(1)}) custom-call(s32[1]{0:T(128)S(6)} %copy.13.count_ref, f32[384]{0:T(512)} %gq_hbm.1, f32[384]{0:T(512)} %gk_hbm.1, bf16[32,384]{1,0:T(8,128)(2,1)} %q_hbm.1, bf16[32,384]{1,0:T(8,128)(2,1)} %k_hbm.1, bf16[32,384]{1,0:T(8,128)(2,1)} %v_hbm.1, bf16[32,384]{1,0:T(8,128)(2,1)} %rk_hbm.1, ...), custom_call_target="tpu_custom_call" | custom-call | flops 1 | bytes 1 | tf_op jit(solution)/shard_map/pallas_call | solution.py:36
  2.2 12.4 %all-to-all-start = ((bf16[8,32,384]{2,1,0:T(8,128)(2,1)}), bf16[8,32,384]{2,1,0:T(8,128)(2,1)S(1)}, u32[]{:S(2)}, u32[]{:S(2)}) async-start(bf16[8,32,384]{2,1,0:T(8,128)(2,1)} %get-tuple-element.9), calls=%async_computation | async-start | bytes 393216 | tf_op jit(solution)/shard_map/all_to_all | solution.py:207
  14.6 18.2 %all-gather = bf16[256,1664]{1,0:T(8,128)(2,1)S(1)} all-gather(bf16[32,1664]{1,0:T(8,128)(2,1)S(1)} %get-tuple-element.10), channel_id=2, replica_groups=mesh['yl'=2,'x'=4,'z'=8,'yh'=4,'c'=2] {'yh','c'}, dimensions={0}, use_global_device_ids=true | all-gather | bytes 958464 | tf_op jit(solution)/shard_map/all_gather | solution.py:255
  32.8 0.0 all-to-all-done.q_ref
  32.9 0.8 %shard_map.119 = f32[8,4,128]{2,1,0:T(4,128)} custom-call(bf16[8,32,384]{2,1,0:T(8,128)(2,1)S(1)} %all-to-all-done.q_ref, bf16[8,32,1664]{2,1,0:T(8,128)(2,1)S(1)} %bitcast.1), custom_call_target="tpu_custom_call" | custom-call | flops 1 | bytes 1 | tf_op jit(solution)/shard_map/pallas_call | solution.py:36
  33.6 5.8 %all-to-all-start.1 = ((f32[8,4,128]{2,1,0:T(4,128)}), f32[8,4,128]{2,1,0:T(4,128)S(1)}, u32[]{:S(2)}, u32[]{:S(2)}) async-start(f32[8,4,128]{2,1,0:T(4,128)} %shard_map.119), calls=%async_computation.1 | async-start | bytes 32768 | tf_op jit(solution)/shard_map/all_to_all | solution.py:257
  40.0 4.1 %all-to-all-done.1.pw_ref = f32[8,4,128]{2,1,0:T(4,128)S(1)} async-done(((f32[8,4,128]{2,1,0:T(4,128)}), f32[8,4,128]{2,1,0:T(4,128)S(1)}, u32[]{:S(2)}, u32[]{:S(2)}) %all-to-all-start.1) | async-done | bytes 16416 | tf_op jit(solution)/shard_map/all_to_all | solution.py:257
  44.1 0.0 copy-start
  44.1 1.3 %shard_map.120 = (bf16[8,112,128]{2,1,0:T(8,128)(2,1)S(1)}, f32[8,128]{1,0:T(8,128)S(1)}) custom-call(s32[1]{0:T(128)S(6)} %copy.14.frame_ref, bf16[8,32,384]{2,1,0:T(8,128)(2,1)S(1)} %all-to-all-done.q_ref, bf16[8,32,1664]{2,1,0:T(8,128)(2,1)S(1)} %bitcast.2, f32[8,4,128]{2,1,0:T(4,128)S(1)} %all-to-all-done.1.pw_ref, bf16[384,5120]{1,0:T(8,128)(2,1)} %weight_ref.3), custom_call_target="tpu_custom_call" | custom-call | flops 4194304 | bytes 4194304 | tf_op jit(solution)/shard_map/pallas_call | solution.py:36
  45.4 0.0 copy-start.1
  45.5 0.0 copy-start.2
  45.5 14.7 %all_to_all.20.part_ref = bf16[8,112,128]{2,1,0:T(8,128)(2,1)S(1)} all-to-all(bf16[8,112,128]{2,1,0:T(8,128)(2,1)S(1)} %get-tuple-element.12), channel_id=1, replica_groups={{56,48,40,32,24,16,8,0},{57,49,41,33,25,17,9,1},{58,50,42,34,26,18,10,2..., dimensions={0} | all-to-all | bytes 458752 | tf_op jit(solution)/shard_map/all_to_all | solution.py:207
  60.2 0.0 copy-done
  60.2 1.3 %shard_map.121 = bf16[8,32,640]{2,1,0:T(8,128)(2,1)S(1)} custom-call(bf16[8,112,128]{2,1,0:T(8,128)(2,1)S(1)} %all_to_all.20.part_ref, bf16[384,5120]{1,0:T(8,128)(2,1)S(1)} %copy-done), custom_call_target="tpu_custom_call" | custom-call | flops 6291456 | bytes 6291456 | tf_op jit(solution)/shard_map/pallas_call | solution.py:36
  61.6 10.2 %all_to_all.21.part_ref = bf16[8,32,640]{2,1,0:T(8,128)(2,1)S(1)} all-to-all(bf16[8,32,640]{2,1,0:T(8,128)(2,1)S(1)} %shard_map.121), channel_id=1, replica_groups=mesh['yl'=2,'x'=4,'z'=8,'yh'=4,'c'=2] {'yl','x'}, dimensions={0} | all-to-all | bytes 655360 | tf_op jit(solution)/shard_map/all_to_all | solution.py:282
  71.8 0.0 copy-done.1
  71.8 0.0 copy-done.2
  71.8 0.7 shard_map.122
Async XLA Ops:
  2.2 30.6 %all-to-all-start = ((bf16[8,32,384]{2,1,0:T(8,128)(2,1)}), bf16[8,32,384]{2,1,0:T(8,128)(2,1)S(1)}, u32[]{:S(2)}, u32[]{:S(2)}) async-start(bf16[8,32,384]{2,1,0:T(8,128)(2,1)} %get-tuple-element.9), calls=%async_computation | async-start | bytes 393216 | tf_op jit(solution)/shard_map/all_to_all | solution.py:207
  33.6 10.5 %all-to-all-start.1 = ((f32[8,4,128]{2,1,0:T(4,128)}), f32[8,4,128]{2,1,0:T(4,128)S(1)}, u32[]{:S(2)}, u32[]{:S(2)}) async-start(f32[8,4,128]{2,1,0:T(4,128)} %shard_map.119), calls=%async_computation.1 | async-start | bytes 32768 | tf_op jit(solution)/shard_map/all_to_all | solution.py:257
  44.1 16.1 %copy-start = (bf16[384,5120]{1,0:T(8,128)(2,1)S(1)}, bf16[384,5120]{1,0:T(8,128)(2,1)}, u32[]{:S(2)}) copy-start(bf16[384,5120]{1,0:T(8,128)(2,1)} %weight_ref.3) | copy-start | bytes 11796484
  45.4 26.3 %copy-start.1 = (f32[50,640]{1,0:T(8,128)S(1)}, f32[50,640]{1,0:T(8,128)}, u32[]{:S(2)}) copy-start(f32[50,640]{1,0:T(8,128)} %gate_ref.1) | copy-start | bytes 384004
  45.5 26.3 %copy-start.2 = (bf16[32,640]{1,0:T(8,128)(2,1)S(1)}, bf16[32,640]{1,0:T(8,128)(2,1)}, u32[]{:S(2)}) copy-start(bf16[32,640]{1,0:T(8,128)(2,1)} %hidden_ref.1) | copy-start | bytes 122884

commit v8 on v7

--- a/solution.py
+++ b/solution.py
@@ -26,6 +26,9 @@
 SEQ_AXES = ("z", "yh", "c")
 KEY_AXES = ("yh", "c")
 QUERY_AXES = "z"
+Z_ORDER = [0, 2, 4, 6, 1, 3, 5, 7]
+HEAD_ORDER = [0, 5, 2, 7, 4, 1, 6, 3]
+KEY_ORDER = [7, 6, 5, 4, 3, 2, 1, 0]
 QB = 8
 KB = 8
 HB = 8
@@ -186,8 +189,8 @@
         )
         pieces.append((mixed / total).astype(BF))
     attended = jnp.concatenate(pieces, axis=1)
-    for w in range(HB):
-        out_ref[w] = jnp.dot(
+    for p, w in enumerate(HEAD_ORDER):
+        out_ref[p] = jnp.dot(
             attended, weight_ref[:, w * WIDTH : (w + 1) * WIDTH], preferred_element_type=F32
         ).astype(BF)
 
@@ -202,9 +205,8 @@
     out_ref[...] = (hidden_ref[...].astype(F32) + gate * projected).astype(BF)
 
 
-def over_z(pieces):
-    order = [list(range(QB))[::-1]]
-    return lax.all_to_all(pieces, QUERY_AXES, 0, 0, tiled=True, axis_index_groups=order)
+def exchange(pieces, axes, order):
+    return lax.all_to_all(pieces, axes, 0, 0, tiled=True, axis_index_groups=[order])
 
 
 def shards(
@@ -251,10 +253,10 @@
             pltpu.SemaphoreType.DMA((7,)),
         ],
     )
-    queries = over_z(queries)
-    kv = lax.all_gather(block, KEY_AXES, axis=0)
+    queries = exchange(queries, QUERY_AXES, Z_ORDER)
+    kv = lax.all_gather(block, KEY_AXES, axis=0, axis_index_groups=[KEY_ORDER])
     powers = call(power_kernel, jax.ShapeDtypeStruct((HB, 4, 128), F32), queries, kv)
-    powers = lax.all_to_all(powers, HEAD_AXES, 0, 0, tiled=True)
+    powers = exchange(powers, HEAD_AXES, HEAD_ORDER)
     parts, step = call(
         attend_kernel,
         (
@@ -271,7 +273,7 @@
         mib=50,
         cost=4 * 1024 * 1024,
     )
-    parts = over_z(parts)
+    parts = exchange(parts, QUERY_AXES, Z_ORDER)
     projected = call(
         project_kernel,
         jax.ShapeDtypeStruct((HB, ROWS, WIDTH), BF),
@@ -279,7 +281,7 @@
         out_weight,
         cost=6 * 1024 * 1024,
     )
-    projected = lax.all_to_all(projected, HEAD_AXES, 0, 0, tiled=True)
+    projected = exchange(projected, HEAD_AXES, HEAD_ORDER)
     return call(
         finish_kernel,
         jax.ShapeDtypeStruct((ROWS, WIDTH), BF),

time: 72.9 us -> 72.8 us (level)
  the two profiles are of different devices: /device:TPU:8 before, /device:TPU:64 now
where the time goes in v8:
time: 72.8 us; the launch traced here: 72.4 us
  blocking collectives  45.3 us (62%)
  starting transfers between devices  14.5 us (20%)
  Pallas kernels  5.66 us (8%)
  waiting for transfers between devices  5.57 us (8%)
  between operations  1.34 us (2%)
    all_to_all x2, blocking collectives, exchange(): lax.all_to_all(pieces, axes, 0, 0, tiled=True, axis_index_groups=[order])  26.1 us
    all_gather x1, blocking collectives, shards(): kv = lax.all_gather(block, KEY_AXES, axis=0, axis_index_groups=[KEY_ORDER])  19.3 us
    all_to_all x2, starting transfers between devices, exchange(): lax.all_to_all(pieces, axes, 0, 0, tiled=True, axis_index_groups=[order])  14.5 us
    pallas_call x5, Pallas kernels, call(): pl.pallas_call(kernel, out_shape=out_shape, in_specs=in_specs or [vmem] *...  5.66 us
    all_to_all x2, waiting for transfers between devices, exchange(): lax.all_to_all(pieces, axes, 0, 0, tiled=True, axis_index_groups=[order])  5.57 us
  transfers between devices with their start and end apart: 2, of which 1 were waited for; matrix products, arithmetic and copies ran while one was open for 0% of the time, Pallas kernels for 0%

profile of v8, /device:TPU:64, one launch (start us, length us, event | category | flops | bytes accessed | tf_op | source)
XLA Modules:
  0.0 72.4 jit_solution(15890482317923678618)
XLA Ops:
  0.7 1.6 %shard_map.118 = (bf16[8,32,384]{2,1,0:T(8,128)(2,1)}, bf16[32,1664]{1,0:T(8,128)(2,1)S(1)}) custom-call(s32[1]{0:T(128)S(6)} %copy.13.count_ref, f32[384]{0:T(512)} %gq_hbm.1, f32[384]{0:T(512)} %gk_hbm.1, bf16[32,384]{1,0:T(8,128)(2,1)} %q_hbm.1, bf16[32,384]{1,0:T(8,128)(2,1)} %k_hbm.1, bf16[32,384]{1,0:T(8,128)(2,1)} %v_hbm.1, bf16[32,384]{1,0:T(8,128)(2,1)} %rk_hbm.1, ...), custom_call_target="tpu_custom_call" | custom-call | flops 1 | bytes 1 | tf_op jit(solution)/shard_map/pallas_call | solution.py:39
  2.2 10.0 %all-to-all-start = ((bf16[8,32,384]{2,1,0:T(8,128)(2,1)}), bf16[8,32,384]{2,1,0:T(8,128)(2,1)S(1)}, u32[]{:S(2)}, u32[]{:S(2)}) async-start(bf16[8,32,384]{2,1,0:T(8,128)(2,1)} %get-tuple-element.9), calls=%async_computation | async-start | bytes 393216 | tf_op jit(solution)/shard_map/all_to_all | solution.py:209
  12.2 19.3 %all-gather = bf16[256,1664]{1,0:T(8,128)(2,1)S(1)} all-gather(bf16[32,1664]{1,0:T(8,128)(2,1)S(1)} %get-tuple-element.10), channel_id=2, replica_groups={{7,6,5,4,3,2,1,0},{15,14,13,12,11,10,9,8},{23,22,21,20,19,18,17,16},{31..., dimensions={0}, use_global_device_ids=true | all-gather | bytes 958464 | tf_op jit(solution)/shard_map/all_gather | solution.py:257
  31.5 0.0 all-to-all-done.q_ref
  31.5 0.8 %shard_map.119 = f32[8,4,128]{2,1,0:T(4,128)} custom-call(bf16[8,32,384]{2,1,0:T(8,128)(2,1)S(1)} %all-to-all-done.q_ref, bf16[8,32,1664]{2,1,0:T(8,128)(2,1)S(1)} %bitcast.1), custom_call_target="tpu_custom_call" | custom-call | flops 1 | bytes 1 | tf_op jit(solution)/shard_map/pallas_call | solution.py:39
  32.2 4.5 %all-to-all-start.1 = ((f32[8,4,128]{2,1,0:T(4,128)}), f32[8,4,128]{2,1,0:T(4,128)S(1)}, u32[]{:S(2)}, u32[]{:S(2)}) async-start(f32[8,4,128]{2,1,0:T(4,128)} %shard_map.119), calls=%async_computation.1 | async-start | bytes 32768 | tf_op jit(solution)/shard_map/all_to_all | solution.py:209
  37.4 5.6 %all-to-all-done.1.pw_ref = f32[8,4,128]{2,1,0:T(4,128)S(1)} async-done(((f32[8,4,128]{2,1,0:T(4,128)}), f32[8,4,128]{2,1,0:T(4,128)S(1)}, u32[]{:S(2)}, u32[]{:S(2)}) %all-to-all-start.1) | async-done | bytes 16416 | tf_op jit(solution)/shard_map/all_to_all | solution.py:209
  42.9 0.0 copy-start
  43.0 1.3 %shard_map.120 = (bf16[8,112,128]{2,1,0:T(8,128)(2,1)S(1)}, f32[8,128]{1,0:T(8,128)S(1)}) custom-call(s32[1]{0:T(128)S(6)} %copy.14.frame_ref, bf16[8,32,384]{2,1,0:T(8,128)(2,1)S(1)} %all-to-all-done.q_ref, bf16[8,32,1664]{2,1,0:T(8,128)(2,1)S(1)} %bitcast.2, f32[8,4,128]{2,1,0:T(4,128)S(1)} %all-to-all-done.1.pw_ref, bf16[384,5120]{1,0:T(8,128)(2,1)} %weight_ref.3), custom_call_target="tpu_custom_call" | custom-call | flops 4194304 | bytes 4194304 | tf_op jit(solution)/shard_map/pallas_call | solution.py:39
  44.3 0.0 copy-start.1
  44.3 0.0 copy-start.2
  44.3 15.8 %all_to_all.20.part_ref = bf16[8,112,128]{2,1,0:T(8,128)(2,1)S(1)} all-to-all(bf16[8,112,128]{2,1,0:T(8,128)(2,1)S(1)} %get-tuple-element.12), channel_id=1, replica_groups={{0,16,32,48,8,24,40,56},{1,17,33,49,9,25,41,57},{2,18,34,50,10,26,42,58..., dimensions={0} | all-to-all | bytes 458752 | tf_op jit(solution)/shard_map/all_to_all | solution.py:209
  60.1 0.0 copy-done
  60.1 1.3 %shard_map.121 = bf16[8,32,640]{2,1,0:T(8,128)(2,1)S(1)} custom-call(bf16[8,112,128]{2,1,0:T(8,128)(2,1)S(1)} %all_to_all.20.part_ref, bf16[384,5120]{1,0:T(8,128)(2,1)S(1)} %copy-done), custom_call_target="tpu_custom_call" | custom-call | flops 6291456 | bytes 6291456 | tf_op jit(solution)/shard_map/pallas_call | solution.py:39
  61.5 10.3 %all_to_all.21.part_ref = bf16[8,32,640]{2,1,0:T(8,128)(2,1)S(1)} all-to-all(bf16[8,32,640]{2,1,0:T(8,128)(2,1)S(1)} %shard_map.121), channel_id=1, replica_groups={{0,320,128,448,256,64,384,192},{1,321,129,449,257,65,385,193},{2,322,13..., dimensions={0} | all-to-all | bytes 655360 | tf_op jit(solution)/shard_map/all_to_all | solution.py:209
  71.7 0.0 copy-done.1
  71.7 0.0 copy-done.2
  71.7 0.7 shard_map.122
Async XLA Ops:
  2.2 29.2 %all-to-all-start = ((bf16[8,32,384]{2,1,0:T(8,128)(2,1)}), bf16[8,32,384]{2,1,0:T(8,128)(2,1)S(1)}, u32[]{:S(2)}, u32[]{:S(2)}) async-start(bf16[8,32,384]{2,1,0:T(8,128)(2,1)} %get-tuple-element.9), calls=%async_computation | async-start | bytes 393216 | tf_op jit(solution)/shard_map/all_to_all | solution.py:209
  32.2 10.7 %all-to-all-start.1 = ((f32[8,4,128]{2,1,0:T(4,128)}), f32[8,4,128]{2,1,0:T(4,128)S(1)}, u32[]{:S(2)}, u32[]{:S(2)}) async-start(f32[8,4,128]{2,1,0:T(4,128)} %shard_map.119), calls=%async_computation.1 | async-start | bytes 32768 | tf_op jit(solution)/shard_map/all_to_all | solution.py:209
  42.9 17.2 %copy-start = (bf16[384,5120]{1,0:T(8,128)(2,1)S(1)}, bf16[384,5120]{1,0:T(8,128)(2,1)}, u32[]{:S(2)}) copy-start(bf16[384,5120]{1,0:T(8,128)(2,1)} %weight_ref.3) | copy-start | bytes 11796484
  44.3 27.5 %copy-start.1 = (f32[50,640]{1,0:T(8,128)S(1)}, f32[50,640]{1,0:T(8,128)}, u32[]{:S(2)}) copy-start(f32[50,640]{1,0:T(8,128)} %gate_ref.1) | copy-start | bytes 384004
  44.3 27.4 %copy-start.2 = (bf16[32,640]{1,0:T(8,128)(2,1)S(1)}, bf16[32,640]{1,0:T(8,128)(2,1)}, u32[]{:S(2)}) copy-start(bf16[32,640]{1,0:T(8,128)(2,1)} %hidden_ref.1) | copy-start | bytes 122884

commit v9 on v8

--- a/solution.py
+++ b/solution.py
@@ -26,9 +26,9 @@
 SEQ_AXES = ("z", "yh", "c")
 KEY_AXES = ("yh", "c")
 QUERY_AXES = "z"
-Z_ORDER = [0, 2, 4, 6, 1, 3, 5, 7]
+Z_ORDER = [7, 5, 3, 1, 0, 2, 4, 6]
 HEAD_ORDER = [0, 5, 2, 7, 4, 1, 6, 3]
-KEY_ORDER = [7, 6, 5, 4, 3, 2, 1, 0]
+KEY_ORDER = [0, 1, 2, 3, 4, 5, 6, 7]
 QB = 8
 KB = 8
 HB = 8

time: 72.8 us -> 72.3 us (level)
  the two profiles are of different devices: /device:TPU:64 before, /device:TPU:8 now
where the time goes in v9:
time: 72.3 us; the launch traced here: 71.9 us
  blocking collectives  42.6 us (59%)
  starting transfers between devices  18.1 us (25%)
  Pallas kernels  5.65 us (8%)
  waiting for transfers between devices  4.13 us (6%)
  between operations  1.34 us (2%)
    all_to_all x2, blocking collectives, exchange(): lax.all_to_all(pieces, axes, 0, 0, tiled=True, axis_index_groups=[order])  24.6 us
    all_to_all x2, starting transfers between devices, exchange(): lax.all_to_all(pieces, axes, 0, 0, tiled=True, axis_index_groups=[order])  18.1 us
    all_gather x1, blocking collectives, shards(): kv = lax.all_gather(block, KEY_AXES, axis=0, axis_index_groups=[KEY_ORDER])  18 us
    pallas_call x5, Pallas kernels, call(): pl.pallas_call(kernel, out_shape=out_shape, in_specs=in_specs or [vmem] *...  5.65 us
    all_to_all x2, waiting for transfers between devices, exchange(): lax.all_to_all(pieces, axes, 0, 0, tiled=True, axis_index_groups=[order])  4.13 us
  transfers between devices with their start and end apart: 2, of which 1 were waited for; matrix products, arithmetic and copies ran while one was open for 0% of the time, Pallas kernels for 0%

profile of v9, /device:TPU:8, one launch (start us, length us, event | category | flops | bytes accessed | tf_op | source)
XLA Modules:
  0.0 71.9 jit_solution(3610309853834865910)
XLA Ops:
  0.7 1.6 %shard_map.118 = (bf16[8,32,384]{2,1,0:T(8,128)(2,1)}, bf16[32,1664]{1,0:T(8,128)(2,1)S(1)}) custom-call(s32[1]{0:T(128)S(6)} %copy.13.count_ref, f32[384]{0:T(512)} %gq_hbm.1, f32[384]{0:T(512)} %gk_hbm.1, bf16[32,384]{1,0:T(8,128)(2,1)} %q_hbm.1, bf16[32,384]{1,0:T(8,128)(2,1)} %k_hbm.1, bf16[32,384]{1,0:T(8,128)(2,1)} %v_hbm.1, bf16[32,384]{1,0:T(8,128)(2,1)} %rk_hbm.1, ...), custom_call_target="tpu_custom_call" | custom-call | flops 1 | bytes 1 | tf_op jit(solution)/shard_map/pallas_call | solution.py:39
  2.2 12.4 %all-to-all-start = ((bf16[8,32,384]{2,1,0:T(8,128)(2,1)}), bf16[8,32,384]{2,1,0:T(8,128)(2,1)S(1)}, u32[]{:S(2)}, u32[]{:S(2)}) async-start(bf16[8,32,384]{2,1,0:T(8,128)(2,1)} %get-tuple-element.9), calls=%async_computation | async-start | bytes 393216 | tf_op jit(solution)/shard_map/all_to_all | solution.py:209
  14.6 18.0 %all-gather = bf16[256,1664]{1,0:T(8,128)(2,1)S(1)} all-gather(bf16[32,1664]{1,0:T(8,128)(2,1)S(1)} %get-tuple-element.10), channel_id=2, replica_groups={{0,1,2,3,4,5,6,7},{8,9,10,11,12,13,14,15},{16,17,18,19,20,21,22,23},{24..., dimensions={0}, use_global_device_ids=true | all-gather | bytes 958464 | tf_op jit(solution)/shard_map/all_gather | solution.py:257
  32.6 0.0 all-to-all-done.q_ref
  32.6 0.8 %shard_map.119 = f32[8,4,128]{2,1,0:T(4,128)} custom-call(bf16[8,32,384]{2,1,0:T(8,128)(2,1)S(1)} %all-to-all-done.q_ref, bf16[8,32,1664]{2,1,0:T(8,128)(2,1)S(1)} %bitcast.1), custom_call_target="tpu_custom_call" | custom-call | flops 1 | bytes 1 | tf_op jit(solution)/shard_map/pallas_call | solution.py:39
  33.3 5.8 %all-to-all-start.1 = ((f32[8,4,128]{2,1,0:T(4,128)}), f32[8,4,128]{2,1,0:T(4,128)S(1)}, u32[]{:S(2)}, u32[]{:S(2)}) async-start(f32[8,4,128]{2,1,0:T(4,128)} %shard_map.119), calls=%async_computation.1 | async-start | bytes 32768 | tf_op jit(solution)/shard_map/all_to_all | solution.py:209
  39.8 4.1 %all-to-all-done.1.pw_ref = f32[8,4,128]{2,1,0:T(4,128)S(1)} async-done(((f32[8,4,128]{2,1,0:T(4,128)}), f32[8,4,128]{2,1,0:T(4,128)S(1)}, u32[]{:S(2)}, u32[]{:S(2)}) %all-to-all-start.1) | async-done | bytes 16416 | tf_op jit(solution)/shard_map/all_to_all | solution.py:209
  43.9 0.0 copy-start
  43.9 1.3 %shard_map.120 = (bf16[8,112,128]{2,1,0:T(8,128)(2,1)S(1)}, f32[8,128]{1,0:T(8,128)S(1)}) custom-call(s32[1]{0:T(128)S(6)} %copy.14.frame_ref, bf16[8,32,384]{2,1,0:T(8,128)(2,1)S(1)} %all-to-all-done.q_ref, bf16[8,32,1664]{2,1,0:T(8,128)(2,1)S(1)} %bitcast.2, f32[8,4,128]{2,1,0:T(4,128)S(1)} %all-to-all-done.1.pw_ref, bf16[384,5120]{1,0:T(8,128)(2,1)} %weight_ref.3), custom_call_target="tpu_custom_call" | custom-call | flops 4194304 | bytes 4194304 | tf_op jit(solution)/shard_map/pallas_call | solution.py:39
  45.2 0.0 copy-start.1
  45.2 0.0 copy-start.2
  45.2 14.4 %all_to_all.20.part_ref = bf16[8,112,128]{2,1,0:T(8,128)(2,1)S(1)} all-to-all(bf16[8,112,128]{2,1,0:T(8,128)(2,1)S(1)} %get-tuple-element.12), channel_id=1, replica_groups={{56,40,24,8,0,16,32,48},{57,41,25,9,1,17,33,49},{58,42,26,10,2,18,34,50..., dimensions={0} | all-to-all | bytes 458752 | tf_op jit(solution)/shard_map/all_to_all | solution.py:209
  59.6 0.0 copy-done
  59.6 1.3 %shard_map.121 = bf16[8,32,640]{2,1,0:T(8,128)(2,1)S(1)} custom-call(bf16[8,112,128]{2,1,0:T(8,128)(2,1)S(1)} %all_to_all.20.part_ref, bf16[384,5120]{1,0:T(8,128)(2,1)S(1)} %copy-done), custom_call_target="tpu_custom_call" | custom-call | flops 6291456 | bytes 6291456 | tf_op jit(solution)/shard_map/pallas_call | solution.py:39
  60.9 10.2 %all_to_all.21.part_ref = bf16[8,32,640]{2,1,0:T(8,128)(2,1)S(1)} all-to-all(bf16[8,32,640]{2,1,0:T(8,128)(2,1)S(1)} %shard_map.121), channel_id=1, replica_groups={{0,320,128,448,256,64,384,192},{1,321,129,449,257,65,385,193},{2,322,13..., dimensions={0} | all-to-all | bytes 655360 | tf_op jit(solution)/shard_map/all_to_all | solution.py:209
  71.2 0.0 copy-done.1
  71.2 0.0 copy-done.2
  71.2 0.7 shard_map.122
Async XLA Ops:
  2.2 30.3 %all-to-all-start = ((bf16[8,32,384]{2,1,0:T(8,128)(2,1)}), bf16[8,32,384]{2,1,0:T(8,128)(2,1)S(1)}, u32[]{:S(2)}, u32[]{:S(2)}) async-start(bf16[8,32,384]{2,1,0:T(8,128)(2,1)} %get-tuple-element.9), calls=%async_computation | async-start | bytes 393216 | tf_op jit(solution)/shard_map/all_to_all | solution.py:209
  33.3 10.6 %all-to-all-start.1 = ((f32[8,4,128]{2,1,0:T(4,128)}), f32[8,4,128]{2,1,0:T(4,128)S(1)}, u32[]{:S(2)}, u32[]{:S(2)}) async-start(f32[8,4,128]{2,1,0:T(4,128)} %shard_map.119), calls=%async_computation.1 | async-start | bytes 32768 | tf_op jit(solution)/shard_map/all_to_all | solution.py:209
  43.9 15.7 %copy-start = (bf16[384,5120]{1,0:T(8,128)(2,1)S(1)}, bf16[384,5120]{1,0:T(8,128)(2,1)}, u32[]{:S(2)}) copy-start(bf16[384,5120]{1,0:T(8,128)(2,1)} %weight_ref.3) | copy-start | bytes 11796484
  45.2 26.0 %copy-start.1 = (f32[50,640]{1,0:T(8,128)S(1)}, f32[50,640]{1,0:T(8,128)}, u32[]{:S(2)}) copy-start(f32[50,640]{1,0:T(8,128)} %gate_ref.1) | copy-start | bytes 384004
  45.2 26.0 %copy-start.2 = (bf16[32,640]{1,0:T(8,128)(2,1)S(1)}, bf16[32,640]{1,0:T(8,128)(2,1)}, u32[]{:S(2)}) copy-start(bf16[32,640]{1,0:T(8,128)(2,1)} %hidden_ref.1) | copy-start | bytes 122884

commit v10 on v9

--- a/solution.py
+++ b/solution.py
@@ -26,7 +26,9 @@
 SEQ_AXES = ("z", "yh", "c")
 KEY_AXES = ("yh", "c")
 QUERY_AXES = "z"
-Z_ORDER = [7, 5, 3, 1, 0, 2, 4, 6]
+QUERY_ORDER = [0, 2, 4, 6, 1, 3, 5, 7]
+PART_ORDER = [7, 5, 3, 1, 0, 2, 4, 6]
+PLACE = [PART_ORDER.index(z) for z in QUERY_ORDER]
 HEAD_ORDER = [0, 5, 2, 7, 4, 1, 6, 3]
 KEY_ORDER = [0, 1, 2, 3, 4, 5, 6, 7]
 QB = 8
@@ -155,9 +157,9 @@
         mixed = jnp.dot(w1.astype(BF), part(1), preferred_element_type=F32) + jnp.dot(
             w2.astype(BF), part(3), preferred_element_type=F32
         )
-        out_ref[:, h * ROWS : (h + 1) * ROWS] = (
-            (mixed / total).astype(BF).reshape(QB, ROWS, HEAD_DIM)
-        )
+        mixed = (mixed / total).astype(BF)
+        for p in range(QB):
+            out_ref[PLACE[p], h * ROWS : (h + 1) * ROWS] = mixed[p * ROWS : (p + 1) * ROWS]
         high = total.astype(BF).astype(F32)
         stats = jnp.where(lane == h, peak, stats)
         stats = jnp.where(lane == HEADS + h, high, stats)
@@ -166,7 +168,7 @@
         lines = stats[half * 128 : (half + 1) * 128].T[:STATS]
         for j in range(4):
             turned = lines if j == 0 else pltpu.roll(lines, 128 - j * ROWS, 1)
-            out_ref[half * 4 + j, HEADS * ROWS :] = turned.astype(BF)
+            out_ref[PLACE[half * 4 + j], HEADS * ROWS :] = turned.astype(BF)
 
 
 def project_kernel(part_ref, weight_ref, out_ref):
@@ -253,7 +255,7 @@
             pltpu.SemaphoreType.DMA((7,)),
         ],
     )
-    queries = exchange(queries, QUERY_AXES, Z_ORDER)
+    queries = exchange(queries, QUERY_AXES, QUERY_ORDER)
     kv = lax.all_gather(block, KEY_AXES, axis=0, axis_index_groups=[KEY_ORDER])
     powers = call(power_kernel, jax.ShapeDtypeStruct((HB, 4, 128), F32), queries, kv)
     powers = exchange(powers, HEAD_AXES, HEAD_ORDER)
@@ -273,7 +275,7 @@
         mib=50,
         cost=4 * 1024 * 1024,
     )
-    parts = exchange(parts, QUERY_AXES, Z_ORDER)
+    parts = exchange(parts, QUERY_AXES, PART_ORDER)
     projected = call(
         project_kernel,
         jax.ShapeDtypeStruct((HB, ROWS, WIDTH), BF),

time: 72.3 us -> 70.9 us (0.981)
  starting transfers between devices: 18.1 us -> 16.1 us
    all_to_all x2, starting transfers between devices: 18.1 us -> 16.1 us  [exchange(): lax.all_to_all(pieces, axes, 0, 0, tiled=True, axis_index_groups=[order])]
where the time goes in v10:
time: 70.9 us; the launch traced here: 70.5 us
  blocking collectives  43.3 us (61%)
  starting transfers between devices  16.1 us (23%)
  Pallas kernels  5.65 us (8%)
  waiting for transfers between devices  4.13 us (6%)
  between operations  1.34 us (2%)
    all_to_all x2, blocking collectives, exchange(): lax.all_to_all(pieces, axes, 0, 0, tiled=True, axis_index_groups=[order])  24.8 us
    all_gather x1, blocking collectives, shards(): kv = lax.all_gather(block, KEY_AXES, axis=0, axis_index_groups=[KEY_ORDER])  18.5 us
    all_to_all x2, starting transfers between devices, exchange(): lax.all_to_all(pieces, axes, 0, 0, tiled=True, axis_index_groups=[order])  16.1 us
    pallas_call x5, Pallas kernels, call(): pl.pallas_call(kernel, out_shape=out_shape, in_specs=in_specs or [vmem] *...  5.65 us
    all_to_all x2, waiting for transfers between devices, exchange(): lax.all_to_all(pieces, axes, 0, 0, tiled=True, axis_index_groups=[order])  4.13 us
  transfers between devices with their start and end apart: 2, of which 1 were waited for; matrix products, arithmetic and copies ran while one was open for 0% of the time, Pallas kernels for 0%

profile of v10, /device:TPU:8, one launch (start us, length us, event | category | flops | bytes accessed | tf_op | source)
XLA Modules:
  0.0 70.5 jit_solution(5201375778773467156)
XLA Ops:
  0.7 1.6 %shard_map.118 = (bf16[8,32,384]{2,1,0:T(8,128)(2,1)}, bf16[32,1664]{1,0:T(8,128)(2,1)S(1)}) custom-call(s32[1]{0:T(128)S(6)} %copy.13.count_ref, f32[384]{0:T(512)} %gq_hbm.1, f32[384]{0:T(512)} %gk_hbm.1, bf16[32,384]{1,0:T(8,128)(2,1)} %q_hbm.1, bf16[32,384]{1,0:T(8,128)(2,1)} %k_hbm.1, bf16[32,384]{1,0:T(8,128)(2,1)} %v_hbm.1, bf16[32,384]{1,0:T(8,128)(2,1)} %rk_hbm.1, ...), custom_call_target="tpu_custom_call" | custom-call | flops 1 | bytes 1 | tf_op jit(solution)/shard_map/pallas_call | solution.py:41
  2.2 10.3 %all-to-all-start = ((bf16[8,32,384]{2,1,0:T(8,128)(2,1)}), bf16[8,32,384]{2,1,0:T(8,128)(2,1)S(1)}, u32[]{:S(2)}, u32[]{:S(2)}) async-start(bf16[8,32,384]{2,1,0:T(8,128)(2,1)} %get-tuple-element.9), calls=%async_computation | async-start | bytes 393216 | tf_op jit(solution)/shard_map/all_to_all | solution.py:211
  12.6 18.5 %all-gather = bf16[256,1664]{1,0:T(8,128)(2,1)S(1)} all-gather(bf16[32,1664]{1,0:T(8,128)(2,1)S(1)} %get-tuple-element.10), channel_id=2, replica_groups={{0,1,2,3,4,5,6,7},{8,9,10,11,12,13,14,15},{16,17,18,19,20,21,22,23},{24..., dimensions={0}, use_global_device_ids=true | all-gather | bytes 958464 | tf_op jit(solution)/shard_map/all_gather | solution.py:259
  31.0 0.0 all-to-all-done.q_ref
  31.0 0.8 %shard_map.119 = f32[8,4,128]{2,1,0:T(4,128)} custom-call(bf16[8,32,384]{2,1,0:T(8,128)(2,1)S(1)} %all-to-all-done.q_ref, bf16[8,32,1664]{2,1,0:T(8,128)(2,1)S(1)} %bitcast.1), custom_call_target="tpu_custom_call" | custom-call | flops 1 | bytes 1 | tf_op jit(solution)/shard_map/pallas_call | solution.py:41
  31.8 5.8 %all-to-all-start.1 = ((f32[8,4,128]{2,1,0:T(4,128)}), f32[8,4,128]{2,1,0:T(4,128)S(1)}, u32[]{:S(2)}, u32[]{:S(2)}) async-start(f32[8,4,128]{2,1,0:T(4,128)} %shard_map.119), calls=%async_computation.1 | async-start | bytes 32768 | tf_op jit(solution)/shard_map/all_to_all | solution.py:211
  38.2 4.1 %all-to-all-done.1.pw_ref = f32[8,4,128]{2,1,0:T(4,128)S(1)} async-done(((f32[8,4,128]{2,1,0:T(4,128)}), f32[8,4,128]{2,1,0:T(4,128)S(1)}, u32[]{:S(2)}, u32[]{:S(2)}) %all-to-all-start.1) | async-done | bytes 16416 | tf_op jit(solution)/shard_map/all_to_all | solution.py:211
  42.3 0.0 copy-start
  42.3 1.3 %shard_map.120 = (bf16[8,112,128]{2,1,0:T(8,128)(2,1)S(1)}, f32[8,128]{1,0:T(8,128)S(1)}) custom-call(s32[1]{0:T(128)S(6)} %copy.14.frame_ref, bf16[8,32,384]{2,1,0:T(8,128)(2,1)S(1)} %all-to-all-done.q_ref, bf16[8,32,1664]{2,1,0:T(8,128)(2,1)S(1)} %bitcast.2, f32[8,4,128]{2,1,0:T(4,128)S(1)} %all-to-all-done.1.pw_ref, bf16[384,5120]{1,0:T(8,128)(2,1)} %weight_ref.3), custom_call_target="tpu_custom_call" | custom-call | flops 4194304 | bytes 4194304 | tf_op jit(solution)/shard_map/pallas_call | solution.py:41
  43.6 0.0 copy-start.1
  43.6 0.0 copy-start.2
  43.6 14.6 %all_to_all.20.part_ref = bf16[8,112,128]{2,1,0:T(8,128)(2,1)S(1)} all-to-all(bf16[8,112,128]{2,1,0:T(8,128)(2,1)S(1)} %get-tuple-element.12), channel_id=1, replica_groups={{56,40,24,8,0,16,32,48},{57,41,25,9,1,17,33,49},{58,42,26,10,2,18,34,50..., dimensions={0} | all-to-all | bytes 458752 | tf_op jit(solution)/shard_map/all_to_all | solution.py:211
  58.2 0.0 copy-done
  58.2 1.3 %shard_map.121 = bf16[8,32,640]{2,1,0:T(8,128)(2,1)S(1)} custom-call(bf16[8,112,128]{2,1,0:T(8,128)(2,1)S(1)} %all_to_all.20.part_ref, bf16[384,5120]{1,0:T(8,128)(2,1)S(1)} %copy-done), custom_call_target="tpu_custom_call" | custom-call | flops 6291456 | bytes 6291456 | tf_op jit(solution)/shard_map/pallas_call | solution.py:41
  59.6 10.2 %all_to_all.21.part_ref = bf16[8,32,640]{2,1,0:T(8,128)(2,1)S(1)} all-to-all(bf16[8,32,640]{2,1,0:T(8,128)(2,1)S(1)} %shard_map.121), channel_id=1, replica_groups={{0,320,128,448,256,64,384,192},{1,321,129,449,257,65,385,193},{2,322,13..., dimensions={0} | all-to-all | bytes 655360 | tf_op jit(solution)/shard_map/all_to_all | solution.py:211
  69.8 0.0 copy-done.1
  69.8 0.0 copy-done.2
  69.8 0.7 shard_map.122
Async XLA Ops:
  2.2 28.8 %all-to-all-start = ((bf16[8,32,384]{2,1,0:T(8,128)(2,1)}), bf16[8,32,384]{2,1,0:T(8,128)(2,1)S(1)}, u32[]{:S(2)}, u32[]{:S(2)}) async-start(bf16[8,32,384]{2,1,0:T(8,128)(2,1)} %get-tuple-element.9), calls=%async_computation | async-start | bytes 393216 | tf_op jit(solution)/shard_map/all_to_all | solution.py:211
  31.8 10.5 %all-to-all-start.1 = ((f32[8,4,128]{2,1,0:T(4,128)}), f32[8,4,128]{2,1,0:T(4,128)S(1)}, u32[]{:S(2)}, u32[]{:S(2)}) async-start(f32[8,4,128]{2,1,0:T(4,128)} %shard_map.119), calls=%async_computation.1 | async-start | bytes 32768 | tf_op jit(solution)/shard_map/all_to_all | solution.py:211
  42.3 15.9 %copy-start = (bf16[384,5120]{1,0:T(8,128)(2,1)S(1)}, bf16[384,5120]{1,0:T(8,128)(2,1)}, u32[]{:S(2)}) copy-start(bf16[384,5120]{1,0:T(8,128)(2,1)} %weight_ref.3) | copy-start | bytes 11796484
  43.6 26.2 %copy-start.1 = (f32[50,640]{1,0:T(8,128)S(1)}, f32[50,640]{1,0:T(8,128)}, u32[]{:S(2)}) copy-start(f32[50,640]{1,0:T(8,128)} %gate_ref.1) | copy-start | bytes 384004
  43.6 26.2 %copy-start.2 = (bf16[32,640]{1,0:T(8,128)(2,1)S(1)}, bf16[32,640]{1,0:T(8,128)(2,1)}, u32[]{:S(2)}) copy-start(bf16[32,640]{1,0:T(8,128)(2,1)} %hidden_ref.1) | copy-start | bytes 122884

commit v11 on v10

--- a/solution.py
+++ b/solution.py
@@ -26,8 +26,8 @@
 SEQ_AXES = ("z", "yh", "c")
 KEY_AXES = ("yh", "c")
 QUERY_AXES = "z"
-QUERY_ORDER = [0, 2, 4, 6, 1, 3, 5, 7]
-PART_ORDER = [7, 5, 3, 1, 0, 2, 4, 6]
+QUERY_ORDER = [4, 3, 5, 2, 6, 1, 7, 0]
+PART_ORDER = [1, 0, 2, 4, 6, 3, 5, 7]
 PLACE = [PART_ORDER.index(z) for z in QUERY_ORDER]
 HEAD_ORDER = [0, 5, 2, 7, 4, 1, 6, 3]
 KEY_ORDER = [0, 1, 2, 3, 4, 5, 6, 7]

time: 70.9 us -> 70.6 us (level)
  the two profiles are of different devices: /device:TPU:8 before, /device:TPU:64 now
where the time goes in v11:
time: 70.6 us; the launch traced here: 70.2 us
  blocking collectives  41.5 us (59%)
  starting transfers between devices  16.1 us (23%)
  Pallas kernels  5.65 us (8%)
  waiting for transfers between devices  5.57 us (8%)
  between operations  1.34 us (2%)
    all_to_all x2, blocking collectives, exchange(): lax.all_to_all(pieces, axes, 0, 0, tiled=True, axis_index_groups=[order])  22.3 us
    all_gather x1, blocking collectives, shards(): kv = lax.all_gather(block, KEY_AXES, axis=0, axis_index_groups=[KEY_ORDER])  19.2 us
    all_to_all x2, starting transfers between devices, exchange(): lax.all_to_all(pieces, axes, 0, 0, tiled=True, axis_index_groups=[order])  16.1 us
    pallas_call x5, Pallas kernels, call(): pl.pallas_call(kernel, out_shape=out_shape, in_specs=in_specs or [vmem] *...  5.65 us
    all_to_all x2, waiting for transfers between devices, exchange(): lax.all_to_all(pieces, axes, 0, 0, tiled=True, axis_index_groups=[order])  5.57 us
  transfers between devices with their start and end apart: 2, of which 1 were waited for; matrix products, arithmetic and copies ran while one was open for 0% of the time, Pallas kernels for 0%

profile of v11, /device:TPU:64, one launch (start us, length us, event | category | flops | bytes accessed | tf_op | source)
XLA Modules:
  0.0 70.2 jit_solution(5420170202583005665)
XLA Ops:
  0.7 1.6 %shard_map.118 = (bf16[8,32,384]{2,1,0:T(8,128)(2,1)}, bf16[32,1664]{1,0:T(8,128)(2,1)S(1)}) custom-call(s32[1]{0:T(128)S(6)} %copy.13.count_ref, f32[384]{0:T(512)} %gq_hbm.1, f32[384]{0:T(512)} %gk_hbm.1, bf16[32,384]{1,0:T(8,128)(2,1)} %q_hbm.1, bf16[32,384]{1,0:T(8,128)(2,1)} %k_hbm.1, bf16[32,384]{1,0:T(8,128)(2,1)} %v_hbm.1, bf16[32,384]{1,0:T(8,128)(2,1)} %rk_hbm.1, ...), custom_call_target="tpu_custom_call" | custom-call | flops 1 | bytes 1 | tf_op jit(solution)/shard_map/pallas_call | solution.py:41
  2.2 11.8 %all-to-all-start = ((bf16[8,32,384]{2,1,0:T(8,128)(2,1)}), bf16[8,32,384]{2,1,0:T(8,128)(2,1)S(1)}, u32[]{:S(2)}, u32[]{:S(2)}) async-start(bf16[8,32,384]{2,1,0:T(8,128)(2,1)} %get-tuple-element.9), calls=%async_computation | async-start | bytes 393216 | tf_op jit(solution)/shard_map/all_to_all | solution.py:211
  14.0 19.2 %all-gather = bf16[256,1664]{1,0:T(8,128)(2,1)S(1)} all-gather(bf16[32,1664]{1,0:T(8,128)(2,1)S(1)} %get-tuple-element.10), channel_id=2, replica_groups={{0,1,2,3,4,5,6,7},{8,9,10,11,12,13,14,15},{16,17,18,19,20,21,22,23},{24..., dimensions={0}, use_global_device_ids=true | all-gather | bytes 958464 | tf_op jit(solution)/shard_map/all_gather | solution.py:259
  33.2 0.0 all-to-all-done.q_ref
  33.2 0.8 %shard_map.119 = f32[8,4,128]{2,1,0:T(4,128)} custom-call(bf16[8,32,384]{2,1,0:T(8,128)(2,1)S(1)} %all-to-all-done.q_ref, bf16[8,32,1664]{2,1,0:T(8,128)(2,1)S(1)} %bitcast.1), custom_call_target="tpu_custom_call" | custom-call | flops 1 | bytes 1 | tf_op jit(solution)/shard_map/pallas_call | solution.py:41
  34.0 4.3 %all-to-all-start.1 = ((f32[8,4,128]{2,1,0:T(4,128)}), f32[8,4,128]{2,1,0:T(4,128)S(1)}, u32[]{:S(2)}, u32[]{:S(2)}) async-start(f32[8,4,128]{2,1,0:T(4,128)} %shard_map.119), calls=%async_computation.1 | async-start | bytes 32768 | tf_op jit(solution)/shard_map/all_to_all | solution.py:211
  38.9 5.6 %all-to-all-done.1.pw_ref = f32[8,4,128]{2,1,0:T(4,128)S(1)} async-done(((f32[8,4,128]{2,1,0:T(4,128)}), f32[8,4,128]{2,1,0:T(4,128)S(1)}, u32[]{:S(2)}, u32[]{:S(2)}) %all-to-all-start.1) | async-done | bytes 16416 | tf_op jit(solution)/shard_map/all_to_all | solution.py:211
  44.5 0.0 copy-start
  44.5 1.3 %shard_map.120 = (bf16[8,112,128]{2,1,0:T(8,128)(2,1)S(1)}, f32[8,128]{1,0:T(8,128)S(1)}) custom-call(s32[1]{0:T(128)S(6)} %copy.14.frame_ref, bf16[8,32,384]{2,1,0:T(8,128)(2,1)S(1)} %all-to-all-done.q_ref, bf16[8,32,1664]{2,1,0:T(8,128)(2,1)S(1)} %bitcast.2, f32[8,4,128]{2,1,0:T(4,128)S(1)} %all-to-all-done.1.pw_ref, bf16[384,5120]{1,0:T(8,128)(2,1)} %weight_ref.3), custom_call_target="tpu_custom_call" | custom-call | flops 4194304 | bytes 4194304 | tf_op jit(solution)/shard_map/pallas_call | solution.py:41
  45.8 0.0 copy-start.1
  45.8 0.0 copy-start.2
  45.8 12.2 %all_to_all.20.part_ref = bf16[8,112,128]{2,1,0:T(8,128)(2,1)S(1)} all-to-all(bf16[8,112,128]{2,1,0:T(8,128)(2,1)S(1)} %get-tuple-element.12), channel_id=1, replica_groups={{8,0,16,32,48,24,40,56},{9,1,17,33,49,25,41,57},{10,2,18,34,50,26,42,58..., dimensions={0} | all-to-all | bytes 458752 | tf_op jit(solution)/shard_map/all_to_all | solution.py:211
  58.0 0.0 copy-done
  58.0 1.3 %shard_map.121 = bf16[8,32,640]{2,1,0:T(8,128)(2,1)S(1)} custom-call(bf16[8,112,128]{2,1,0:T(8,128)(2,1)S(1)} %all_to_all.20.part_ref, bf16[384,5120]{1,0:T(8,128)(2,1)S(1)} %copy-done), custom_call_target="tpu_custom_call" | custom-call | flops 6291456 | bytes 6291456 | tf_op jit(solution)/shard_map/pallas_call | solution.py:41
  59.3 10.1 %all_to_all.21.part_ref = bf16[8,32,640]{2,1,0:T(8,128)(2,1)S(1)} all-to-all(bf16[8,32,640]{2,1,0:T(8,128)(2,1)S(1)} %shard_map.121), channel_id=1, replica_groups={{0,320,128,448,256,64,384,192},{1,321,129,449,257,65,385,193},{2,322,13..., dimensions={0} | all-to-all | bytes 655360 | tf_op jit(solution)/shard_map/all_to_all | solution.py:211
  69.5 0.0 copy-done.1
  69.5 0.0 copy-done.2
  69.5 0.7 shard_map.122
Async XLA Ops:
  2.2 31.0 %all-to-all-start = ((bf16[8,32,384]{2,1,0:T(8,128)(2,1)}), bf16[8,32,384]{2,1,0:T(8,128)(2,1)S(1)}, u32[]{:S(2)}, u32[]{:S(2)}) async-start(bf16[8,32,384]{2,1,0:T(8,128)(2,1)} %get-tuple-element.9), calls=%async_computation | async-start | bytes 393216 | tf_op jit(solution)/shard_map/all_to_all | solution.py:211
  34.0 10.5 %all-to-all-start.1 = ((f32[8,4,128]{2,1,0:T(4,128)}), f32[8,4,128]{2,1,0:T(4,128)S(1)}, u32[]{:S(2)}, u32[]{:S(2)}) async-start(f32[8,4,128]{2,1,0:T(4,128)} %shard_map.119), calls=%async_computation.1 | async-start | bytes 32768 | tf_op jit(solution)/shard_map/all_to_all | solution.py:211
  44.5 13.5 %copy-start = (bf16[384,5120]{1,0:T(8,128)(2,1)S(1)}, bf16[384,5120]{1,0:T(8,128)(2,1)}, u32[]{:S(2)}) copy-start(bf16[384,5120]{1,0:T(8,128)(2,1)} %weight_ref.3) | copy-start | bytes 11796484
  45.8 23.7 %copy-start.1 = (f32[50,640]{1,0:T(8,128)S(1)}, f32[50,640]{1,0:T(8,128)}, u32[]{:S(2)}) copy-start(f32[50,640]{1,0:T(8,128)} %gate_ref.1) | copy-start | bytes 384004
  45.8 23.7 %copy-start.2 = (bf16[32,640]{1,0:T(8,128)(2,1)S(1)}, bf16[32,640]{1,0:T(8,128)(2,1)}, u32[]{:S(2)}) copy-start(bf16[32,640]{1,0:T(8,128)(2,1)} %hidden_ref.1) | copy-start | bytes 122884

commit v12 on v11

--- a/solution.py
+++ b/solution.py
@@ -26,7 +26,7 @@
 SEQ_AXES = ("z", "yh", "c")
 KEY_AXES = ("yh", "c")
 QUERY_AXES = "z"
-QUERY_ORDER = [4, 3, 5, 2, 6, 1, 7, 0]
+QUERY_ORDER = [4, 5, 3, 6, 2, 7, 1, 0]
 PART_ORDER = [1, 0, 2, 4, 6, 3, 5, 7]
 PLACE = [PART_ORDER.index(z) for z in QUERY_ORDER]
 HEAD_ORDER = [0, 5, 2, 7, 4, 1, 6, 3]
@@ -36,13 +36,13 @@
 HB = 8
 
 
-def call(kernel, out_shape, *args, in_specs=None, n_out=1, cost=1, mib=16, scratch=()):
+def call(kernel, out_shape, *args, in_specs=None, out_specs=None, n_out=1, cost=1, mib=16, scratch=()):
     vmem = pl.BlockSpec(memory_space=pltpu.VMEM)
     return pl.pallas_call(
         kernel,
         out_shape=out_shape,
         in_specs=in_specs or [vmem] * len(args),
-        out_specs=vmem if n_out == 1 else [vmem] * n_out,
+        out_specs=out_specs or (vmem if n_out == 1 else [vmem] * n_out),
         scratch_shapes=scratch,
         cost_estimate=pl.CostEstimate(flops=cost, bytes_accessed=cost, transcendentals=0),
         compiler_params=pltpu.CompilerParams(vmem_limit_bytes=mib * 1024 * 1024),
@@ -58,7 +58,7 @@
     v_hbm,
     rk_hbm,
     rv_hbm,
-    qb_ref,
+    qb_hbm,
     kv_ref,
     gq_ref,
     gk_ref,
@@ -71,11 +71,14 @@
     copies = [pltpu.make_async_copy(a, b, sems.at[n]) for n, (a, b) in enumerate(pairs)]
     for copy in copies:
         copy.start()
-    for copy in copies[:3]:
+    copies[0].wait()
+    spread = [
+        pltpu.make_async_copy(q_ref, qb_hbm.at[peer], sems.at[7 + peer]) for peer in range(QB)
+    ]
+    for copy in spread:
+        copy.start()
+    for copy in copies[1:3]:
         copy.wait()
-    query = q_ref[...]
-    for peer in range(QB):
-        qb_ref[peer] = query
     count = count_ref[0].astype(F32)
     parts = []
     for ref in (gq_ref, gk_ref):
@@ -86,7 +89,7 @@
             rest = rest - part
     lines = [jnp.full((1, 128), count, F32)] + parts + [jnp.zeros((ROWS - 19, 128), F32)]
     kv_ref[:, 4 * FEAT :] = jnp.concatenate(lines, axis=0).astype(BF)
-    for copy in copies[3:]:
+    for copy in copies[3:] + spread:
         copy.wait()
 
 
@@ -247,12 +250,12 @@
         pin(ref_key),
         pin(ref_value),
         in_specs=[smem] + [hbm] * 7,
-        n_out=2,
+        out_specs=[hbm, vmem],
         scratch=[
             pltpu.VMEM((FEAT,), F32),
             pltpu.VMEM((FEAT,), F32),
             pltpu.VMEM((ROWS, FEAT), BF),
-            pltpu.SemaphoreType.DMA((7,)),
+            pltpu.SemaphoreType.DMA((7 + QB,)),
         ],
     )
     queries = exchange(queries, QUERY_AXES, QUERY_ORDER)

time: 70.6 us -> 70.5 us (level)
  the two profiles are of different devices: /device:TPU:64 before, /device:TPU:2 now
where the time goes in v12:
time: 70.5 us; the launch traced here: 70.1 us
  blocking collectives  40.6 us (58%)
  starting transfers between devices  18.4 us (26%)
  Pallas kernels  5.62 us (8%)
  waiting for transfers between devices  4.11 us (6%)
  between operations  1.34 us (2%)
    all_to_all x2, blocking collectives, exchange(): lax.all_to_all(pieces, axes, 0, 0, tiled=True, axis_index_groups=[order])  21.4 us
    all_gather x1, blocking collectives, shards(): kv = lax.all_gather(block, KEY_AXES, axis=0, axis_index_groups=[KEY_ORDER])  19.2 us
    all_to_all x2, starting transfers between devices, exchange(): lax.all_to_all(pieces, axes, 0, 0, tiled=True, axis_index_groups=[order])  18.4 us
    pallas_call x5, Pallas kernels, call(): pl.pallas_call(kernel, out_shape=out_shape, in_specs=in_specs or [vmem] *...  5.62 us
    all_to_all x2, waiting for transfers between devices, exchange(): lax.all_to_all(pieces, axes, 0, 0, tiled=True, axis_index_groups=[order])  4.11 us
  transfers between devices with their start and end apart: 2, of which 1 were waited for; matrix products, arithmetic and copies ran while one was open for 0% of the time, Pallas kernels for 0%

profile of v12, /device:TPU:2, one launch (start us, length us, event | category | flops | bytes accessed | tf_op | source)
XLA Modules:
  0.0 70.1 jit_solution(602802621233750481)
XLA Ops:
  0.7 1.5 %shard_map.118 = (bf16[8,32,384]{2,1,0:T(8,128)(2,1)}, bf16[32,1664]{1,0:T(8,128)(2,1)S(1)}) custom-call(s32[1]{0:T(128)S(6)} %copy.13.count_ref, f32[384]{0:T(512)} %gq_hbm.1, f32[384]{0:T(512)} %gk_hbm.1, bf16[32,384]{1,0:T(8,128)(2,1)} %q_hbm.1, bf16[32,384]{1,0:T(8,128)(2,1)} %k_hbm.1, bf16[32,384]{1,0:T(8,128)(2,1)} %v_hbm.1, bf16[32,384]{1,0:T(8,128)(2,1)} %rk_hbm.1, ...), custom_call_target="tpu_custom_call" | custom-call | flops 1 | bytes 1 | tf_op jit(solution)/shard_map/pallas_call | solution.py:41
  2.2 13.6 %all-to-all-start = ((bf16[8,32,384]{2,1,0:T(8,128)(2,1)}), bf16[8,32,384]{2,1,0:T(8,128)(2,1)S(1)}, u32[]{:S(2)}, u32[]{:S(2)}) async-start(bf16[8,32,384]{2,1,0:T(8,128)(2,1)} %get-tuple-element.9), calls=%async_computation | async-start | bytes 393216 | tf_op jit(solution)/shard_map/all_to_all | solution.py:214
  15.8 19.2 %all-gather = bf16[256,1664]{1,0:T(8,128)(2,1)S(1)} all-gather(bf16[32,1664]{1,0:T(8,128)(2,1)S(1)} %get-tuple-element.10), channel_id=2, replica_groups={{0,1,2,3,4,5,6,7},{8,9,10,11,12,13,14,15},{16,17,18,19,20,21,22,23},{24..., dimensions={0}, use_global_device_ids=true | all-gather | bytes 958464 | tf_op jit(solution)/shard_map/all_gather | solution.py:262
  35.0 0.0 all-to-all-done.q_ref
  35.0 0.8 %shard_map.119 = f32[8,4,128]{2,1,0:T(4,128)} custom-call(bf16[8,32,384]{2,1,0:T(8,128)(2,1)S(1)} %all-to-all-done.q_ref, bf16[8,32,1664]{2,1,0:T(8,128)(2,1)S(1)} %bitcast.1), custom_call_target="tpu_custom_call" | custom-call | flops 1 | bytes 1 | tf_op jit(solution)/shard_map/pallas_call | solution.py:41
  35.7 4.8 %all-to-all-start.1 = ((f32[8,4,128]{2,1,0:T(4,128)}), f32[8,4,128]{2,1,0:T(4,128)S(1)}, u32[]{:S(2)}, u32[]{:S(2)}) async-start(f32[8,4,128]{2,1,0:T(4,128)} %shard_map.119), calls=%async_computation.1 | async-start | bytes 32768 | tf_op jit(solution)/shard_map/all_to_all | solution.py:214
  41.2 4.1 %all-to-all-done.1.pw_ref = f32[8,4,128]{2,1,0:T(4,128)S(1)} async-done(((f32[8,4,128]{2,1,0:T(4,128)}), f32[8,4,128]{2,1,0:T(4,128)S(1)}, u32[]{:S(2)}, u32[]{:S(2)}) %all-to-all-start.1) | async-done | bytes 16416 | tf_op jit(solution)/shard_map/all_to_all | solution.py:214
  45.3 0.0 copy-start
  45.3 1.3 %shard_map.120 = (bf16[8,112,128]{2,1,0:T(8,128)(2,1)S(1)}, f32[8,128]{1,0:T(8,128)S(1)}) custom-call(s32[1]{0:T(128)S(6)} %copy.14.frame_ref, bf16[8,32,384]{2,1,0:T(8,128)(2,1)S(1)} %all-to-all-done.q_ref, bf16[8,32,1664]{2,1,0:T(8,128)(2,1)S(1)} %bitcast.2, f32[8,4,128]{2,1,0:T(4,128)S(1)} %all-to-all-done.1.pw_ref, bf16[384,5120]{1,0:T(8,128)(2,1)} %weight_ref.3), custom_call_target="tpu_custom_call" | custom-call | flops 4194304 | bytes 4194304 | tf_op jit(solution)/shard_map/pallas_call | solution.py:41
  46.6 0.0 copy-start.1
  46.7 0.0 copy-start.2
  46.7 10.9 %all_to_all.20.part_ref = bf16[8,112,128]{2,1,0:T(8,128)(2,1)S(1)} all-to-all(bf16[8,112,128]{2,1,0:T(8,128)(2,1)S(1)} %get-tuple-element.12), channel_id=1, replica_groups={{8,0,16,32,48,24,40,56},{9,1,17,33,49,25,41,57},{10,2,18,34,50,26,42,58..., dimensions={0} | all-to-all | bytes 458752 | tf_op jit(solution)/shard_map/all_to_all | solution.py:214
  57.6 0.0 copy-done
  57.6 1.3 %shard_map.121 = bf16[8,32,640]{2,1,0:T(8,128)(2,1)S(1)} custom-call(bf16[8,112,128]{2,1,0:T(8,128)(2,1)S(1)} %all_to_all.20.part_ref, bf16[384,5120]{1,0:T(8,128)(2,1)S(1)} %copy-done), custom_call_target="tpu_custom_call" | custom-call | flops 6291456 | bytes 6291456 | tf_op jit(solution)/shard_map/pallas_call | solution.py:41
  59.0 10.4 %all_to_all.21.part_ref = bf16[8,32,640]{2,1,0:T(8,128)(2,1)S(1)} all-to-all(bf16[8,32,640]{2,1,0:T(8,128)(2,1)S(1)} %shard_map.121), channel_id=1, replica_groups={{0,320,128,448,256,64,384,192},{1,321,129,449,257,65,385,193},{2,322,13..., dimensions={0} | all-to-all | bytes 655360 | tf_op jit(solution)/shard_map/all_to_all | solution.py:214
  69.4 0.0 copy-done.1
  69.4 0.0 copy-done.2
  69.4 0.7 shard_map.122
Async XLA Ops:
  2.2 32.8 %all-to-all-start = ((bf16[8,32,384]{2,1,0:T(8,128)(2,1)}), bf16[8,32,384]{2,1,0:T(8,128)(2,1)S(1)}, u32[]{:S(2)}, u32[]{:S(2)}) async-start(bf16[8,32,384]{2,1,0:T(8,128)(2,1)} %get-tuple-element.9), calls=%async_computation | async-start | bytes 393216 | tf_op jit(solution)/shard_map/all_to_all | solution.py:214
  35.7 9.6 %all-to-all-start.1 = ((f32[8,4,128]{2,1,0:T(4,128)}), f32[8,4,128]{2,1,0:T(4,128)S(1)}, u32[]{:S(2)}, u32[]{:S(2)}) async-start(f32[8,4,128]{2,1,0:T(4,128)} %shard_map.119), calls=%async_computation.1 | async-start | bytes 32768 | tf_op jit(solution)/shard_map/all_to_all | solution.py:214
  45.3 12.3 %copy-start = (bf16[384,5120]{1,0:T(8,128)(2,1)S(1)}, bf16[384,5120]{1,0:T(8,128)(2,1)}, u32[]{:S(2)}) copy-start(bf16[384,5120]{1,0:T(8,128)(2,1)} %weight_ref.3) | copy-start | bytes 11796484
  46.6 22.7 %copy-start.1 = (f32[50,640]{1,0:T(8,128)S(1)}, f32[50,640]{1,0:T(8,128)}, u32[]{:S(2)}) copy-start(f32[50,640]{1,0:T(8,128)} %gate_ref.1) | copy-start | bytes 384004
  46.7 22.7 %copy-start.2 = (bf16[32,640]{1,0:T(8,128)(2,1)S(1)}, bf16[32,640]{1,0:T(8,128)(2,1)}, u32[]{:S(2)}) copy-start(bf16[32,640]{1,0:T(8,128)(2,1)} %hidden_ref.1) | copy-start | bytes 122884

commit v13 on v12

--- a/solution.py
+++ b/solution.py
@@ -30,7 +30,7 @@
 PART_ORDER = [1, 0, 2, 4, 6, 3, 5, 7]
 PLACE = [PART_ORDER.index(z) for z in QUERY_ORDER]
 HEAD_ORDER = [0, 5, 2, 7, 4, 1, 6, 3]
-KEY_ORDER = [0, 1, 2, 3, 4, 5, 6, 7]
+KEY_ORDER = [7, 6, 5, 4, 3, 2, 1, 0]
 QB = 8
 KB = 8
 HB = 8

time: 70.5 us -> 70.5 us (level)
  the two profiles are of different devices: /device:TPU:2 before, /device:TPU:8 now
where the time goes in v13:
time: 70.5 us; the launch traced here: 70 us
  blocking collectives  39.5 us (56%)
  starting transfers between devices  19.4 us (28%)
  Pallas kernels  5.62 us (8%)
  waiting for transfers between devices  4.13 us (6%)
  between operations  1.34 us (2%)
    all_to_all x2, blocking collectives, exchange(): lax.all_to_all(pieces, axes, 0, 0, tiled=True, axis_index_groups=[order])  21.3 us
    all_to_all x2, starting transfers between devices, exchange(): lax.all_to_all(pieces, axes, 0, 0, tiled=True, axis_index_groups=[order])  19.4 us
    all_gather x1, blocking collectives, shards(): kv = lax.all_gather(block, KEY_AXES, axis=0, axis_index_groups=[KEY_ORDER])  18.2 us
    pallas_call x5, Pallas kernels, call(): pl.pallas_call(kernel, out_shape=out_shape, in_specs=in_specs or [vmem] *...  5.62 us
    all_to_all x2, waiting for transfers between devices, exchange(): lax.all_to_all(pieces, axes, 0, 0, tiled=True, axis_index_groups=[order])  4.13 us
  transfers between devices with their start and end apart: 2, of which 1 were waited for; matrix products, arithmetic and copies ran while one was open for 0% of the time, Pallas kernels for 0%

profile of v13, /device:TPU:8, one launch (start us, length us, event | category | flops | bytes accessed | tf_op | source)
XLA Modules:
  0.0 70.0 jit_solution(10862160111709884316)
XLA Ops:
  0.7 1.5 %shard_map.118 = (bf16[8,32,384]{2,1,0:T(8,128)(2,1)}, bf16[32,1664]{1,0:T(8,128)(2,1)S(1)}) custom-call(s32[1]{0:T(128)S(6)} %copy.13.count_ref, f32[384]{0:T(512)} %gq_hbm.1, f32[384]{0:T(512)} %gk_hbm.1, bf16[32,384]{1,0:T(8,128)(2,1)} %q_hbm.1, bf16[32,384]{1,0:T(8,128)(2,1)} %k_hbm.1, bf16[32,384]{1,0:T(8,128)(2,1)} %v_hbm.1, bf16[32,384]{1,0:T(8,128)(2,1)} %rk_hbm.1, ...), custom_call_target="tpu_custom_call" | custom-call | flops 1 | bytes 1 | tf_op jit(solution)/shard_map/pallas_call | solution.py:41
  2.2 13.6 %all-to-all-start = ((bf16[8,32,384]{2,1,0:T(8,128)(2,1)}), bf16[8,32,384]{2,1,0:T(8,128)(2,1)S(1)}, u32[]{:S(2)}, u32[]{:S(2)}) async-start(bf16[8,32,384]{2,1,0:T(8,128)(2,1)} %get-tuple-element.9), calls=%async_computation | async-start | bytes 393216 | tf_op jit(solution)/shard_map/all_to_all | solution.py:214
  15.8 18.2 %all-gather = bf16[256,1664]{1,0:T(8,128)(2,1)S(1)} all-gather(bf16[32,1664]{1,0:T(8,128)(2,1)S(1)} %get-tuple-element.10), channel_id=2, replica_groups={{7,6,5,4,3,2,1,0},{15,14,13,12,11,10,9,8},{23,22,21,20,19,18,17,16},{31..., dimensions={0}, use_global_device_ids=true | all-gather | bytes 958464 | tf_op jit(solution)/shard_map/all_gather | solution.py:262
  34.0 0.0 all-to-all-done.q_ref
  34.0 0.8 %shard_map.119 = f32[8,4,128]{2,1,0:T(4,128)} custom-call(bf16[8,32,384]{2,1,0:T(8,128)(2,1)S(1)} %all-to-all-done.q_ref, bf16[8,32,1664]{2,1,0:T(8,128)(2,1)S(1)} %bitcast.1), custom_call_target="tpu_custom_call" | custom-call | flops 1 | bytes 1 | tf_op jit(solution)/shard_map/pallas_call | solution.py:41
  34.8 5.8 %all-to-all-start.1 = ((f32[8,4,128]{2,1,0:T(4,128)}), f32[8,4,128]{2,1,0:T(4,128)S(1)}, u32[]{:S(2)}, u32[]{:S(2)}) async-start(f32[8,4,128]{2,1,0:T(4,128)} %shard_map.119), calls=%async_computation.1 | async-start | bytes 32768 | tf_op jit(solution)/shard_map/all_to_all | solution.py:214
  41.2 4.1 %all-to-all-done.1.pw_ref = f32[8,4,128]{2,1,0:T(4,128)S(1)} async-done(((f32[8,4,128]{2,1,0:T(4,128)}), f32[8,4,128]{2,1,0:T(4,128)S(1)}, u32[]{:S(2)}, u32[]{:S(2)}) %all-to-all-start.1) | async-done | bytes 16416 | tf_op jit(solution)/shard_map/all_to_all | solution.py:214
  45.3 0.0 copy-start
  45.3 1.3 %shard_map.120 = (bf16[8,112,128]{2,1,0:T(8,128)(2,1)S(1)}, f32[8,128]{1,0:T(8,128)S(1)}) custom-call(s32[1]{0:T(128)S(6)} %copy.14.frame_ref, bf16[8,32,384]{2,1,0:T(8,128)(2,1)S(1)} %all-to-all-done.q_ref, bf16[8,32,1664]{2,1,0:T(8,128)(2,1)S(1)} %bitcast.2, f32[8,4,128]{2,1,0:T(4,128)S(1)} %all-to-all-done.1.pw_ref, bf16[384,5120]{1,0:T(8,128)(2,1)} %weight_ref.3), custom_call_target="tpu_custom_call" | custom-call | flops 4194304 | bytes 4194304 | tf_op jit(solution)/shard_map/pallas_call | solution.py:41
  46.6 0.0 copy-start.1
  46.6 0.0 copy-start.2
  46.7 10.9 %all_to_all.20.part_ref = bf16[8,112,128]{2,1,0:T(8,128)(2,1)S(1)} all-to-all(bf16[8,112,128]{2,1,0:T(8,128)(2,1)S(1)} %get-tuple-element.12), channel_id=1, replica_groups={{8,0,16,32,48,24,40,56},{9,1,17,33,49,25,41,57},{10,2,18,34,50,26,42,58..., dimensions={0} | all-to-all | bytes 458752 | tf_op jit(solution)/shard_map/all_to_all | solution.py:214
  57.6 0.0 copy-done
  57.6 1.3 %shard_map.121 = bf16[8,32,640]{2,1,0:T(8,128)(2,1)S(1)} custom-call(bf16[8,112,128]{2,1,0:T(8,128)(2,1)S(1)} %all_to_all.20.part_ref, bf16[384,5120]{1,0:T(8,128)(2,1)S(1)} %copy-done), custom_call_target="tpu_custom_call" | custom-call | flops 6291456 | bytes 6291456 | tf_op jit(solution)/shard_map/pallas_call | solution.py:41
  58.9 10.4 %all_to_all.21.part_ref = bf16[8,32,640]{2,1,0:T(8,128)(2,1)S(1)} all-to-all(bf16[8,32,640]{2,1,0:T(8,128)(2,1)S(1)} %shard_map.121), channel_id=1, replica_groups={{0,320,128,448,256,64,384,192},{1,321,129,449,257,65,385,193},{2,322,13..., dimensions={0} | all-to-all | bytes 655360 | tf_op jit(solution)/shard_map/all_to_all | solution.py:214
  69.3 0.0 copy-done.1
  69.3 0.0 copy-done.2
  69.3 0.7 shard_map.122
Async XLA Ops:
  2.2 31.8 %all-to-all-start = ((bf16[8,32,384]{2,1,0:T(8,128)(2,1)}), bf16[8,32,384]{2,1,0:T(8,128)(2,1)S(1)}, u32[]{:S(2)}, u32[]{:S(2)}) async-start(bf16[8,32,384]{2,1,0:T(8,128)(2,1)} %get-tuple-element.9), calls=%async_computation | async-start | bytes 393216 | tf_op jit(solution)/shard_map/all_to_all | solution.py:214
  34.8 10.6 %all-to-all-start.1 = ((f32[8,4,128]{2,1,0:T(4,128)}), f32[8,4,128]{2,1,0:T(4,128)S(1)}, u32[]{:S(2)}, u32[]{:S(2)}) async-start(f32[8,4,128]{2,1,0:T(4,128)} %shard_map.119), calls=%async_computation.1 | async-start | bytes 32768 | tf_op jit(solution)/shard_map/all_to_all | solution.py:214
  45.3 12.2 %copy-start = (bf16[384,5120]{1,0:T(8,128)(2,1)S(1)}, bf16[384,5120]{1,0:T(8,128)(2,1)}, u32[]{:S(2)}) copy-start(bf16[384,5120]{1,0:T(8,128)(2,1)} %weight_ref.3) | copy-start | bytes 11796484
  46.6 22.6 %copy-start.1 = (f32[50,640]{1,0:T(8,128)S(1)}, f32[50,640]{1,0:T(8,128)}, u32[]{:S(2)}) copy-start(f32[50,640]{1,0:T(8,128)} %gate_ref.1) | copy-start | bytes 384004
  46.6 22.6 %copy-start.2 = (bf16[32,640]{1,0:T(8,128)(2,1)S(1)}, bf16[32,640]{1,0:T(8,128)(2,1)}, u32[]{:S(2)}) copy-start(bf16[32,640]{1,0:T(8,128)(2,1)} %hidden_ref.1) | copy-start | bytes 122884
